TPU v7x, 512 devices: a whole 4x4x16 slice. The times are simulated.
512 devices in a mesh: dp: 8 (over x, core), expert: 64 (over z, y).
Axes of the slice: x: 4, y: 4, z: 16, core: 2. Of those that a mesh axis runs over, the one named last changes fastest.
Arguments:
- tokens: bfloat16 [8192, 4096], P(('dp', 'expert')), may hold values from -6 to 6
- route_ids: int32 [8192, 8], P(('dp', 'expert')), may hold values from 0 to 127, all different within a row; in each aligned block of 16 rows (0 to 15, 16 to 31, ...) at most 2 rows name the same one
- gate_weights: float32 [8192, 8], P(('dp', 'expert')), may hold values from 0.05 to 0.3
- tenant_ids: int32 [8192], P(('dp', 'expert')), may hold values from 0 to 3
- up_weight: bfloat16 [128, 4096, 1024], P('expert', 'dp'), may hold values from -0.09375 to 0.09375
- down_weight: bfloat16 [128, 1024, 4096], P('expert', None, 'dp'), may hold values from -0.1875 to 0.1875
- adapter_in: bfloat16 [128, 4096, 64], P('expert', 'dp'), may hold values from -0.09375 to 0.09375
- adapter_out: bfloat16 [128, 64, 1024], P('expert'), may hold values from -1.5 to 1.5
Outputs:
- mixed: bfloat16 [8192, 4096], P(('dp', 'expert'))
Inputs may be any that keep to these rules, and one draw needn't show every extreme that they name: `route_ids`: the 8 experts of one token differ; among the 16 tokens of one device no expert is named more than 2 times, and some expert is named 2 times.
All inputs are finite; a program needn't handle non-finite values.
Results may differ from a plain program's by a relative error of at most 0.025.
Values may be sent and summed in bfloat16 or wider, within the bound.
No kernel may reach another device: no remote copies, remote signals or barrier semaphores. Data moves between devices by JAX's collectives and lax.ppermute only.
A program may use at most 64 MiB of HBM per device.

v0:
```python
import jax
import jax.numpy as jnp
from jax import lax
from jax.sharding import PartitionSpec as P

RANK = 16


def per_device(
    tokens, route_ids, gate_weights, tenant_ids, up_weight, down_weight, adapter_in, adapter_out
):
    n_dp = lax.axis_size("dp")
    n_col = lax.axis_size("expert")
    tok_count = tokens.shape[0]
    chosen = route_ids.shape[1]
    features = tokens.shape[1]
    exp_local = up_weight.shape[0]
    piece = up_weight.shape[1]
    units = up_weight.shape[2]
    adapter_cols = adapter_in.shape[2]
    experts_all = exp_local * n_col
    capacity = max(2, 2 * tok_count * chosen // experts_all)
    send_rows = experts_all * capacity
    flat_routes = route_ids.reshape(-1)
    order = jnp.arange(flat_routes.shape[0], dtype=jnp.int32)
    same = flat_routes[:, None] == flat_routes[None, :]
    earlier = order[None, :] < order[:, None]
    rank = jnp.sum((same & earlier).astype(jnp.int32), axis=1)
    target = flat_routes * capacity + rank
    outgoing = (
        jnp.zeros((send_rows, features), jnp.bfloat16)
        .at[target]
        .set(jnp.repeat(tokens, chosen, axis=0))
    )
    tag_line = (
        jnp.full((send_rows,), -1.0, jnp.float32)
        .at[target]
        .set(jnp.repeat(tenant_ids, chosen).astype(jnp.float32))
    )
    tag_grid = jnp.broadcast_to(tag_line[:, None], (send_rows, n_dp)).astype(jnp.bfloat16)
    sending = outgoing.reshape(n_col, exp_local, capacity, n_dp, piece)
    tag_send = tag_grid.reshape(n_col, exp_local, capacity, n_dp, 1)
    arrived, arrived_tags = (
        lax.all_to_all(
            lax.all_to_all(sending, "dp", split_axis=3, concat_axis=2, tiled=True),
            "expert",
            split_axis=0,
            concat_axis=2,
            tiled=True,
        ),
        lax.all_to_all(
            lax.all_to_all(tag_send, "dp", split_axis=3, concat_axis=2, tiled=True),
            "expert",
            split_axis=0,
            concat_axis=2,
            tiled=True,
        ),
    )
    rows_all = arrived.shape[2]
    grid = arrived.reshape(exp_local, rows_all, piece)
    tags = arrived_tags.reshape(exp_local, rows_all).astype(jnp.float32)
    up_part = jnp.einsum("erd,edf->erf", grid, up_weight, preferred_element_type=jnp.float32)
    shrink_part = jnp.einsum("erd,edl->erl", grid, adapter_in, preferred_element_type=jnp.float32)
    owner = (jnp.arange(adapter_cols, dtype=jnp.int32) // RANK).astype(jnp.float32)
    shrink = lax.psum(shrink_part.astype(jnp.bfloat16), "dp").astype(jnp.float32)
    keep = owner[None, None, :] == tags[..., None]
    masked_values = jnp.where(keep, shrink, jnp.zeros((), jnp.float32))
    up_portion = lax.psum_scatter(
        up_part.astype(jnp.bfloat16), "dp", scatter_dimension=2, tiled=True
    ).astype(jnp.float32)
    share = units // n_dp
    mapping_portion = lax.dynamic_slice_in_dim(
        adapter_out, lax.axis_index("dp") * share, share, 2
    ).astype(jnp.float32)
    low_rank_adapter = jnp.einsum(
        "erl,elf->erf", masked_values, mapping_portion, precision=lax.Precision.HIGHEST
    )
    hidden_portion = jax.nn.silu(up_portion + low_rank_adapter).astype(jnp.bfloat16)
    hidden_activations = lax.all_gather(hidden_portion, "dp", axis=2, tiled=True)
    expert_out = jnp.einsum(
        "erf,efd->erd", hidden_activations, down_weight, preferred_element_type=jnp.float32
    ).astype(jnp.bfloat16)
    going_back = expert_out.reshape(1, exp_local, rows_all, 1, piece)
    returned = lax.all_to_all(
        lax.all_to_all(going_back, "expert", split_axis=2, concat_axis=0, tiled=True),
        "dp",
        split_axis=2,
        concat_axis=3,
        tiled=True,
    )
    results = returned.reshape(send_rows, features)
    picked = results[target].astype(jnp.float32).reshape(tok_count, chosen, features)
    mixed = jnp.sum(picked * gate_weights[:, :, None], axis=1)
    return mixed.astype(jnp.bfloat16)


def solution(mesh):
    placed = (
        P(("dp", "expert"), None),
        P(("dp", "expert"), None),
        P(("dp", "expert"), None),
        P(("dp", "expert")),
        P("expert", "dp", None),
        P("expert", None, "dp"),
        P("expert", "dp", None),
        P("expert", None, None),
    )
    return jax.shard_map(
        per_device, mesh=mesh, in_specs=placed, out_specs=P(("dp", "expert"), None), check_vma=False
    )
```

profile of v0, /device:TPU:1, one launch (start us, length us, event | category | flops | bytes accessed | tf_op | source)
XLA Modules:
  0.0 524.5 jit_solution(6549004976233603520)
XLA Ops:
  6.5 0.8 broadcast_multiply_fusion
  7.4 0.8 copy.42
  8.2 0.1 mul.33
  8.3 0.1 eq.28
  8.4 0.2 convert_reduce_fusion
  8.6 4.0 scatter_custom_fusion
  12.6 2.5 copy.57
  15.1 1.6 copy.43
  16.7 35.8 %all_to_all.93 = bf16[64,2,2,8,512]{4,2,1,0,3:T(2,128)(2,1)S(1)} all-to-all(bf16[64,2,2,8,512]{4,2,1,0,3:T(2,128)(2,1)S(1)} %copy.43), channel_id=1, replica_groups=mesh['dp'=8,'expert'=64] {'dp'}, dimensions={3} | all-to-all | bytes 4194304 | tf_op jit(solution)/shard_map/all_to_all | solution.py:45
  52.5 0.5 copy.44
  53.0 1.2 copy.45
  54.2 109.7 %all_to_all.94 = bf16[64,2,16,1,512]{4,2,1,3,0:T(8,128)(2,1)S(1)} all-to-all(bf16[64,2,16,1,512]{4,2,1,3,0:T(8,128)(2,1)S(1)} %copy.45), channel_id=1, replica_groups=mesh['dp'=8,'expert'=64] {'expert'}, dimensions={0} | all-to-all | bytes 4194304 | tf_op jit(solution)/shard_map/all_to_all | solution.py:44
  163.9 0.2 copy.46
  164.1 1.3 copy-done.1
  165.4 4.3 convolution_convert_fusion
  169.7 11.3 %copy.55 = bf16[2,1024,1024]{1,0,2:T(2,128)(2,1)} copy(bf16[2,1024,1024]{2,1,0:T(8,128)(2,1)} %convolution_convert_fusion) | data formatting | bytes 8388608
  181.1 5.6 %copy.58 = bf16[128,8,2,1024]{3,1,2,0:T(8,128)(2,1)} copy(bf16[128,8,2,1024]{3,2,1,0:T(2,128)(2,1)} %bitcast.70) | data formatting | bytes 8388608
  186.7 0.6 copy-done.4
  187.3 0.1 broadcast_in_dim.35
  187.4 0.1 reshape.115
  187.4 1.0 scatter_custom_fusion.1
  188.4 0.2 broadcast_in_dim.36
  188.6 0.1 copy.47
  188.7 0.7 reshape.125
  189.4 9.2 %all-to-all-start.2 = ((bf16[8,2,128]{2,1,0:T(2,128)(2,1)}), bf16[8,2,128]{2,1,0:T(2,128)(2,1)S(1)}, u32[]{:S(2)}, u32[]{:S(2)}) async-start(bf16[8,2,128]{2,1,0:T(2,128)(2,1)} %reshape.125), calls=%async_computation.2 | async-start | bytes 8192 | tf_op jit(solution)/shard_map/all_to_all | solution.py:52
  198.6 4.6 all-to-all-done.2
  203.2 0.1 reshape.126
  203.3 0.7 copy.49
  204.1 5.4 %all-to-all-start.3 = ((bf16[64,2,16,1,1]{2,1,4,3,0:T(2,128)(2,1)}), bf16[64,2,16,1,1]{2,1,4,3,0:T(2,128)(2,1)S(1)}, u32[]{:S(2)}, u32[]{:S(2)}) async-start(bf16[64,2,16,1,1]{2,1,4,3,0:T(2,128)(2,1)} %copy.49), calls=%async_computation.3 | async-start | bytes 65536 | tf_op jit(solution)/shard_map/all_to_all | solution.py:51
  209.6 3.1 convolution_convert_fusion.1
  212.8 10.1 %all-to-all-done.3 = bf16[64,2,16,1,1]{2,1,4,3,0:T(2,128)(2,1)S(1)} async-done(((bf16[64,2,16,1,1]{2,1,4,3,0:T(2,128)(2,1)}), bf16[64,2,16,1,1]{2,1,4,3,0:T(2,128)(2,1)S(1)}, u32[]{:S(2)}, u32[]{:S(2)}) %all-to-all-start.3) | async-done | bytes 4128 | tf_op jit(solution)/shard_map/all_to_all | solution.py:51
  222.9 0.1 reshape.92
  223.0 2.2 reduce-scatter.4.cloned.1.call-done
  225.3 1.4 reshape.120
  226.7 0.5 copy.56
  227.3 75.4 %all-reduce.2.cloned.1.call-done = bf16[2,1024,64]{1,2,0:T(8,128)(2,1)} async-done(((bf16[2,1024,64]{1,2,0:T(8,128)(2,1)}), bf16[2,1024,64]{1,2,0:T(8,128)(2,1)}) %all-reduce.2.cloned.1.call-update) | async-done | bytes 262160 | tf_op jit(solution)/shard_map/psum | solution.py:65
  302.7 2.8 multiply_convert_fusion
  305.6 44.9 %all-gather.2.cloned.1.call-done = bf16[2,1024,1024]{2,1,0:T(8,128)(2,1)} async-done(((bf16[2,1024,128]{2,1,0:T(8,128)(2,1)}), bf16[2,1024,1024]{2,1,0:T(8,128)(2,1)}) %all-gather.2.cloned.1.call-update) | async-done | bytes 4194320 | tf_op jit(solution)/shard_map/all_gather | solution.py:79
  350.5 5.2 convert_bitcast_fusion
  355.7 2.2 copy.51
  357.8 112.2 %all_to_all.95 = bf16[1,2,1024,1,512]{4,1,3,0,2:T(2,128)(2,1)S(1)} all-to-all(bf16[1,2,1024,1,512]{4,1,3,0,2:T(2,128)(2,1)S(1)} %copy.51), channel_id=1, replica_groups=mesh['dp'=8,'expert'=64] {'expert'}, dimensions={2} | all-to-all | bytes 4194304 | tf_op jit(solution)/shard_map/all_to_all | solution.py:85
  470.1 2.5 copy.61
  472.5 8.4 %all-to-all-start.5 = ((bf16[64,2,16,1,512]{4,0,1,3,2:T(8,128)(2,1)}), bf16[64,2,16,1,512]{4,0,1,3,2:T(8,128)(2,1)}, u32[]{:S(2)}, u32[]{:S(2)}) async-start(bf16[64,2,16,1,512]{4,0,1,3,2:T(8,128)(2,1)} %bitcast.73), calls=%async_computation.5 | async-start | bytes 4194304 | tf_op jit(solution)/shard_map/all_to_all | solution.py:84
  481.1 26.4 %all-to-all-done.5 = bf16[64,2,16,1,512]{4,0,1,3,2:T(8,128)(2,1)} async-done(((bf16[64,2,16,1,512]{4,0,1,3,2:T(8,128)(2,1)}), bf16[64,2,16,1,512]{4,0,1,3,2:T(8,128)(2,1)}, u32[]{:S(2)}, u32[]{:S(2)}) %all-to-all-start.5) | async-done | bytes 2097184 | tf_op jit(solution)/shard_map/all_to_all | solution.py:84
  507.4 2.8 copy.53
  510.2 2.2 copy.59
  512.4 4.1 gather_fusion
  516.5 1.4 fusion
  (26 shorter events, 0.4 us)
Async XLA Ops:
  6.5 158.9 %copy-start = (bf16[2,512,1024]{2,1,0:T(8,128)(2,1)S(1)}, bf16[2,512,1024]{2,1,0:T(8,128)(2,1)}, u32[]{:S(2)}) copy-start(bf16[2,512,1024]{2,1,0:T(8,128)(2,1)} %param.12) | copy-start | bytes 6291460
  6.5 218.7 %reduce-scatter.4.cloned.1.call-start = ((), (), s32[]{:S(2)}) async-start(), calls=%async_computation.9 | async-start | bytes 4718592
  164.1 1.4 copy-start.1
  186.6 0.7 copy-start.4
  186.6 22.9 %copy-start.2 = (bf16[2,512,64]{1,2,0:T(8,128)(2,1)S(1)}, bf16[2,512,64]{1,2,0:T(8,128)(2,1)}, u32[]{:S(2)}) copy-start(bf16[2,512,64]{1,2,0:T(8,128)(2,1)} %param.14) | copy-start | bytes 393220
  189.4 13.8 %all-to-all-start.2 = ((bf16[8,2,128]{2,1,0:T(2,128)(2,1)}), bf16[8,2,128]{2,1,0:T(2,128)(2,1)S(1)}, u32[]{:S(2)}, u32[]{:S(2)}) async-start(bf16[8,2,128]{2,1,0:T(2,128)(2,1)} %reshape.125), calls=%async_computation.2 | async-start | bytes 8192 | tf_op jit(solution)/shard_map/all_to_all | solution.py:52
  204.1 18.8 %all-to-all-start.3 = ((bf16[64,2,16,1,1]{2,1,4,3,0:T(2,128)(2,1)}), bf16[64,2,16,1,1]{2,1,4,3,0:T(2,128)(2,1)S(1)}, u32[]{:S(2)}, u32[]{:S(2)}) async-start(bf16[64,2,16,1,1]{2,1,4,3,0:T(2,128)(2,1)} %copy.49), calls=%async_computation.3 | async-start | bytes 65536 | tf_op jit(solution)/shard_map/all_to_all | solution.py:51
  209.5 93.2 %all-reduce.2.cloned.1.call-start = ((), (), s32[]{:S(2)}) async-start(), calls=%async_computation.7 | async-start | bytes 524288 | tf_op jit(solution)/shard_map/psum | solution.py:65
  212.7 137.7 %all-gather.2.cloned.1.call-start = ((), (), s32[]{:S(2)}) async-start(), calls=%async_computation.8 | async-start | bytes 4718592 | tf_op jit(solution)/shard_map/all_gather | solution.py:79
  472.5 8.4 %copy-start.3 = (f32[16,8]{0,1:T(8,128)S(1)}, f32[16,8]{0,1:T(8,128)}, u32[]{:S(2)}) copy-start(f32[16,8]{0,1:T(8,128)} %param.10) | copy-start | bytes 1540
  472.5 34.9 %all-to-all-start.5 = ((bf16[64,2,16,1,512]{4,0,1,3,2:T(8,128)(2,1)}), bf16[64,2,16,1,512]{4,0,1,3,2:T(8,128)(2,1)}, u32[]{:S(2)}, u32[]{:S(2)}) async-start(bf16[64,2,16,1,512]{4,0,1,3,2:T(8,128)(2,1)} %bitcast.73), calls=%async_computation.5 | async-start | bytes 4194304 | tf_op jit(solution)/shard_map/all_to_all | solution.py:84
Sparse Core Ops, SparseCore 0:
  186.8 38.4 reduce-scatter.3
  227.6 75.0 all-reduce.1
  305.7 44.7 all-gather.1
where the time goes:
time: 525 us; the launch traced here: 524 us
  blocking collectives  258 us (49%)
  waiting for transfers between devices  164 us (31%)
  local copies, waits for them, and re-layouts  48.5 us (9%)
  starting transfers between devices  23.2 us (4%)
  matrix products  15.4 us (3%)
  between operations  13.3 us (3%)
    all_to_all x1, blocking collectives, per_device(): lax.all_to_all(going_back, 'expert', split_axis=2, concat_axis=0, tiled=T...  112 us
    all_to_all x1, blocking collectives, per_device(): lax.all_to_all(lax.all_to_all(sending, 'dp', split_axis=3, concat_axis=2,...  110 us
    psum x1, waiting for transfers between devices, per_device(): lax.psum(shrink_part.astype(jnp.bfloat16), 'dp').astype(jnp.float32)  75.4 us
    all_gather x1, waiting for transfers between devices, per_device(): lax.all_gather(hidden_portion, 'dp', axis=2, tiled=True)  44.9 us
    all_to_all x1, blocking collectives, per_device(): lax.all_to_all(sending, 'dp', split_axis=3, concat_axis=2, tiled=True)  35.8 us
    unnamed x21, local copies, waits for them, and re-layouts  27.1 us
    all_to_all x1, waiting for transfers between devices, per_device(): lax.all_to_all(lax.all_to_all(going_back, 'expert', split_axis=2, concat_...  26.4 us
  transfers between devices with their start and end apart: 6, of which 6 were waited for; matrix products, arithmetic and copies ran while one was open for 2% of the time, Pallas kernels for 0%

commit v1 on v0

v1 whole, which is shorter than its diff:
```python
import functools
import jax
import jax.numpy as jnp
from jax import lax
from jax.experimental import pallas as pl
from jax.experimental.pallas import tpu as pltpu
from jax.sharding import Mesh, PartitionSpec as P

BF = jnp.bfloat16
F32 = jnp.float32
TOK = 16
TOP = 8
PLANE = 8
TEN = 4
RANK = 16
WIDE = 1024
META = 128
ROUTE_AT = 64
GATE_AT = 72
GROUP = 256


def _matches(meta, z):
    lane = lax.broadcasted_iota(jnp.int32, (GROUP, META), 1)
    expert = jnp.where(lane < PLANE, lane + z * PLANE, -1).astype(F32)
    return [meta[:, ROUTE_AT + k : ROUTE_AT + k + 1] == expert for k in range(TOP)]


def _slots(matches):
    named = sum(m.astype(F32) for m in matches)
    row = lax.broadcasted_iota(jnp.int32, (GROUP, GROUP), 0)
    col = lax.broadcasted_iota(jnp.int32, (GROUP, GROUP), 1)
    before = ((row // TOK == col // TOK) & (col < row)).astype(BF)
    rank = jnp.dot(before, named.astype(BF), preferred_element_type=F32)
    seat = named * (rank + 1.0)
    spread = _spread()
    at = jnp.dot(seat.astype(BF), spread, preferred_element_type=F32)
    want = (col % 2 + 1).astype(F32)
    return (at == want) & (row // TOK == (col % 32) // 2)


def _spread():
    e = lax.broadcasted_iota(jnp.int32, (META, GROUP), 0)
    j = lax.broadcasted_iota(jnp.int32, (META, GROUP), 1)
    return (e == j // 32).astype(BF)


def _select_kernel(z_ref, t_ref, o_ref):
    t = t_ref[...].reshape(GROUP, WIDE + META)
    slots = _slots(_matches(t[:, WIDE:].astype(F32), z_ref[0])).astype(BF)
    out = lax.dot_general(slots, t, (((0,), (0,)), ((), ())), preferred_element_type=F32)
    o_ref[...] = out.astype(BF).reshape(PLANE, 32, WIDE + META)


def _select(z, table):
    return pl.pallas_call(
        _select_kernel,
        grid_spec=pltpu.PrefetchScalarGridSpec(
            num_scalar_prefetch=1,
            grid=(4,),
            in_specs=[pl.BlockSpec((4, 64, WIDE + META), lambda g, z: (g, 0, 0))],
            out_specs=pl.BlockSpec((PLANE, 32, WIDE + META), lambda g, z: (0, g, 0)),
        ),
        out_shape=jax.ShapeDtypeStruct((PLANE, 128, WIDE + META), BF),
        compiler_params=pltpu.CompilerParams(vmem_limit_bytes=32 << 20),
        name="select",
    )(z, table)


def _up_kernel(x_ref, w_ref, o_ref):
    acc = jnp.dot(x_ref[:, :WIDE], w_ref[...], preferred_element_type=F32)
    o_ref[:, :WIDE] = acc[:, :WIDE].astype(BF)
    o_ref[:, WIDE:] = (acc[:, WIDE:] * x_ref[:, WIDE:].astype(F32)).astype(BF)


def _up(x, w):
    rows = x.shape[0]
    return pl.pallas_call(
        _up_kernel,
        grid=(rows // 256,),
        in_specs=[
            pl.BlockSpec((256, WIDE + META), lambda g: (g, 0)),
            pl.BlockSpec((WIDE, WIDE + META), lambda g: (0, 0)),
        ],
        out_specs=pl.BlockSpec((256, WIDE + META), lambda g: (g, 0)),
        out_shape=jax.ShapeDtypeStruct((rows, WIDE + META), BF),
        compiler_params=pltpu.CompilerParams(vmem_limit_bytes=32 << 20),
        name="up",
    )(x, w)


def _act_kernel(c_ref, u_ref, a_ref, o_ref):
    lora = jnp.dot(u_ref[:, WIDE : WIDE + 64], a_ref[0], preferred_element_type=F32)
    v = u_ref[:, :WIDE].astype(F32) + lora
    o_ref[...] = (v / (1.0 + jnp.exp(-v))).astype(BF)


def _act(c, u, adapter_out):
    rows = u.shape[0]
    return pl.pallas_call(
        _act_kernel,
        grid_spec=pltpu.PrefetchScalarGridSpec(
            num_scalar_prefetch=1,
            grid=(rows // 128,),
            in_specs=[
                pl.BlockSpec((128, WIDE + META), lambda g, c: (g, 0)),
                pl.BlockSpec((1, 64, WIDE), lambda g, c: (c[0], 0, 0)),
            ],
            out_specs=pl.BlockSpec((128, WIDE), lambda g, c: (g, 0)),
        ),
        out_shape=jax.ShapeDtypeStruct((rows, WIDE), BF),
        compiler_params=pltpu.CompilerParams(vmem_limit_bytes=32 << 20),
        name="act",
    )(c, u, adapter_out)


def _down_kernel(x_ref, w_ref, o_ref):
    o_ref[...] = jnp.dot(x_ref[...], w_ref[...], preferred_element_type=F32).astype(BF)


def _down(x, w):
    rows = x.shape[0]
    return pl.pallas_call(
        _down_kernel,
        grid=(rows // 256,),
        in_specs=[
            pl.BlockSpec((256, WIDE), lambda g: (g, 0)),
            pl.BlockSpec((WIDE, WIDE), lambda g: (0, 0)),
        ],
        out_specs=pl.BlockSpec((256, WIDE), lambda g: (g, 0)),
        out_shape=jax.ShapeDtypeStruct((rows, WIDE), BF),
        compiler_params=pltpu.CompilerParams(vmem_limit_bytes=32 << 20),
        name="down",
    )(x, w)


def _combine_kernel(z_ref, m_ref, y_ref, o_ref):
    meta = m_ref[...].reshape(GROUP, META).astype(F32)
    matches = _matches(meta, z_ref[0])
    gate = sum(jnp.where(m, meta[:, GATE_AT + k : GATE_AT + k + 1], 0.0) for k, m in enumerate(matches))
    gates = jnp.dot(gate.astype(BF), _spread(), preferred_element_type=F32)
    weight = jnp.where(_slots(matches), gates, 0.0).astype(BF)
    out = jnp.dot(weight, y_ref[...].reshape(GROUP, WIDE), preferred_element_type=F32)
    o_ref[...] = out.astype(BF).reshape(4, 64, WIDE)


def _combine(z, table, back):
    return pl.pallas_call(
        _combine_kernel,
        grid_spec=pltpu.PrefetchScalarGridSpec(
            num_scalar_prefetch=1,
            grid=(4,),
            in_specs=[
                pl.BlockSpec((4, 64, META), lambda g, z: (g, 0, WIDE // META)),
                pl.BlockSpec((PLANE, 32, WIDE), lambda g, z: (0, g, 0)),
            ],
            out_specs=pl.BlockSpec((4, 64, WIDE), lambda g, z: (g, 0, 0)),
        ),
        out_shape=jax.ShapeDtypeStruct((16, 64, WIDE), BF),
        compiler_params=pltpu.CompilerParams(vmem_limit_bytes=32 << 20),
        name="combine",
    )(z, table, back)


def per_device(tokens, route_ids, gate_weights, tenant_ids, up_weight, down_weight, adapter_in, adapter_out):
    z = lax.axis_index("z").astype(jnp.int32).reshape(1)
    core = lax.axis_index("core").astype(jnp.int32)

    def both(w, axis):
        own = lax.dynamic_index_in_dim(w, core, 0, keepdims=False)
        other = lax.dynamic_index_in_dim(w, 1 - core, 0, keepdims=False)
        other = lax.ppermute(other, "core", [(0, 1), (1, 0)])
        first = jnp.where(core == 0, own, other)
        second = jnp.where(core == 0, other, own)
        return jnp.concatenate([first, second], axis=axis)

    w_up = both(up_weight, 0)
    w_in = both(adapter_in, 0)
    w_down = both(down_weight, 1)
    w_cat = jnp.concatenate([w_up, w_in, jnp.zeros((WIDE, META - TEN * RANK), BF)], axis=1)

    owner = jnp.arange(TEN * RANK, dtype=jnp.int32) // RANK
    mask = (owner[None, :] == tenant_ids[:, None]).astype(BF)
    meta = jnp.concatenate(
        [mask, route_ids.astype(BF), gate_weights.astype(BF), jnp.zeros((TOK, META - 80), BF)], axis=1
    )
    pieces = tokens.reshape(TOK, 4, WIDE).transpose(1, 0, 2)
    rows = jnp.concatenate([pieces, jnp.broadcast_to(meta[None], (4, TOK, META))], axis=2)
    mine = lax.all_to_all(rows, "x", 0, 0, tiled=True).reshape(64, WIDE + META)
    table = lax.all_gather(mine, "z", axis=0)
    sending = _select(z, table)
    arrived = lax.all_to_all(sending, ("y", "core"), 0, 0, tiled=True).reshape(1024, WIDE + META)
    part = _up(arrived, w_cat)
    summed = lax.psum_scatter(part, "x", scatter_dimension=0, tiled=True)
    hidden_part = _act(core.reshape(1), summed, adapter_out)
    hidden = lax.all_gather(hidden_part, "x", axis=0, tiled=True)
    out = _down(hidden, w_down).reshape(8, 128, WIDE)
    back = lax.all_to_all(out, ("y", "core"), 0, 0, tiled=True)
    partial = _combine(z, table, back).reshape(1024, WIDE)
    mixed = lax.psum_scatter(partial, "z", scatter_dimension=0, tiled=True)
    home = lax.all_to_all(mixed.reshape(4, TOK, WIDE), "x", 0, 0, tiled=True)
    return home.transpose(1, 0, 2).reshape(TOK, 4 * WIDE)


def solution(mesh):
    fine = Mesh(mesh.devices.reshape(4, 2, 16, 4), ("x", "core", "z", "y"))
    dp, ex = ("x", "core"), ("z", "y")
    every = dp + ex
    placed = (
        P(every, None),
        P(every, None),
        P(every, None),
        P(every),
        P(ex, dp, None),
        P(ex, None, dp),
        P(ex, dp, None),
        P(ex, None, None),
    )
    return jax.shard_map(per_device, mesh=fine, in_specs=placed, out_specs=P(every, None), check_vma=False)
```

time: 525 us -> 354 us (0.67)
  the two profiles are of different devices: /device:TPU:1 before, /device:TPU:8 now
where the time goes in v1:
time: 354 us; the launch traced here: 353 us
  waiting for transfers between devices  227 us (64%)
  blocking collectives  51.3 us (14%)
  local copies, waits for them, and re-layouts  25.1 us (7%)
  Pallas kernels  15.4 us (4%)
  between operations  13.3 us (4%)
  starting transfers between devices  10.9 us (3%)
  other arithmetic  9.89 us (3%)
    all_gather x1, waiting for transfers between devices, per_device(): table = lax.all_gather(mine, 'z', axis=0)  77 us
    reduce_scatter x1, waiting for transfers between devices, per_device(): mixed = lax.psum_scatter(partial, 'z', scatter_dimension=0, tiled=True)  72.6 us
    reduce_scatter x1, waiting for transfers between devices, per_device(): summed = lax.psum_scatter(part, 'x', scatter_dimension=0, tiled=True)  35.5 us
    all_to_all x1, blocking collectives, per_device(): back = lax.all_to_all(out, ('y', 'core'), 0, 0, tiled=True)  30.8 us
    all_gather x1, waiting for transfers between devices, per_device(): hidden = lax.all_gather(hidden_part, 'x', axis=0, tiled=True)  29.5 us
    unnamed x22, local copies, waits for them, and re-layouts  11.8 us
    all_to_all x1, blocking collectives, per_device(): mine = lax.all_to_all(rows, 'x', 0, 0, tiled=True).reshape(64, WIDE + META)  10.3 us
    all_to_all x1, blocking collectives, per_device(): home = lax.all_to_all(mixed.reshape(4, TOK, WIDE), 'x', 0, 0, tiled=True)  10.2 us
  transfers between devices with their start and end apart: 8, of which 7 were waited for; matrix products, arithmetic and copies ran while one was open for 5% of the time, Pallas kernels for 0%

profile of v1, /device:TPU:8, one launch (start us, length us, event | category | flops | bytes accessed | tf_op | source)
XLA Modules:
  0.0 352.6 jit_solution(4715656082201720961)
XLA Ops:
  6.5 0.9 copy.29
  7.5 0.7 convert_element_type.10
  8.2 0.1 copy.21
  8.2 0.7 convert_element_type.11
  8.9 0.1 copy.22
  9.0 0.7 compare_convert_fusion
  9.7 0.1 pad.11.clone
  9.8 0.1 maximum_maximum_fusion
  9.9 10.3 %all_to_all.20 = bf16[4,16,1152]{2,1,0:T(8,128)(2,1)} all-to-all(bf16[4,16,1152]{2,1,0:T(8,128)(2,1)S(1)} %pad_maximum_fusion.3), channel_id=1, replica_groups=mesh['x'=4,'core'=2,'z'=16,'y'=4] {'x'}, dimensions={0} | all-to-all | bytes 294912 | tf_op jit(solution)/shard_map/all_to_all | solution.py:189
  20.2 77.0 %all-gather.3.cloned.1.call-done.t_ref.m_ref = bf16[16,64,1152]{2,1,0:T(8,128)(2,1)} async-done(((bf16[1,64,1152]{2,1,0:T(8,128)(2,1)}), bf16[16,64,1152]{2,1,0:T(8,128)(2,1)}) %all-gather.3.cloned.1.call-update) | async-done | bytes 2359312 | tf_op jit(solution)/shard_map/all_gather | solution.py:190
  97.2 1.7 copy-done.2
  98.9 4.0 %select.9 = bf16[8,128,1152]{2,1,0:T(8,128)(2,1)S(1)} custom-call(s32[1]{0:T(128)} %bitcast.z_ref, bf16[16,64,1152]{2,1,0:T(8,128)(2,1)S(1)} %copy-done.2), custom_call_target="tpu_custom_call" | custom-call | tf_op jit(solution)/shard_map/select/pallas_call | solution.py:56
  102.9 1.4 copy-done.4
  104.3 4.6 %all-to-all-start.1 = ((bf16[8,128,1152]{2,1,0:T(8,128)(2,1)}), bf16[8,128,1152]{2,1,0:T(8,128)(2,1)S(1)}, u32[]{:S(2)}, u32[]{:S(2)}) async-start(bf16[8,128,1152]{2,1,0:T(8,128)(2,1)} %copy-done.4), calls=%async_computation.1 | async-start | bytes 4718592 | tf_op jit(solution)/shard_map/all_to_all | solution.py:192
  108.9 2.3 dynamic-slice_bitcast_fusion.1
  111.2 2.0 collective-permute-start
  113.3 1.5 constant_dynamic-slice_fusion.1
  114.8 0.8 copy.24
  115.5 2.3 collective-permute-start.1
  117.8 1.0 copy.23
  118.8 0.3 collective-permute-done.1
  119.1 0.9 bitcast_select_fusion.5
  120.0 0.7 pad_maximum_fusion.2
  120.8 1.4 bitcast_select_fusion.3
  122.2 1.6 pad_maximum_fusion
  123.8 4.6 %concatenate.22.w_ref = bf16[1024,1152]{1,0:T(8,128)(2,1)} concatenate(bf16[1024,1024]{1,0:T(8,128)(2,1)} %pad_maximum_fusion, bf16[1024,64]{1,0:T(8,128)(2,1)S(1)} %copy-done.10, bf16[1024,64]{1,0:T(8,128)(2,1)S(1)} %broadcast_in_dim.16), dimensions={1} | concatenate | bytes 4718592 | tf_op jit(solution)/shard_map/concatenate | solution.py:180
  128.4 9.1 %all-to-all-done.1 = bf16[8,128,1152]{2,1,0:T(8,128)(2,1)S(1)} async-done(((bf16[8,128,1152]{2,1,0:T(8,128)(2,1)}), bf16[8,128,1152]{2,1,0:T(8,128)(2,1)S(1)}, u32[]{:S(2)}, u32[]{:S(2)}) %all-to-all-start.1) | async-done | bytes 2359328 | tf_op jit(solution)/shard_map/all_to_all | solution.py:192
  137.5 1.7 copy-done.1
  139.1 3.4 up.1
  142.6 1.4 copy-done
  144.1 35.5 %reduce-scatter.3.cloned.1.call-done.u_ref = bf16[256,1152]{1,0:T(8,128)(2,1)} async-done(((bf16[1024,1152]{1,0:T(8,128)(2,1)}), bf16[256,1152]{1,0:T(8,128)(2,1)}) %reduce-scatter.3.cloned.1.call-update) | async-done | bytes 589840 | tf_op jit(solution)/shard_map/reduce_scatter | solution.py:194
  179.6 1.1 copy-done.8
  180.7 1.3 act.1
  182.0 1.3 dynamic-slice_bitcast_fusion
  183.3 1.9 collective-permute-start.2
  185.3 2.6 collective-permute-done.2
  187.9 1.4 bitcast_select_fusion.1
  189.2 1.7 pad_maximum_fusion.1.w_ref
  190.9 29.5 %all-gather.5.cloned.1.call-done.x_ref = bf16[1024,1024]{1,0:T(8,128)(2,1)} async-done(((bf16[256,1024]{1,0:T(8,128)(2,1)}), bf16[1024,1024]{1,0:T(8,128)(2,1)}) %all-gather.5.cloned.1.call-update) | async-done | bytes 2097168 | tf_op jit(solution)/shard_map/all_gather | solution.py:196
  220.4 1.6 copy-done.5
  222.0 1.6 copy-done.7
  223.6 2.9 down.1
  226.5 30.8 %all_to_all.21.y_ref = bf16[8,128,1024]{2,1,0:T(8,128)(2,1)S(1)} all-to-all(bf16[8,128,1024]{2,1,0:T(8,128)(2,1)S(1)} %bitcast.32), channel_id=1, replica_groups=mesh['x'=4,'core'=2,'z'=16,'y'=4] {'y','core'}, dimensions={0} | all-to-all | bytes 4194304 | tf_op jit(solution)/shard_map/all_to_all | solution.py:198
  257.3 3.8 %combine.1 = bf16[16,64,1024]{2,1,0:T(8,128)(2,1)S(1)} custom-call(s32[1]{0:T(128)} %bitcast.z_ref, bf16[16,64,1152]{2,1,0:T(8,128)(2,1)S(1)} %copy-done.3, bf16[8,128,1024]{2,1,0:T(8,128)(2,1)S(1)} %all_to_all.21.y_ref), custom_call_target="tpu_custom_call" | custom-call | tf_op jit(solution)/shard_map/combine/pallas_call | solution.py:148
  261.2 1.3 copy-done.6
  262.5 72.6 %reduce-scatter.5.cloned.1.call-done = bf16[64,1024]{1,0:T(8,128)(2,1)} async-done(((bf16[1024,1024]{1,0:T(8,128)(2,1)}), bf16[64,1024]{1,0:T(8,128)(2,1)}) %reduce-scatter.5.cloned.1.call-update) | async-done | bytes 131088 | tf_op jit(solution)/shard_map/reduce_scatter | solution.py:200
  335.1 10.2 %all_to_all.22 = bf16[4,16,1024]{2,1,0:T(8,128)(2,1)S(1)} all-to-all(bf16[4,16,1024]{2,1,0:T(8,128)(2,1)} %bitcast.39), channel_id=1, replica_groups=mesh['x'=4,'core'=2,'z'=16,'y'=4] {'x'}, dimensions={0} | all-to-all | bytes 262144 | tf_op jit(solution)/shard_map/all_to_all | solution.py:201
  345.4 0.7 copy.27
  (28 shorter events, 0.2 us)
Async XLA Ops:
  6.5 90.7 %all-gather.3.cloned.1.call-start = ((), (), s32[]{:S(2)}) async-start(), calls=%async_computation.6 | async-start | bytes 2506752 | tf_op jit(solution)/shard_map/all_gather | solution.py:190
  97.2 1.7 copy-start.2
  102.9 1.4 copy-start.4
  104.3 33.1 %all-to-all-start.1 = ((bf16[8,128,1152]{2,1,0:T(8,128)(2,1)}), bf16[8,128,1152]{2,1,0:T(8,128)(2,1)S(1)}, u32[]{:S(2)}, u32[]{:S(2)}) async-start(bf16[8,128,1152]{2,1,0:T(8,128)(2,1)} %copy-done.4), calls=%async_computation.1 | async-start | bytes 4718592 | tf_op jit(solution)/shard_map/all_to_all | solution.py:192
  108.9 70.7 %reduce-scatter.3.cloned.1.call-start = ((), (), s32[]{:S(2)}) async-start(), calls=%async_computation.7 | async-start | bytes 2949120 | tf_op jit(solution)/shard_map/reduce_scatter | solution.py:194
  111.2 9.6 %collective-permute-start = (bf16[512,1024]{1,0:T(8,128)(2,1)}, bf16[512,1024]{1,0:T(8,128)(2,1)S(1)}, u32[]{:S(2)}, u32[]{:S(2)}) collective-permute-start(bf16[512,1024]{1,0:T(8,128)(2,1)} %dynamic-slice_bitcast_fusion.1), channel_id=1, source_target_pairs={{0,64},{64,0},{1,65},{65,1},{2,66},{66,2},{3,67},{67,3},{4,68},{68... | collective-permute-start | bytes 3145736 | tf_op jit(solution)/shard_map/ppermute | solution.py:172
  115.5 3.6 %collective-permute-start.1 = (bf16[512,64]{1,0:T(8,128)(2,1)}, bf16[512,64]{1,0:T(8,128)(2,1)}, u32[]{:S(2)}, u32[]{:S(2)}) collective-permute-start(bf16[512,64]{1,0:T(8,128)(2,1)} %bitcast.37), channel_id=1, source_target_pairs={{0,64},{64,0},{1,65},{65,1},{2,66},{66,2},{3,67},{67,3},{4,68},{68... | collective-permute-start | bytes 196616 | tf_op jit(solution)/shard_map/ppermute | solution.py:172
  122.2 1.6 copy-start.10
  137.5 1.7 copy-start.1
  142.6 1.4 copy-start
  144.0 35.6 %copy-start.9 = (bf16[2,64,1024]{2,1,0:T(8,128)(2,1)S(1)}, bf16[2,64,1024]{2,1,0:T(8,128)(2,1)}, u32[]{:S(2)}) copy-start(bf16[2,64,1024]{2,1,0:T(8,128)(2,1)} %a_ref.1) | copy-start | bytes 786436
  144.0 76.4 %all-gather.5.cloned.1.call-start = ((), (), s32[]{:S(2)}) async-start(), calls=%async_computation.8 | async-start | bytes 2621440 | tf_op jit(solution)/shard_map/all_gather | solution.py:196
  179.6 1.1 copy-start.8
  182.0 153.2 %reduce-scatter.5.cloned.1.call-start = ((), (), s32[]{:S(2)}) async-start(), calls=%async_computation.9 | async-start | bytes 2228224 | tf_op jit(solution)/shard_map/reduce_scatter | solution.py:200
  183.3 4.6 %collective-permute-start.2 = (bf16[1024,512]{1,0:T(8,128)(2,1)S(1)}, bf16[1024,512]{1,0:T(8,128)(2,1)S(1)}, u32[]{:S(2)}, u32[]{:S(2)}) collective-permute-start(bf16[1024,512]{1,0:T(8,128)(2,1)S(1)} %dynamic-slice_bitcast_fusion), channel_id=1, source_target_pairs={{0,64},{64,0},{1,65},{65,1},{2,66},{66,2},{3,67},{67,3},{4,68},{68... | collective-permute-start | bytes 3145736 | tf_op jit(solution)/shard_map/ppermute | solution.py:172
  220.4 1.6 copy-start.5
  222.0 1.6 copy-start.7
  226.5 30.8 %copy-start.3 = (bf16[16,64,1152]{2,1,0:T(8,128)(2,1)S(1)}, bf16[16,64,1152]{2,1,0:T(8,128)(2,1)}, u32[]{:S(2)}) copy-start(bf16[16,64,1152]{2,1,0:T(8,128)(2,1)} %all-gather.3.cloned.1.call-done.t_ref.m_ref) | copy-start | bytes 7077892
  261.2 1.3 copy-start.6
Sparse Core Ops, SparseCore 0:
  20.3 76.8 all-gather.2
  144.1 35.3 reduce-scatter.2
  182.1 38.2 all-gather.4
  262.6 72.4 reduce-scatter.4

commit v2 on v1

v2 whole, which is shorter than its diff:
```python
import jax
import jax.numpy as jnp
from jax import lax
from jax.experimental import pallas as pl
from jax.experimental.pallas import tpu as pltpu
from jax.sharding import Mesh, PartitionSpec as P

BF = jnp.bfloat16
F32 = jnp.float32
TOK = 16
TOP = 8
PLANE = 8
TEN = 4
RANK = 16
WIDE = 1024
META = 128
ROUTE_AT = 64
GATE_AT = 72
GROUP = 256
F16 = jnp.float16
PARAMS = pltpu.CompilerParams(vmem_limit_bytes=24 << 20)


def _matches(meta, z):
    lane = lax.broadcasted_iota(jnp.int32, (GROUP, META), 1)
    expert = jnp.where(lane < PLANE, lane + z * PLANE, -1).astype(F32)
    return [meta[:, ROUTE_AT + k : ROUTE_AT + k + 1] == expert for k in range(TOP)]


def _slots(matches):
    named = sum(m.astype(F32) for m in matches)
    row = lax.broadcasted_iota(jnp.int32, (GROUP, GROUP), 0)
    col = lax.broadcasted_iota(jnp.int32, (GROUP, GROUP), 1)
    before = ((row // TOK == col // TOK) & (col < row)).astype(BF)
    rank = jnp.dot(before, named.astype(BF), preferred_element_type=F32)
    seat = named * (rank + 1.0)
    spread = _spread()
    at = jnp.dot(seat.astype(BF), spread, preferred_element_type=F32)
    want = (col % 2 + 1).astype(F32)
    return (at == want) & (row // TOK == (col % 32) // 2)


def _spread():
    e = lax.broadcasted_iota(jnp.int32, (META, GROUP), 0)
    j = lax.broadcasted_iota(jnp.int32, (META, GROUP), 1)
    return (e == j // 32).astype(BF)


def _whole(after):
    return [pl.BlockSpec(memory_space=pl.ANY) for _ in after]


def _select_kernel(z_ref, t_ref, *rest):
    o_ref = rest[-1]
    t = t_ref[...].reshape(GROUP, WIDE + META)
    slots = _slots(_matches(t[:, WIDE:].astype(F32), z_ref[0])).astype(BF)
    out = lax.dot_general(slots, t, (((0,), (0,)), ((), ())), preferred_element_type=F32)
    o_ref[...] = out.astype(BF).reshape(PLANE, 32, WIDE + META)


def _select(z, table, half, after=()):
    return pl.pallas_call(
        _select_kernel,
        grid_spec=pltpu.PrefetchScalarGridSpec(
            num_scalar_prefetch=1,
            grid=(2,),
            in_specs=[pl.BlockSpec((8, 32, WIDE + META), lambda g, z: (g, half, 0))] + _whole(after),
            out_specs=pl.BlockSpec((PLANE, 32, WIDE + META), lambda g, z: (0, g, 0)),
        ),
        out_shape=jax.ShapeDtypeStruct((PLANE, 64, WIDE + META), BF),
        compiler_params=PARAMS,
        name="select",
    )(z, table, *after)


def _up_kernel(c_ref, x_own, x_other, mask, w_own, w_other, a_own, a_other, *rest):
    o_ref = rest[-1]
    up = jnp.dot(x_own[...], w_own[0], preferred_element_type=F32)
    up += jnp.dot(x_other[...], w_other[...], preferred_element_type=F32)
    o_ref[:, :WIDE] = up.astype(BF)
    shrink = jnp.dot(x_own[...], a_own[0], preferred_element_type=F32)
    shrink += jnp.dot(x_other[...], a_other[...], preferred_element_type=F32)
    shrink *= mask[:, :64].astype(F32)
    o_ref[:, WIDE:] = jnp.concatenate([shrink, jnp.zeros_like(shrink)], axis=1).astype(BF)


def _up(c, x, w, w_other, a, a_other, after=()):
    rows = x.shape[0]
    step = 256
    return pl.pallas_call(
        _up_kernel,
        grid_spec=pltpu.PrefetchScalarGridSpec(
            num_scalar_prefetch=1,
            grid=(rows // step,),
            in_specs=[
                pl.BlockSpec((step, 512), lambda g, c: (g, c[0])),
                pl.BlockSpec((step, 512), lambda g, c: (g, 1 - c[0])),
                pl.BlockSpec((step, META), lambda g, c: (g, WIDE // META)),
                pl.BlockSpec((1, 512, WIDE), lambda g, c: (c[0], 0, 0)),
                pl.BlockSpec((512, WIDE), lambda g, c: (0, 0)),
                pl.BlockSpec((1, 512, 64), lambda g, c: (c[0], 0, 0)),
                pl.BlockSpec((512, 64), lambda g, c: (0, 0)),
            ]
            + _whole(after),
            out_specs=pl.BlockSpec((step, WIDE + META), lambda g, c: (g, 0)),
        ),
        out_shape=jax.ShapeDtypeStruct((rows, WIDE + META), BF),
        compiler_params=PARAMS,
        name="up",
    )(c, x, x, x, w, w_other, a, a_other, *after)


def _act_kernel(c_ref, u_ref, a_ref, o_ref):
    lora = jnp.dot(u_ref[:, WIDE : WIDE + 64], a_ref[0], preferred_element_type=F32)
    v = u_ref[:, :WIDE].astype(F32) + lora
    o_ref[...] = (v / (1.0 + jnp.exp(-v))).astype(BF)


def _act(c, u, adapter_out):
    rows = u.shape[0]
    step = 64
    return pl.pallas_call(
        _act_kernel,
        grid_spec=pltpu.PrefetchScalarGridSpec(
            num_scalar_prefetch=1,
            grid=(rows // step,),
            in_specs=[
                pl.BlockSpec((step, WIDE + META), lambda g, c: (g, 0)),
                pl.BlockSpec((1, 64, WIDE), lambda g, c: (c[0], 0, 0)),
            ],
            out_specs=pl.BlockSpec((step, WIDE), lambda g, c: (g, 0)),
        ),
        out_shape=jax.ShapeDtypeStruct((rows, WIDE), BF),
        compiler_params=PARAMS,
        name="act",
    )(c, u, adapter_out)


def _down_kernel(at, own, left, right, far_low, far_high, w_own, w_other, o_ref):
    g = pl.program_id(0)
    core = at[0]

    def run(h):
        for side, w in ((core, w_own[0]), (1 - core, w_other[...])):
            cols = pl.ds(pl.multiple_of(side * 512, 512), 512)
            o_ref[:, cols] = jnp.dot(h, w, preferred_element_type=F32).astype(BF)

    @pl.when(g == 0)
    def _():
        run(own[...])

    @pl.when(g == 1)
    def _():
        run(left[...])

    @pl.when(g == 2)
    def _():
        run(right[...])

    @pl.when(g == 3)
    def _():
        run(jnp.concatenate([far_low[...], far_high[...]], axis=0))


def _down(at, parts, w, w_other):
    rows = parts[0].shape[0]
    place = (0, 3, 1, 2)

    def target(g, at):
        off = jnp.where(g == 0, place[0], jnp.where(g == 1, place[1], jnp.where(g == 2, place[2], place[3])))
        return (lax.rem(at[1] + off, 4), 0)

    return pl.pallas_call(
        _down_kernel,
        grid_spec=pltpu.PrefetchScalarGridSpec(
            num_scalar_prefetch=1,
            grid=(4,),
            in_specs=[pl.BlockSpec(p.shape, lambda g, at: (0, 0)) for p in parts]
            + [
                pl.BlockSpec((1, WIDE, 512), lambda g, at: (at[0], 0, 0)),
                pl.BlockSpec((WIDE, 512), lambda g, at: (0, 0)),
            ],
            out_specs=pl.BlockSpec((rows, WIDE), target),
        ),
        out_shape=jax.ShapeDtypeStruct((4 * rows, WIDE), BF),
        compiler_params=PARAMS,
        name="down",
    )(at, *parts, w, w_other)


def _combine_kernel(z_ref, m_ref, y_ref, *rest):
    o_ref = rest[-1]
    meta = m_ref[...].reshape(GROUP, META).astype(F32)
    matches = _matches(meta, z_ref[0])
    gate = sum(jnp.where(m, meta[:, GATE_AT + k : GATE_AT + k + 1], 0.0) for k, m in enumerate(matches))
    gates = jnp.dot(gate.astype(BF), _spread(), preferred_element_type=F32)
    weight = jnp.where(_slots(matches), gates, 0.0).astype(BF)
    out = jnp.dot(weight, y_ref[...].reshape(GROUP, WIDE), preferred_element_type=F32)
    o_ref[...] = out.astype(BF).reshape(8, 32, WIDE)


def _combine(z, table, back, half, after=()):
    return pl.pallas_call(
        _combine_kernel,
        grid_spec=pltpu.PrefetchScalarGridSpec(
            num_scalar_prefetch=1,
            grid=(2,),
            in_specs=[
                pl.BlockSpec((8, 32, META), lambda g, z: (g, half, WIDE // META)),
                pl.BlockSpec((PLANE, 32, WIDE), lambda g, z: (0, g, 0)),
            ]
            + _whole(after),
            out_specs=pl.BlockSpec((8, 32, WIDE), lambda g, z: (g, 0, 0)),
        ),
        out_shape=jax.ShapeDtypeStruct((16, 32, WIDE), BF),
        compiler_params=PARAMS,
        name="combine",
    )(z, table, back, *after)


def _total_kernel(p_ref, *rest):
    o_ref = rest[-1]
    o_ref[...] = jnp.sum(p_ref[...].astype(F32), axis=0).astype(BF)


def _total(p, after=()):
    n, rows, wide = p.shape
    return pl.pallas_call(
        _total_kernel,
        grid=(2,),
        in_specs=[pl.BlockSpec((n, rows // 2, wide), lambda g: (0, g, 0))] + _whole(after),
        out_specs=pl.BlockSpec((rows // 2, wide), lambda g: (g, 0)),
        out_shape=jax.ShapeDtypeStruct((rows, wide), BF),
        compiler_params=PARAMS,
        name="total",
    )(p, *after)


def _shift(v, axis, size, by):
    return lax.ppermute(v, axis, [(i, (i + by) % size) for i in range(size)])


def _gather_x(h):
    k = h.shape[0] // 2
    left, right = _shift(h, "x", 4, 1), _shift(h, "x", 4, -1)
    return [h, left, right, _shift(left[:k], "x", 4, 1), _shift(right[k:], "x", 4, -1)]


def per_device(tokens, route_ids, gate_weights, tenant_ids, up_weight, down_weight, adapter_in, adapter_out):
    z = lax.axis_index("z").astype(jnp.int32).reshape(1)
    core = lax.axis_index("core").astype(jnp.int32)
    c = core.reshape(1)
    at = jnp.stack([core, lax.axis_index("x").astype(jnp.int32)])

    def swapped(w):
        return _shift(lax.dynamic_index_in_dim(w, 1 - core, 0, keepdims=False), "core", 2, 1)

    owner = jnp.arange(TEN * RANK, dtype=jnp.int32) // RANK
    mask = (owner[None, :] == tenant_ids[:, None]).astype(BF)
    meta = jnp.concatenate(
        [mask, route_ids.astype(BF), gate_weights.astype(BF), jnp.zeros((TOK, META - 80), BF)], axis=1
    )
    pieces = tokens.reshape(TOK, 4, WIDE).transpose(1, 0, 2)
    rows = jnp.concatenate([pieces, jnp.broadcast_to(meta[None], (4, TOK, META))], axis=2)
    mine = lax.all_to_all(rows, "x", 0, 0, tiled=True).reshape(64, WIDE + META)
    table = lax.all_gather(mine.astype(F16), "z", axis=0).astype(BF)

    up_other, in_other, down_other = swapped(up_weight), swapped(adapter_in), swapped(down_weight)
    halves = (0, 1)
    sending, part, back = [], [], []
    for h in (0, 1):
        sending.append(_select(z, table, h, sending[-1:]))
    for h in (0, 1):
        arrived = lax.all_to_all(sending[h], ("y", "core"), 0, 0, tiled=True).reshape(512, WIDE + META)
        part.append(_up(c, arrived, up_weight, up_other, adapter_in, in_other, part[-1:]))
    for h in (0, 1):
        summed = lax.psum_scatter(part[h], "x", scatter_dimension=0, tiled=True)
        hidden = _gather_x(_act(c, summed, adapter_out))
        out = _down(at, hidden, down_weight, down_other).reshape(8, 64, WIDE)
        back.append(lax.all_to_all(out, ("y", "core"), 0, 0, tiled=True))
    plane, total = [], []
    for h in (0, 1):
        plane.append(_combine(z, table, back[h], h, plane[-1:]))
    for h in (0, 1):
        total.append(_total(lax.all_to_all(plane[h], "z", 0, 0, tiled=True), total[-1:]))
    mixed = jnp.concatenate(total, axis=0)
    home = lax.all_to_all(mixed.reshape(4, TOK, WIDE), "x", 0, 0, tiled=True)
    return home.transpose(1, 0, 2).reshape(TOK, 4 * WIDE)


def solution(mesh):
    fine = Mesh(mesh.devices.reshape(4, 2, 16, 4), ("x", "core", "z", "y"))
    dp, ex = ("x", "core"), ("z", "y")
    every = dp + ex
    placed = (
        P(every, None),
        P(every, None),
        P(every, None),
        P(every),
        P(ex, dp, None),
        P(ex, None, dp),
        P(ex, dp, None),
        P(ex, None, None),
    )
    return jax.shard_map(per_device, mesh=fine, in_specs=placed, out_specs=P(every, None), check_vma=False)
```

time: 354 us -> 362 us (1.023)
  the two profiles are of different devices: /device:TPU:8 before, /device:TPU:1 now
where the time goes in v2:
time: 362 us; the launch traced here: 355 us
  waiting for transfers between devices  122 us (34%)
  starting transfers between devices  88.9 us (25%)
  blocking collectives  69.9 us (19%)
  local copies, waits for them, and re-layouts  33.3 us (9%)
  Pallas kernels  24.2 us (7%)
  between operations  13.8 us (4%)
    all_to_all x2, waiting for transfers between devices, per_device(): lax.all_to_all(plane[h], 'z', 0, 0, tiled=True)  85.5 us
    all_gather x1, blocking collectives, per_device(): table = lax.all_gather(mine.astype(F16), 'z', axis=0).astype(BF)  40.6 us
    ppermute x11, starting transfers between devices, _shift(): return lax.ppermute(v, axis, [(i, (i + by) % size) for i in range(size)])  39.3 us
    unnamed x51, local copies, waits for them, and re-layouts  22.4 us
    all_to_all x1, blocking collectives, per_device(): lax.all_to_all(sending[h], ('y', 'core'), 0, 0, tiled=True)  20 us
    all_to_all x2, starting transfers between devices, per_device(): lax.all_to_all(plane[h], 'z', 0, 0, tiled=True)  18.9 us
    ppermute x11, waiting for transfers between devices, _shift(): return lax.ppermute(v, axis, [(i, (i + by) % size) for i in range(size)])  14.2 us
    all_to_all x1, starting transfers between devices, per_device(): lax.all_to_all(sending[h], ('y', 'core'), 0, 0, tiled=True)  13.5 us
  transfers between devices with their start and end apart: 19, of which 10 were waited for; matrix products, arithmetic and copies ran while one was open for 3% of the time, Pallas kernels for 6%

profile of v2, /device:TPU:1, one launch (start us, length us, event | category | flops | bytes accessed | tf_op | source)
XLA Modules:
  0.0 355.4 jit_solution(1114837166783805522)
XLA Ops:
  10.6 4.8 %all-to-all-start = ((bf16[4,16,1152]{2,1,0:T(8,128)(2,1)}), bf16[4,16,1152]{2,1,0:T(8,128)(2,1)S(1)}, u32[]{:S(2)}, u32[]{:S(2)}) async-start(bf16[4,16,1152]{2,1,0:T(8,128)(2,1)} %pad_maximum_fusion), calls=%async_computation | async-start | bytes 294912 | tf_op jit(solution)/shard_map/all_to_all | solution.py:265
  15.4 2.3 dynamic-slice_bitcast_fusion.1
  17.7 7.3 %collective-permute-start = (bf16[512,1024]{1,0:T(8,128)(2,1)}, bf16[512,1024]{1,0:T(8,128)(2,1)}, u32[]{:S(2)}, u32[]{:S(2)}) collective-permute-start(bf16[512,1024]{1,0:T(8,128)(2,1)} %dynamic-slice_bitcast_fusion.1), channel_id=1, source_target_pairs={{0,64},{64,0},{1,65},{65,1},{2,66},{66,2},{3,67},{67,3},{4,68},{68... | collective-permute-start | bytes 3145736 | tf_op jit(solution)/shard_map/ppermute | solution.py:240
  25.1 40.6 %all-gather.1 = f16[16,64,1152]{2,1,0:T(8,128)(2,1)S(1)} all-gather(f16[1,64,1152]{2,1,0:T(8,128)(2,1)S(1)} %bitcast.32), channel_id=1, replica_groups=mesh['x'=4,'core'=2,'z'=16,'y'=4] {'z'}, dimensions={0}, use_global_device_ids=true | all-gather | bytes 2506752 | tf_op jit(solution)/shard_map/all_gather | solution.py:266
  66.1 2.1 select.10.rest_0_
  68.3 1.0 copy-done.6
  69.3 13.5 %all-to-all-start.1 = ((bf16[8,64,1152]{2,1,0:T(8,128)(2,1)}), bf16[8,64,1152]{2,1,0:T(8,128)(2,1)S(1)}, u32[]{:S(2)}, u32[]{:S(2)}) async-start(bf16[8,64,1152]{2,1,0:T(8,128)(2,1)} %copy-done.6), calls=%async_computation.1 | async-start | bytes 2359296 | tf_op jit(solution)/shard_map/all_to_all | solution.py:274
  82.8 1.5 constant_dynamic-slice_fusion
  84.2 1.6 copy.19
  85.8 2.0 collective-permute-start.1
  87.8 1.7 copy.20.a_own
  89.5 9.7 %all-to-all-done.1 = bf16[8,64,1152]{2,1,0:T(8,128)(2,1)S(1)} async-done(((bf16[8,64,1152]{2,1,0:T(8,128)(2,1)}), bf16[8,64,1152]{2,1,0:T(8,128)(2,1)S(1)}, u32[]{:S(2)}, u32[]{:S(2)}) %all-to-all-start.1) | async-done | bytes 1179680 | tf_op jit(solution)/shard_map/all_to_all | solution.py:274
  99.3 1.6 copy-done
  101.8 3.1 up.2.rest_0_
  106.0 1.3 copy-done.7
  107.3 2.1 select.11
  109.4 20.0 %all_to_all.40 = bf16[8,64,1152]{2,1,0:T(8,128)(2,1)S(1)} all-to-all(bf16[8,64,1152]{2,1,0:T(8,128)(2,1)S(1)} %select.11), channel_id=1, replica_groups=mesh['x'=4,'core'=2,'z'=16,'y'=4] {'y','core'}, dimensions={0} | all-to-all | bytes 2359296 | tf_op jit(solution)/shard_map/all_to_all | solution.py:274
  129.5 4.0 %up.3 = bf16[512,1152]{1,0:T(8,128)(2,1)} custom-call(s32[1]{0:T(128)} %bitcast.3.c_ref, bf16[512,1152]{1,0:T(8,128)(2,1)S(1)} %bitcast.24, bf16[512,1152]{1,0:T(8,128)(2,1)S(1)} %bitcast.25, bf16[512,1152]{1,0:T(8,128)(2,1)S(1)} %bitcast.26, bf16[2,512,1024]{2,1,0:T(8,128)(2,1)S(1)} %copy-done.1, bf16[512,1024]{1,0:T(8,128)(2,1)} %collective-permute-done.w_other, ...), custom_call_target="tpu_custom_call" | custom-call | tf_op jit(solution)/shard_map/up/pallas_call | solution.py:90
  133.5 2.3 dynamic-slice_bitcast_fusion
  135.8 2.8 collective-permute-start.6
  140.9 2.1 collective-permute-start.2
  143.1 4.4 %collective-permute-start.3 = (bf16[128,1024]{1,0:T(8,128)(2,1)S(1)}, bf16[128,1024]{1,0:T(8,128)(2,1)S(1)}, u32[]{:S(2)}, u32[]{:S(2)}) collective-permute-start(bf16[128,1024]{1,0:T(8,128)(2,1)S(1)} %act.2.own), channel_id=1, source_target_pairs={{0,384},{128,0},{256,128},{384,256},{1,385},{129,1},{257,129},{385... | collective-permute-start | bytes 786440 | tf_op jit(solution)/shard_map/ppermute | solution.py:240
  148.2 3.8 %collective-permute-done.2.left = bf16[128,1024]{1,0:T(8,128)(2,1)S(1)} collective-permute-done((bf16[128,1024]{1,0:T(8,128)(2,1)S(1)}, bf16[128,1024]{1,0:T(8,128)(2,1)S(1)}, u32[]{:S(2)}, u32[]{:S(2)}) %collective-permute-start.2) | collective-permute-done | bytes 262176 | tf_op jit(solution)/shard_map/ppermute | solution.py:240
  152.7 1.9 collective-permute-start.4
  155.4 5.3 %collective-permute-start.5 = (bf16[64,1024]{1,0:T(8,128)(2,1)}, bf16[64,1024]{1,0:T(8,128)(2,1)}, u32[]{:S(2)}, u32[]{:S(2)}) collective-permute-start(bf16[64,1024]{1,0:T(8,128)(2,1)} %slice.17), channel_id=1, source_target_pairs={{0,384},{128,0},{256,128},{384,256},{1,385},{129,1},{257,129},{385... | collective-permute-start | bytes 393224 | tf_op jit(solution)/shard_map/ppermute | solution.py:240
  160.8 1.8 collective-permute-done.4.far_low
  162.6 2.0 collective-permute-done.5.far_high
  164.6 1.6 copy-done.2
  169.1 3.3 down.2
  173.4 6.0 %all-to-all-start.2 = ((bf16[8,64,1024]{2,1,0:T(8,128)(2,1)}), bf16[8,64,1024]{2,1,0:T(8,128)(2,1)S(1)}, u32[]{:S(2)}, u32[]{:S(2)}) async-start(bf16[8,64,1024]{2,1,0:T(8,128)(2,1)} %bitcast.30), calls=%async_computation.3 | async-start | bytes 2097152 | tf_op jit(solution)/shard_map/all_to_all | solution.py:280
  181.8 2.5 collective-permute-start.7
  184.3 4.6 %collective-permute-start.8 = (bf16[128,1024]{1,0:T(8,128)(2,1)S(1)}, bf16[128,1024]{1,0:T(8,128)(2,1)S(1)}, u32[]{:S(2)}, u32[]{:S(2)}) collective-permute-start(bf16[128,1024]{1,0:T(8,128)(2,1)S(1)} %act.3.own), channel_id=1, source_target_pairs={{0,384},{128,0},{256,128},{384,256},{1,385},{129,1},{257,129},{385... | collective-permute-start | bytes 786440 | tf_op jit(solution)/shard_map/ppermute | solution.py:240
  188.9 4.6 %collective-permute-done.7.left = bf16[128,1024]{1,0:T(8,128)(2,1)S(1)} collective-permute-done((bf16[128,1024]{1,0:T(8,128)(2,1)S(1)}, bf16[128,1024]{1,0:T(8,128)(2,1)S(1)}, u32[]{:S(2)}, u32[]{:S(2)}) %collective-permute-start.7) | collective-permute-done | bytes 262176 | tf_op jit(solution)/shard_map/ppermute | solution.py:240
  193.5 1.9 collective-permute-start.9
  195.5 4.6 %collective-permute-start.10 = (bf16[64,1024]{1,0:T(8,128)(2,1)S(1)}, bf16[64,1024]{1,0:T(8,128)(2,1)S(1)}, u32[]{:S(2)}, u32[]{:S(2)}) collective-permute-start(bf16[64,1024]{1,0:T(8,128)(2,1)S(1)} %slice.19), channel_id=1, source_target_pairs={{0,384},{128,0},{256,128},{384,256},{1,385},{129,1},{257,129},{385... | collective-permute-start | bytes 393224 | tf_op jit(solution)/shard_map/ppermute | solution.py:240
  200.9 1.0 collective-permute-done.10.far_high
  202.0 1.6 copy-done.3
  203.6 1.2 copy-done.12
  204.8 2.4 down.3
  208.2 6.3 %all-to-all-start.5 = ((bf16[8,64,1024]{2,1,0:T(8,128)(2,1)}), bf16[8,64,1024]{2,1,0:T(8,128)(2,1)}, u32[]{:S(2)}, u32[]{:S(2)}) async-start(bf16[8,64,1024]{2,1,0:T(8,128)(2,1)} %bitcast.31), calls=%async_computation.7 | async-start | bytes 2097152 | tf_op jit(solution)/shard_map/all_to_all | solution.py:280
  214.5 2.8 combine.2.rest_0_
  217.3 12.4 %all-to-all-done.5.y_ref = bf16[8,64,1024]{2,1,0:T(8,128)(2,1)} async-done(((bf16[8,64,1024]{2,1,0:T(8,128)(2,1)}), bf16[8,64,1024]{2,1,0:T(8,128)(2,1)}, u32[]{:S(2)}, u32[]{:S(2)}) %all-to-all-start.5) | async-done | bytes 1048608 | tf_op jit(solution)/shard_map/all_to_all | solution.py:280
  229.7 5.3 %all-to-all-start.3 = ((bf16[16,32,1024]{2,1,0:T(8,128)(2,1)}), bf16[16,32,1024]{2,1,0:T(8,128)(2,1)S(1)}, u32[]{:S(2)}, u32[]{:S(2)}) async-start(bf16[16,32,1024]{2,1,0:T(8,128)(2,1)} %combine.2.rest_0_), calls=%async_computation.4 | async-start | bytes 2097152 | tf_op jit(solution)/shard_map/all_to_all | solution.py:285
  235.0 2.9 combine.3
  239.0 40.5 %all-to-all-done.3.p_ref = bf16[16,32,1024]{2,1,0:T(8,128)(2,1)S(1)} async-done(((bf16[16,32,1024]{2,1,0:T(8,128)(2,1)}), bf16[16,32,1024]{2,1,0:T(8,128)(2,1)S(1)}, u32[]{:S(2)}, u32[]{:S(2)}) %all-to-all-start.3) | async-done | bytes 1048608 | tf_op jit(solution)/shard_map/all_to_all | solution.py:285
  279.5 13.6 %all-to-all-start.6 = ((bf16[16,32,1024]{2,1,0:T(8,128)(2,1)}), bf16[16,32,1024]{2,1,0:T(8,128)(2,1)S(1)}, u32[]{:S(2)}, u32[]{:S(2)}) async-start(bf16[16,32,1024]{2,1,0:T(8,128)(2,1)} %copy-done.10), calls=%async_computation.8 | async-start | bytes 2097152 | tf_op jit(solution)/shard_map/all_to_all | solution.py:285
  293.4 45.0 %all-to-all-done.6.p_ref = bf16[16,32,1024]{2,1,0:T(8,128)(2,1)S(1)} async-done(((bf16[16,32,1024]{2,1,0:T(8,128)(2,1)}), bf16[16,32,1024]{2,1,0:T(8,128)(2,1)S(1)}, u32[]{:S(2)}, u32[]{:S(2)}) %all-to-all-start.6) | async-done | bytes 1048608 | tf_op jit(solution)/shard_map/all_to_all | solution.py:285
  338.6 9.3 %all_to_all.41 = bf16[4,16,1024]{2,1,0:T(8,128)(2,1)S(1)} all-to-all(bf16[4,16,1024]{2,1,0:T(8,128)(2,1)S(1)} %bitcast.34), channel_id=1, replica_groups=mesh['x'=4,'core'=2,'z'=16,'y'=4] {'x'}, dimensions={0} | all-to-all | bytes 262144 | tf_op jit(solution)/shard_map/all_to_all | solution.py:287
  (83 shorter events, 21.6 us)
Async XLA Ops:
  10.6 14.4 %all-to-all-start = ((bf16[4,16,1152]{2,1,0:T(8,128)(2,1)}), bf16[4,16,1152]{2,1,0:T(8,128)(2,1)S(1)}, u32[]{:S(2)}, u32[]{:S(2)}) async-start(bf16[4,16,1152]{2,1,0:T(8,128)(2,1)} %pad_maximum_fusion), calls=%async_computation | async-start | bytes 294912 | tf_op jit(solution)/shard_map/all_to_all | solution.py:265
  17.7 71.8 %collective-permute-start = (bf16[512,1024]{1,0:T(8,128)(2,1)}, bf16[512,1024]{1,0:T(8,128)(2,1)}, u32[]{:S(2)}, u32[]{:S(2)}) collective-permute-start(bf16[512,1024]{1,0:T(8,128)(2,1)} %dynamic-slice_bitcast_fusion.1), channel_id=1, source_target_pairs={{0,64},{64,0},{1,65},{65,1},{2,66},{66,2},{3,67},{67,3},{4,68},{68... | collective-permute-start | bytes 3145736 | tf_op jit(solution)/shard_map/ppermute | solution.py:240
  68.2 1.0 copy-start.6
  69.3 30.0 %all-to-all-start.1 = ((bf16[8,64,1152]{2,1,0:T(8,128)(2,1)}), bf16[8,64,1152]{2,1,0:T(8,128)(2,1)S(1)}, u32[]{:S(2)}, u32[]{:S(2)}) async-start(bf16[8,64,1152]{2,1,0:T(8,128)(2,1)} %copy-done.6), calls=%async_computation.1 | async-start | bytes 2359296 | tf_op jit(solution)/shard_map/all_to_all | solution.py:274
  82.8 55.8 %reduce-scatter.3.cloned.1.call-start = ((), (), s32[]{:S(2)}) async-start(), calls=%async_computation.10 | async-start | bytes 1474560 | tf_op jit(solution)/shard_map/reduce_scatter | solution.py:277
  85.8 3.7 %collective-permute-start.1 = (bf16[512,64]{1,0:T(8,128)(2,1)}, bf16[512,64]{1,0:T(8,128)(2,1)}, u32[]{:S(2)}, u32[]{:S(2)}) collective-permute-start(bf16[512,64]{1,0:T(8,128)(2,1)} %bitcast.36), channel_id=1, source_target_pairs={{0,64},{64,0},{1,65},{65,1},{2,66},{66,2},{3,67},{67,3},{4,68},{68... | collective-permute-start | bytes 196616 | tf_op jit(solution)/shard_map/ppermute | solution.py:240
  99.3 1.6 copy-start
  100.9 0.9 copy-start.13
  104.9 1.0 copy-start.4
  106.0 73.5 %reduce-scatter.5.cloned.1.call-start = ((), (), s32[]{:S(2)}) async-start(), calls=%async_computation.11 | async-start | bytes 1474560 | tf_op jit(solution)/shard_map/reduce_scatter | solution.py:277
  106.0 1.3 copy-start.7
  107.3 22.2 %copy-start.5 = (bf16[512,1152]{1,0:T(8,128)(2,1)S(1)}, bf16[512,1152]{1,0:T(8,128)(2,1)}, u32[]{:S(2)}) copy-start(bf16[512,1152]{1,0:T(8,128)(2,1)} %copy-done.4) | copy-start | bytes 3538948
  109.4 20.1 %copy-start.1 = (bf16[2,512,1024]{2,1,0:T(8,128)(2,1)S(1)}, bf16[2,512,1024]{2,1,0:T(8,128)(2,1)}, u32[]{:S(2)}) copy-start(bf16[2,512,1024]{2,1,0:T(8,128)(2,1)} %w_own.6) | copy-start | bytes 6291460
  109.4 20.1 %copy-start.14 = (bf16[2,512,64]{2,1,0:T(8,128)(2,1)S(1)}, bf16[2,512,64]{2,1,0:T(8,128)(2,1)}, u32[]{:S(2)}) copy-start(bf16[2,512,64]{2,1,0:T(8,128)(2,1)} %copy.20.a_own) | copy-start | bytes 393220
  135.8 25.0 %collective-permute-start.6 = (bf16[1024,512]{1,0:T(8,128)(2,1)}, bf16[1024,512]{1,0:T(8,128)(2,1)S(1)}, u32[]{:S(2)}, u32[]{:S(2)}) collective-permute-start(bf16[1024,512]{1,0:T(8,128)(2,1)} %dynamic-slice_bitcast_fusion), channel_id=1, source_target_pairs={{0,64},{64,0},{1,65},{65,1},{2,66},{66,2},{3,67},{67,3},{4,68},{68... | collective-permute-start | bytes 3145736 | tf_op jit(solution)/shard_map/ppermute | solution.py:240
  138.6 1.0 copy-start.15
  139.5 1.0 copy-start.24
  140.9 11.0 %collective-permute-start.2 = (bf16[128,1024]{1,0:T(8,128)(2,1)S(1)}, bf16[128,1024]{1,0:T(8,128)(2,1)S(1)}, u32[]{:S(2)}, u32[]{:S(2)}) collective-permute-start(bf16[128,1024]{1,0:T(8,128)(2,1)S(1)} %act.2.own), channel_id=1, source_target_pairs={{0,128},{128,256},{256,384},{384,0},{1,129},{129,257},{257,385},{3... | collective-permute-start | bytes 786440 | tf_op jit(solution)/shard_map/ppermute | solution.py:240
  143.1 11.5 %collective-permute-start.3 = (bf16[128,1024]{1,0:T(8,128)(2,1)S(1)}, bf16[128,1024]{1,0:T(8,128)(2,1)S(1)}, u32[]{:S(2)}, u32[]{:S(2)}) collective-permute-start(bf16[128,1024]{1,0:T(8,128)(2,1)S(1)} %act.2.own), channel_id=1, source_target_pairs={{0,384},{128,0},{256,128},{384,256},{1,385},{129,1},{257,129},{385... | collective-permute-start | bytes 786440 | tf_op jit(solution)/shard_map/ppermute | solution.py:240
  147.5 0.7 copy-start.17
  152.0 2.6 copy-start.19
  152.7 9.9 %collective-permute-start.4 = (bf16[64,1024]{1,0:T(8,128)(2,1)}, bf16[64,1024]{1,0:T(8,128)(2,1)S(1)}, u32[]{:S(2)}, u32[]{:S(2)}) collective-permute-start(bf16[64,1024]{1,0:T(8,128)(2,1)} %slice.16), channel_id=1, source_target_pairs={{0,128},{128,256},{256,384},{384,0},{1,129},{129,257},{257,385},{3... | collective-permute-start | bytes 393224 | tf_op jit(solution)/shard_map/ppermute | solution.py:240
  154.6 0.8 copy-start.21
  155.4 9.2 %collective-permute-start.5 = (bf16[64,1024]{1,0:T(8,128)(2,1)}, bf16[64,1024]{1,0:T(8,128)(2,1)}, u32[]{:S(2)}, u32[]{:S(2)}) collective-permute-start(bf16[64,1024]{1,0:T(8,128)(2,1)} %slice.17), channel_id=1, source_target_pairs={{0,384},{128,0},{256,128},{384,256},{1,385},{129,1},{257,129},{385... | collective-permute-start | bytes 393224 | tf_op jit(solution)/shard_map/ppermute | solution.py:240
  160.8 11.6 %copy-start.11 = (bf16[1024,512]{1,0:T(8,128)(2,1)}, bf16[1024,512]{1,0:T(8,128)(2,1)S(1)}, u32[]{:S(2)}) copy-start(bf16[1024,512]{1,0:T(8,128)(2,1)S(1)} %collective-permute-done.6.w_other) | copy-start | bytes 3145732
  164.6 1.6 copy-start.2
  166.2 1.0 copy-start.18
  167.2 1.0 copy-start.20
  168.1 0.9 copy-start.22
  172.4 1.0 copy-start.8
  173.4 34.8 %all-to-all-start.2 = ((bf16[8,64,1024]{2,1,0:T(8,128)(2,1)}), bf16[8,64,1024]{2,1,0:T(8,128)(2,1)S(1)}, u32[]{:S(2)}, u32[]{:S(2)}) async-start(bf16[8,64,1024]{2,1,0:T(8,128)(2,1)} %bitcast.30), calls=%async_computation.3 | async-start | bytes 2097152 | tf_op jit(solution)/shard_map/all_to_all | solution.py:280
  179.4 1.0 copy-start.16
  180.4 1.0 copy-start.23
  181.8 11.7 %collective-permute-start.7 = (bf16[128,1024]{1,0:T(8,128)(2,1)S(1)}, bf16[128,1024]{1,0:T(8,128)(2,1)S(1)}, u32[]{:S(2)}, u32[]{:S(2)}) collective-permute-start(bf16[128,1024]{1,0:T(8,128)(2,1)S(1)} %act.3.own), channel_id=1, source_target_pairs={{0,128},{128,256},{256,384},{384,0},{1,129},{129,257},{257,385},{3... | collective-permute-start | bytes 786440 | tf_op jit(solution)/shard_map/ppermute | solution.py:240
  184.3 11.1 %collective-permute-start.8 = (bf16[128,1024]{1,0:T(8,128)(2,1)S(1)}, bf16[128,1024]{1,0:T(8,128)(2,1)S(1)}, u32[]{:S(2)}, u32[]{:S(2)}) collective-permute-start(bf16[128,1024]{1,0:T(8,128)(2,1)S(1)} %act.3.own), channel_id=1, source_target_pairs={{0,384},{128,0},{256,128},{384,256},{1,385},{129,1},{257,129},{385... | collective-permute-start | bytes 786440 | tf_op jit(solution)/shard_map/ppermute | solution.py:240
  193.5 7.4 %collective-permute-start.9 = (bf16[64,1024]{1,0:T(8,128)(2,1)S(1)}, bf16[64,1024]{1,0:T(8,128)(2,1)S(1)}, u32[]{:S(2)}, u32[]{:S(2)}) collective-permute-start(bf16[64,1024]{1,0:T(8,128)(2,1)S(1)} %slice.18), channel_id=1, source_target_pairs={{0,128},{128,256},{256,384},{384,0},{1,129},{129,257},{257,385},{3... | collective-permute-start | bytes 393224 | tf_op jit(solution)/shard_map/ppermute | solution.py:240
  195.5 6.5 %collective-permute-start.10 = (bf16[64,1024]{1,0:T(8,128)(2,1)S(1)}, bf16[64,1024]{1,0:T(8,128)(2,1)S(1)}, u32[]{:S(2)}, u32[]{:S(2)}) collective-permute-start(bf16[64,1024]{1,0:T(8,128)(2,1)S(1)} %slice.19), channel_id=1, source_target_pairs={{0,384},{128,0},{256,128},{384,256},{1,385},{129,1},{257,129},{385... | collective-permute-start | bytes 393224 | tf_op jit(solution)/shard_map/ppermute | solution.py:240
  202.0 1.6 copy-start.3
  203.6 1.2 copy-start.12
  207.2 1.0 copy-start.9
  208.2 21.5 %all-to-all-start.5 = ((bf16[8,64,1024]{2,1,0:T(8,128)(2,1)}), bf16[8,64,1024]{2,1,0:T(8,128)(2,1)}, u32[]{:S(2)}, u32[]{:S(2)}) async-start(bf16[8,64,1024]{2,1,0:T(8,128)(2,1)} %bitcast.31), calls=%async_computation.7 | async-start | bytes 2097152 | tf_op jit(solution)/shard_map/all_to_all | solution.py:280
  229.7 49.7 %all-to-all-start.3 = ((bf16[16,32,1024]{2,1,0:T(8,128)(2,1)}), bf16[16,32,1024]{2,1,0:T(8,128)(2,1)S(1)}, u32[]{:S(2)}, u32[]{:S(2)}) async-start(bf16[16,32,1024]{2,1,0:T(8,128)(2,1)} %combine.2.rest_0_), calls=%async_computation.4 | async-start | bytes 2097152 | tf_op jit(solution)/shard_map/all_to_all | solution.py:285
  238.0 1.0 copy-start.10
  279.5 58.9 %all-to-all-start.6 = ((bf16[16,32,1024]{2,1,0:T(8,128)(2,1)}), bf16[16,32,1024]{2,1,0:T(8,128)(2,1)S(1)}, u32[]{:S(2)}, u32[]{:S(2)}) async-start(bf16[16,32,1024]{2,1,0:T(8,128)(2,1)} %copy-done.10), calls=%async_computation.8 | async-start | bytes 2097152 | tf_op jit(solution)/shard_map/all_to_all | solution.py:285
Sparse Core Ops, SparseCore 0:
  106.1 24.0 reduce-scatter.2
  133.6 33.6 reduce-scatter.4

commit v3 on v1

v3 whole, which is shorter than its diff:
```python
import jax
import jax.numpy as jnp
from jax import lax
from jax.experimental import pallas as pl
from jax.experimental.pallas import tpu as pltpu
from jax.sharding import Mesh, PartitionSpec as P

BF = jnp.bfloat16
F16 = jnp.float16
F32 = jnp.float32
TOK = 16
TOP = 8
PLANE = 8
TEN = 4
RANK = 16
PIECE = 1024
WIDE = 4096
META = 128
ROUTE_AT = 64
GATE_AT = 72
GROUP = 256
AROUND = (0, 3, 1, 2)


def _matches(meta, z):
    lane = lax.broadcasted_iota(jnp.int32, (GROUP, META), 1)
    expert = jnp.where(lane < PLANE, lane + z * PLANE, -1).astype(F32)
    return [meta[:, ROUTE_AT + k : ROUTE_AT + k + 1] == expert for k in range(TOP)]


def _slots(matches):
    named = sum(m.astype(F32) for m in matches)
    row = lax.broadcasted_iota(jnp.int32, (GROUP, GROUP), 0)
    col = lax.broadcasted_iota(jnp.int32, (GROUP, GROUP), 1)
    before = ((row // TOK == col // TOK) & (col < row)).astype(BF)
    rank = jnp.dot(before, named.astype(BF), preferred_element_type=F32)
    seat = named * (rank + 1.0)
    spread = _spread()
    at = jnp.dot(seat.astype(BF), spread, preferred_element_type=F32)
    want = (col % 2 + 1).astype(F32)
    return (at == want) & (row // TOK == (col % 32) // 2)


def _spread():
    e = lax.broadcasted_iota(jnp.int32, (META, GROUP), 0)
    j = lax.broadcasted_iota(jnp.int32, (META, GROUP), 1)
    return (e == j // 32).astype(BF)


def _params(mib):
    return pltpu.CompilerParams(vmem_limit_bytes=mib << 20)


def _piece(g, x):
    off = jnp.where(g == 0, AROUND[0], jnp.where(g == 1, AROUND[1], jnp.where(g == 2, AROUND[2], AROUND[3])))
    return lax.rem(x + off, 4)


def _select_kernel(z_ref, m_ref, t_ref, o_ref):
    slots = _slots(_matches(m_ref[...].reshape(GROUP, META).astype(F32), z_ref[0])).astype(BF)
    t = t_ref[...].reshape(GROUP, t_ref.shape[2])
    out = lax.dot_general(slots, t, (((0,), (0,)), ((), ())), preferred_element_type=F32)
    o_ref[...] = out.astype(BF).reshape(o_ref.shape)


def _select(z, table):
    width = (WIDE + META) // 3
    return pl.pallas_call(
        _select_kernel,
        grid_spec=pltpu.PrefetchScalarGridSpec(
            num_scalar_prefetch=1,
            grid=(3,),
            in_specs=[
                pl.BlockSpec((16, TOK, META), lambda g, z: (0, 0, WIDE // META)),
                pl.BlockSpec((16, TOK, width), lambda g, z: (0, 0, g)),
            ],
            out_specs=pl.BlockSpec((PLANE, 32, width), lambda g, z: (0, 0, g)),
        ),
        out_shape=jax.ShapeDtypeStruct((PLANE, 32, WIDE + META), BF),
        compiler_params=_params(24),
        name="select",
    )(z, table, table)


def _up_kernel(at, x_ref, m_ref, own, left, right, far_low, far_high, a_in, a_out, o_ref, acc, shrink):
    g = pl.program_id(0)

    def add(w):
        acc[...] += jnp.dot(x_ref[...], w, preferred_element_type=F32)

    @pl.when(g == 0)
    def _():
        acc[...] = jnp.dot(x_ref[...], own[...], preferred_element_type=F32)
        shrink[...] = jnp.zeros_like(shrink)

    @pl.when(g == 1)
    def _():
        add(left[...])

    @pl.when(g == 2)
    def _():
        add(right[...])

    shrink[...] += jnp.dot(x_ref[...], a_in[...], preferred_element_type=F32)

    @pl.when(g == 3)
    def _():
        acc[...] += jnp.dot(x_ref[:, :512], far_low[...], preferred_element_type=F32)
        acc[...] += jnp.dot(x_ref[:, 512:], far_high[...], preferred_element_type=F32)
        kept = shrink[...] * m_ref[:, :64].astype(F32)
        high = kept.astype(BF)
        low = (kept - high.astype(F32)).astype(BF)
        v = acc[...] + jnp.dot(high, a_out[0], preferred_element_type=F32)
        v += jnp.dot(low, a_out[0], preferred_element_type=F32)
        o_ref[...] = (v / (1.0 + jnp.exp(-v))).astype(BF)


def _up(at, rows, w, a_in, a_out):
    full = lambda p: pl.BlockSpec(p.shape, lambda g, at: (0, 0))
    return pl.pallas_call(
        _up_kernel,
        grid_spec=pltpu.PrefetchScalarGridSpec(
            num_scalar_prefetch=1,
            grid=(4,),
            in_specs=[
                pl.BlockSpec((GROUP, PIECE), lambda g, at: (0, _piece(g, at[1]))),
                pl.BlockSpec((GROUP, META), lambda g, at: (0, WIDE // META)),
            ]
            + [full(p) for p in w]
            + [
                pl.BlockSpec((PIECE, 64), lambda g, at: (_piece(g, at[1]), 0)),
                pl.BlockSpec((1, 64, PIECE), lambda g, at: (at[0], 0, 0)),
            ],
            out_specs=pl.BlockSpec((GROUP, PIECE), lambda g, at: (0, 0)),
            scratch_shapes=[pltpu.VMEM((GROUP, PIECE), F32), pltpu.VMEM((GROUP, 64), F32)],
        ),
        out_shape=jax.ShapeDtypeStruct((GROUP, PIECE), BF),
        compiler_params=_params(32),
        name="up",
    )(at, rows, rows, *w, a_in, a_out)


def _down_kernel(at, h_ref, own, left, right, far_low, far_high, o_ref):
    g = pl.program_id(0)
    for i, w in enumerate((own, left, right)):

        @pl.when(g == i)
        def _():
            o_ref[...] = jnp.dot(h_ref[...], w[...], preferred_element_type=F32).astype(BF)

    @pl.when(g == 3)
    def _():
        out = jnp.dot(h_ref[:, :512], far_low[...], preferred_element_type=F32)
        out += jnp.dot(h_ref[:, 512:], far_high[...], preferred_element_type=F32)
        o_ref[...] = out.astype(BF)


def _down(at, hidden, w):
    full = lambda p: pl.BlockSpec(p.shape, lambda g, at: (0, 0))
    return pl.pallas_call(
        _down_kernel,
        grid_spec=pltpu.PrefetchScalarGridSpec(
            num_scalar_prefetch=1,
            grid=(4,),
            in_specs=[full(hidden)] + [full(p) for p in w],
            out_specs=pl.BlockSpec((GROUP, PIECE), lambda g, at: (0, _piece(g, at[1]))),
        ),
        out_shape=jax.ShapeDtypeStruct((GROUP, WIDE), BF),
        compiler_params=_params(32),
        name="down",
    )(at, hidden, *w)


def _combine_kernel(z_ref, m_ref, y_ref, o_ref, weight):
    @pl.when(pl.program_id(0) == 0)
    def _():
        meta = m_ref[...].reshape(GROUP, META).astype(F32)
        matches = _matches(meta, z_ref[0])
        gate = sum(jnp.where(m, meta[:, GATE_AT + k : GATE_AT + k + 1], 0.0) for k, m in enumerate(matches))
        gates = jnp.dot(gate.astype(BF), _spread(), preferred_element_type=F32)
        weight[...] = jnp.where(_slots(matches), gates, 0.0).astype(BF)

    out = jnp.dot(weight[...], y_ref[...].reshape(GROUP, PIECE), preferred_element_type=F32)
    o_ref[...] = out.astype(BF)


def _combine(z, table, back):
    return pl.pallas_call(
        _combine_kernel,
        grid_spec=pltpu.PrefetchScalarGridSpec(
            num_scalar_prefetch=1,
            grid=(4,),
            in_specs=[
                pl.BlockSpec((16, TOK, META), lambda g, z: (0, 0, WIDE // META)),
                pl.BlockSpec((PLANE, 32, PIECE), lambda g, z: (0, 0, g)),
            ],
            out_specs=pl.BlockSpec((GROUP, PIECE), lambda g, z: (0, g)),
            scratch_shapes=[pltpu.VMEM((GROUP, GROUP), BF)],
        ),
        out_shape=jax.ShapeDtypeStruct((GROUP, WIDE), BF),
        compiler_params=_params(24),
        name="combine",
    )(z, table, back)


def _shift(v, axis, size, by):
    return lax.ppermute(v, axis, [(i, (i + by) % size) for i in range(size)])


def _gather_x(w):
    left, right = _shift(w, "x", 4, 1), _shift(w, "x", 4, -1)
    return [w, left, right, _shift(left[:512], "x", 4, 1), _shift(right[512:], "x", 4, -1)]


def per_device(tokens, route_ids, gate_weights, tenant_ids, up_weight, down_weight, adapter_in, adapter_out):
    z = lax.axis_index("z").astype(jnp.int32).reshape(1)
    core = lax.axis_index("core").astype(jnp.int32)
    at = jnp.stack([core, lax.axis_index("x").astype(jnp.int32)])

    def both(w, axis):
        own = lax.dynamic_index_in_dim(w, core, 0, keepdims=False)
        other = _shift(lax.dynamic_index_in_dim(w, 1 - core, 0, keepdims=False), "core", 2, 1)
        first, second = jnp.where(core == 0, own, other), jnp.where(core == 0, other, own)
        return jnp.concatenate([first, second], axis=axis)

    w_up = _gather_x(both(up_weight, 0))
    w_down = _gather_x(both(down_weight, 1))
    a_in = lax.dynamic_index_in_dim(lax.all_gather(adapter_in, ("x", "core"), axis=1, tiled=True), core, 0, keepdims=False)

    owner = jnp.arange(TEN * RANK, dtype=jnp.int32) // RANK
    mask = (owner[None, :] == tenant_ids[:, None]).astype(F16)
    meta = jnp.concatenate(
        [mask, route_ids.astype(F16), gate_weights.astype(F16), jnp.zeros((TOK, META - 80), F16)], axis=1
    )
    mine = jnp.concatenate([tokens.astype(F16), meta], axis=1)
    table = lax.all_gather(mine, "z", axis=0).astype(BF)
    sending = _select(z, table)
    arrived = lax.all_to_all(sending, ("y", "core"), 0, 0, tiled=True).reshape(GROUP, WIDE + META)
    hidden = _up(at, arrived, w_up, a_in, adapter_out)
    out = _down(at, hidden, w_down).reshape(PLANE, 32, WIDE)
    back = lax.all_to_all(out, ("y", "core"), 0, 0, tiled=True)
    partial = _combine(z, table, back)
    return lax.psum_scatter(partial, "z", scatter_dimension=0, tiled=True)


def solution(mesh):
    fine = Mesh(mesh.devices.reshape(4, 2, 16, 4), ("x", "core", "z", "y"))
    dp, ex = ("x", "core"), ("z", "y")
    every = dp + ex
    placed = (
        P(every, None),
        P(every, None),
        P(every, None),
        P(every),
        P(ex, dp, None),
        P(ex, None, dp),
        P(ex, dp, None),
        P(ex, None, None),
    )
    return jax.shard_map(per_device, mesh=fine, in_specs=placed, out_specs=P(every, None), check_vma=False)
```

time: 354 us -> 292 us (0.82)
  the two profiles are of different devices: /device:TPU:8 before, /device:TPU:4 now
where the time goes in v3:
time: 292 us; the launch traced here: 291 us
  waiting for transfers between devices  112 us (38%)
  blocking collectives  78.9 us (27%)
  starting transfers between devices  38 us (13%)
  Pallas kernels  21.5 us (7%)
  local copies, waits for them, and re-layouts  20.3 us (7%)
  between operations  13.7 us (5%)
  other arithmetic  6.72 us (2%)
    reduce_scatter x1, waiting for transfers between devices, per_device(): return lax.psum_scatter(partial, 'z', scatter_dimension=0, tiled=True)  73.9 us
    all_gather x1, blocking collectives, per_device(): table = lax.all_gather(mine, 'z', axis=0).astype(BF)  48.9 us
    ppermute x10, waiting for transfers between devices, _shift(): return lax.ppermute(v, axis, [(i, (i + by) % size) for i in range(size)])  37.7 us
    ppermute x10, starting transfers between devices, _shift(): return lax.ppermute(v, axis, [(i, (i + by) % size) for i in range(size)])  33.5 us
    all_to_all x1, blocking collectives, per_device(): back = lax.all_to_all(out, ('y', 'core'), 0, 0, tiled=True)  30 us
    pallas_call x1, Pallas kernels, _up(): pl.pallas_call(_up_kernel, grid_spec=pltpu.PrefetchScalarGridSpec(num_sca...  8.81 us
    pallas_call x1, Pallas kernels, _down(): pl.pallas_call(_down_kernel, grid_spec=pltpu.PrefetchScalarGridSpec(num_s...  7.13 us
  transfers between devices with their start and end apart: 13, of which 6 were waited for; matrix products, arithmetic and copies ran while one was open for 8% of the time, Pallas kernels for 4%

profile of v3, /device:TPU:4, one launch (start us, length us, event | category | flops | bytes accessed | tf_op | source)
XLA Modules:
  0.0 290.8 jit_solution(4521014545822909283)
XLA Ops:
  6.5 2.4 dynamic-slice_bitcast_fusion.1
  8.9 1.9 collective-permute-start
  10.9 2.3 dynamic-slice_bitcast_fusion
  13.2 2.4 collective-permute-start.5
  15.6 0.0 all-gather.4.cloned.1.call-update
  15.6 1.4 bitcast_select_fusion.3
  17.0 0.0 copy-start.4
  17.0 1.5 pad_maximum_fusion.own
  18.5 3.1 %collective-permute-start.1 = (bf16[1024,1024]{1,0:T(8,128)(2,1)}, bf16[1024,1024]{1,0:T(8,128)(2,1)}, u32[]{:S(2)}, u32[]{:S(2)}) collective-permute-start(bf16[1024,1024]{1,0:T(8,128)(2,1)} %pad_maximum_fusion.own), channel_id=1, source_target_pairs={{0,128},{128,256},{256,384},{384,0},{1,129},{129,257},{257,385},{3... | collective-permute-start | bytes 6291464 | tf_op jit(solution)/shard_map/ppermute | solution.py:207
  21.6 2.7 collective-permute-start.2
  24.4 0.1 bitcast_select_fusion.1
  24.6 0.0 copy-start.5
  24.6 1.6 pad_maximum_fusion.1.own
  26.3 6.9 %collective-permute-start.6 = (bf16[1024,1024]{1,0:T(8,128)(2,1)}, bf16[1024,1024]{1,0:T(8,128)(2,1)}, u32[]{:S(2)}, u32[]{:S(2)}) collective-permute-start(bf16[1024,1024]{1,0:T(8,128)(2,1)} %pad_maximum_fusion.1.own), channel_id=1, source_target_pairs={{0,128},{128,256},{256,384},{384,0},{1,129},{129,257},{257,385},{3... | collective-permute-start | bytes 6291464 | tf_op jit(solution)/shard_map/ppermute | solution.py:207
  33.2 1.9 collective-permute-start.7
  35.2 0.1 copy.9
  35.3 0.1 copy.10
  35.4 0.1 compare_convert_fusion
  35.5 0.1 concatenate.9
  35.6 48.9 %all-gather.5 = f16[256,4224]{1,0:T(8,128)(2,1)} all-gather(f16[16,4224]{1,0:T(8,128)(2,1)S(1)} %concatenate.9), channel_id=2, replica_groups=mesh['x'=4,'core'=2,'z'=16,'y'=4] {'z'}, dimensions={0}, use_global_device_ids=true | all-gather | bytes 2297856 | tf_op jit(solution)/shard_map/all_gather | solution.py:236
  84.5 1.9 convert_element_type.20
  86.3 3.3 %select.9 = bf16[8,32,4224]{2,1,0:T(8,128)(2,1)S(1)} custom-call(s32[1]{0:T(128)} %bitcast.z_ref, bf16[16,16,4224]{2,1,0:T(8,128)(2,1)S(1)} %bitcast.17, bf16[16,16,4224]{2,1,0:T(8,128)(2,1)S(1)} %bitcast.18), custom_call_target="tpu_custom_call" | custom-call | tf_op jit(solution)/shard_map/select/pallas_call | solution.py:68
  89.6 1.3 copy-done
  91.0 4.5 %all-to-all-start = ((bf16[8,32,4224]{2,1,0:T(8,128)(2,1)}), bf16[8,32,4224]{2,1,0:T(8,128)(2,1)}, u32[]{:S(2)}, u32[]{:S(2)}) async-start(bf16[8,32,4224]{2,1,0:T(8,128)(2,1)} %copy-done), calls=%async_computation | async-start | bytes 4325376 | tf_op jit(solution)/shard_map/all_to_all | solution.py:238
  95.5 0.0 reduce-scatter.2.cloned.1.call-start
  95.5 2.4 slice.16
  97.9 4.1 %collective-permute-start.3 = (bf16[512,1024]{1,0:T(8,128)(2,1)}, bf16[512,1024]{1,0:T(8,128)(2,1)}, u32[]{:S(2)}, u32[]{:S(2)}) collective-permute-start(bf16[512,1024]{1,0:T(8,128)(2,1)} %slice.16), channel_id=1, source_target_pairs={{0,128},{128,256},{256,384},{384,0},{1,129},{129,257},{257,385},{3... | collective-permute-start | bytes 3145736 | tf_op jit(solution)/shard_map/ppermute | solution.py:207
  102.0 2.3 slice.17
  104.3 1.9 collective-permute-start.4
  106.2 12.2 %collective-permute-done.6.left = bf16[1024,1024]{1,0:T(8,128)(2,1)} collective-permute-done((bf16[1024,1024]{1,0:T(8,128)(2,1)}, bf16[1024,1024]{1,0:T(8,128)(2,1)}, u32[]{:S(2)}, u32[]{:S(2)}) %collective-permute-start.6) | collective-permute-done | bytes 2097184 | tf_op jit(solution)/shard_map/ppermute | solution.py:207
  118.4 2.3 slice.18
  120.7 6.6 %collective-permute-start.8 = (bf16[512,1024]{1,0:T(8,128)(2,1)}, bf16[512,1024]{1,0:T(8,128)(2,1)}, u32[]{:S(2)}, u32[]{:S(2)}) collective-permute-start(bf16[512,1024]{1,0:T(8,128)(2,1)} %slice.18), channel_id=1, source_target_pairs={{0,128},{128,256},{256,384},{384,0},{1,129},{129,257},{257,385},{3... | collective-permute-start | bytes 3145736 | tf_op jit(solution)/shard_map/ppermute | solution.py:207
  127.3 2.2 slice.19
  129.5 1.9 collective-permute-start.9
  131.5 0.1 pad_add_fusion.at
  131.5 1.8 constant_dynamic-slice_fusion
  133.4 1.5 copy.11
  135.0 5.9 %collective-permute-done.3.far_low = bf16[512,1024]{1,0:T(8,128)(2,1)} collective-permute-done((bf16[512,1024]{1,0:T(8,128)(2,1)}, bf16[512,1024]{1,0:T(8,128)(2,1)}, u32[]{:S(2)}, u32[]{:S(2)}) %collective-permute-start.3) | collective-permute-done | bytes 1048608 | tf_op jit(solution)/shard_map/ppermute | solution.py:207
  140.9 7.0 %collective-permute-done.4.far_high = bf16[512,1024]{1,0:T(8,128)(2,1)} collective-permute-done((bf16[512,1024]{1,0:T(8,128)(2,1)}, bf16[512,1024]{1,0:T(8,128)(2,1)}, u32[]{:S(2)}, u32[]{:S(2)}) %collective-permute-start.4) | collective-permute-done | bytes 1048608 | tf_op jit(solution)/shard_map/ppermute | solution.py:207
  147.8 8.8 %up.1.h_ref = bf16[256,1024]{1,0:T(8,128)(2,1)S(1)} custom-call(s32[2]{0:T(128)S(1)} %pad_add_fusion.at, bf16[256,4224]{1,0:T(8,128)(2,1)} %bitcast.4.x_ref.m_ref, bf16[256,4224]{1,0:T(8,128)(2,1)} %bitcast.4.x_ref.m_ref, bf16[1024,1024]{1,0:T(8,128)(2,1)} %pad_maximum_fusion.own, bf16[1024,1024]{1,0:T(8,128)(2,1)} %collective-permute-done.1.left, ...), custom_call_target="tpu_custom_call" | custom-call | tf_op jit(solution)/shard_map/up/pallas_call | solution.py:120
  156.6 5.8 %collective-permute-done.8.far_low = bf16[512,1024]{1,0:T(8,128)(2,1)} collective-permute-done((bf16[512,1024]{1,0:T(8,128)(2,1)}, bf16[512,1024]{1,0:T(8,128)(2,1)}, u32[]{:S(2)}, u32[]{:S(2)}) %collective-permute-start.8) | collective-permute-done | bytes 1048608 | tf_op jit(solution)/shard_map/ppermute | solution.py:207
  162.4 7.0 %collective-permute-done.9.far_high = bf16[512,1024]{1,0:T(8,128)(2,1)} collective-permute-done((bf16[512,1024]{1,0:T(8,128)(2,1)}, bf16[512,1024]{1,0:T(8,128)(2,1)}, u32[]{:S(2)}, u32[]{:S(2)}) %collective-permute-start.9) | collective-permute-done | bytes 1048608 | tf_op jit(solution)/shard_map/ppermute | solution.py:207
  169.3 7.1 %down.1 = bf16[256,4096]{1,0:T(8,128)(2,1)S(1)} custom-call(s32[2]{0:T(128)S(1)} %pad_add_fusion.at, bf16[256,1024]{1,0:T(8,128)(2,1)S(1)} %up.1.h_ref, bf16[1024,1024]{1,0:T(8,128)(2,1)} %pad_maximum_fusion.1.own, bf16[1024,1024]{1,0:T(8,128)(2,1)} %collective-permute-done.6.left, bf16[1024,1024]{1,0:T(8,128)(2,1)} %collective-permute-done.7.right, ...), custom_call_target="tpu_custom_call" | custom-call | tf_op jit(solution)/shard_map/down/pallas_call | solution.py:160
  176.5 30.0 %all_to_all.10.y_ref = bf16[8,32,4096]{2,1,0:T(8,128)(2,1)S(1)} all-to-all(bf16[8,32,4096]{2,1,0:T(8,128)(2,1)S(1)} %bitcast.20), channel_id=1, replica_groups=mesh['x'=4,'core'=2,'z'=16,'y'=4] {'y','core'}, dimensions={0} | all-to-all | bytes 4194304 | tf_op jit(solution)/shard_map/all_to_all | solution.py:241
  206.4 2.3 combine.1
  208.7 1.3 copy-done.1
  210.0 0.0 reduce-scatter.2.cloned.1.call-update
  210.1 73.9 %reduce-scatter.2.cloned.1.call-done = bf16[16,4096]{1,0:T(8,128)(2,1)} async-done(((bf16[256,4096]{1,0:T(8,128)(2,1)}), bf16[16,4096]{1,0:T(8,128)(2,1)}) %reduce-scatter.2.cloned.1.call-update) | async-done | bytes 131088 | tf_op jit(solution)/shard_map/reduce_scatter | solution.py:243
  (27 shorter events, 0.1 us)
Async XLA Ops:
  6.5 125.0 %all-gather.4.cloned.1.call-start = ((), (), s32[]{:S(2)}) async-start(), calls=%async_computation.3 | async-start | bytes 1179648 | tf_op jit(solution)/shard_map/all_gather | solution.py:228
  6.5 9.1 %copy-start.3 = (bf16[2,512,1024]{2,1,0:T(8,128)(2,1)S(1)}, bf16[2,512,1024]{2,1,0:T(8,128)(2,1)}, u32[]{:S(2)}) copy-start(bf16[2,512,1024]{2,1,0:T(8,128)(2,1)} %param.12) | copy-start | bytes 6291460
  8.9 6.7 %collective-permute-start = (bf16[512,1024]{1,0:T(8,128)(2,1)}, bf16[512,1024]{1,0:T(8,128)(2,1)}, u32[]{:S(2)}, u32[]{:S(2)}) collective-permute-start(bf16[512,1024]{1,0:T(8,128)(2,1)} %dynamic-slice_bitcast_fusion.1), channel_id=1, source_target_pairs={{0,64},{64,0},{1,65},{65,1},{2,66},{66,2},{3,67},{67,3},{4,68},{68... | collective-permute-start | bytes 3145736 | tf_op jit(solution)/shard_map/ppermute | solution.py:207
  13.2 11.2 %collective-permute-start.5 = (bf16[1024,512]{1,0:T(8,128)(2,1)}, bf16[1024,512]{1,0:T(8,128)(2,1)S(1)}, u32[]{:S(2)}, u32[]{:S(2)}) collective-permute-start(bf16[1024,512]{1,0:T(8,128)(2,1)} %dynamic-slice_bitcast_fusion), channel_id=1, source_target_pairs={{0,64},{64,0},{1,65},{65,1},{2,66},{66,2},{3,67},{67,3},{4,68},{68... | collective-permute-start | bytes 3145736 | tf_op jit(solution)/shard_map/ppermute | solution.py:207
  17.0 7.4 %copy-start.4 = (bf16[2,1024,512]{2,1,0:T(8,128)(2,1)S(1)}, bf16[2,1024,512]{2,1,0:T(8,128)(2,1)}, u32[]{:S(2)}) copy-start(bf16[2,1024,512]{2,1,0:T(8,128)(2,1)} %param.13) | copy-start | bytes 6291460
  18.5 77.0 %collective-permute-start.1 = (bf16[1024,1024]{1,0:T(8,128)(2,1)}, bf16[1024,1024]{1,0:T(8,128)(2,1)}, u32[]{:S(2)}, u32[]{:S(2)}) collective-permute-start(bf16[1024,1024]{1,0:T(8,128)(2,1)} %pad_maximum_fusion.own), channel_id=1, source_target_pairs={{0,128},{128,256},{256,384},{384,0},{1,129},{129,257},{257,385},{3... | collective-permute-start | bytes 6291464 | tf_op jit(solution)/shard_map/ppermute | solution.py:207
  21.6 80.3 %collective-permute-start.2 = (bf16[1024,1024]{1,0:T(8,128)(2,1)}, bf16[1024,1024]{1,0:T(8,128)(2,1)}, u32[]{:S(2)}, u32[]{:S(2)}) collective-permute-start(bf16[1024,1024]{1,0:T(8,128)(2,1)} %pad_maximum_fusion.own), channel_id=1, source_target_pairs={{0,384},{128,0},{256,128},{384,256},{1,385},{129,1},{257,129},{385... | collective-permute-start | bytes 6291464 | tf_op jit(solution)/shard_map/ppermute | solution.py:207
  24.6 10.6 %copy-start.5 = (bf16[16,4096]{1,0:T(8,128)(2,1)S(1)}, bf16[16,4096]{1,0:T(8,128)(2,1)}, u32[]{:S(2)}) copy-start(bf16[16,4096]{1,0:T(8,128)(2,1)} %param.8) | copy-start | bytes 393220
  24.6 10.6 %copy-start.6 = (s32[16,8]{0,1:T(8,128)S(1)}, s32[16,8]{0,1:T(8,128)}, u32[]{:S(2)}) copy-start(s32[16,8]{0,1:T(8,128)} %param.9) | copy-start | bytes 1540
  24.6 10.7 %copy-start.7 = (f32[16,8]{0,1:T(8,128)S(1)}, f32[16,8]{0,1:T(8,128)}, u32[]{:S(2)}) copy-start(f32[16,8]{0,1:T(8,128)} %param.10) | copy-start | bytes 1540
  24.6 10.8 %copy-start.8 = (s32[16]{0:T(128)S(1)}, s32[16]{0:T(128)}, u32[]{:S(2)}) copy-start(s32[16]{0:T(128)} %param.11) | copy-start | bytes 196
  26.3 92.1 %collective-permute-start.6 = (bf16[1024,1024]{1,0:T(8,128)(2,1)}, bf16[1024,1024]{1,0:T(8,128)(2,1)}, u32[]{:S(2)}, u32[]{:S(2)}) collective-permute-start(bf16[1024,1024]{1,0:T(8,128)(2,1)} %pad_maximum_fusion.1.own), channel_id=1, source_target_pairs={{0,128},{128,256},{256,384},{384,0},{1,129},{129,257},{257,385},{3... | collective-permute-start | bytes 6291464 | tf_op jit(solution)/shard_map/ppermute | solution.py:207
  33.2 94.1 %collective-permute-start.7 = (bf16[1024,1024]{1,0:T(8,128)(2,1)}, bf16[1024,1024]{1,0:T(8,128)(2,1)}, u32[]{:S(2)}, u32[]{:S(2)}) collective-permute-start(bf16[1024,1024]{1,0:T(8,128)(2,1)} %pad_maximum_fusion.1.own), channel_id=1, source_target_pairs={{0,384},{128,0},{256,128},{384,256},{1,385},{129,1},{257,129},{385... | collective-permute-start | bytes 6291464 | tf_op jit(solution)/shard_map/ppermute | solution.py:207
  89.6 1.4 copy-start
  91.0 44.0 %all-to-all-start = ((bf16[8,32,4224]{2,1,0:T(8,128)(2,1)}), bf16[8,32,4224]{2,1,0:T(8,128)(2,1)}, u32[]{:S(2)}, u32[]{:S(2)}) async-start(bf16[8,32,4224]{2,1,0:T(8,128)(2,1)} %copy-done), calls=%async_computation | async-start | bytes 4325376 | tf_op jit(solution)/shard_map/all_to_all | solution.py:238
  95.5 188.5 %reduce-scatter.2.cloned.1.call-start = ((), (), s32[]{:S(2)}) async-start(), calls=%async_computation.4 | async-start | bytes 2228224 | tf_op jit(solution)/shard_map/reduce_scatter | solution.py:243
  97.9 43.0 %collective-permute-start.3 = (bf16[512,1024]{1,0:T(8,128)(2,1)}, bf16[512,1024]{1,0:T(8,128)(2,1)}, u32[]{:S(2)}, u32[]{:S(2)}) collective-permute-start(bf16[512,1024]{1,0:T(8,128)(2,1)} %slice.16), channel_id=1, source_target_pairs={{0,128},{128,256},{256,384},{384,0},{1,129},{129,257},{257,385},{3... | collective-permute-start | bytes 3145736 | tf_op jit(solution)/shard_map/ppermute | solution.py:207
  104.3 43.5 %collective-permute-start.4 = (bf16[512,1024]{1,0:T(8,128)(2,1)}, bf16[512,1024]{1,0:T(8,128)(2,1)}, u32[]{:S(2)}, u32[]{:S(2)}) collective-permute-start(bf16[512,1024]{1,0:T(8,128)(2,1)} %slice.17), channel_id=1, source_target_pairs={{0,384},{128,0},{256,128},{384,256},{1,385},{129,1},{257,129},{385... | collective-permute-start | bytes 3145736 | tf_op jit(solution)/shard_map/ppermute | solution.py:207
  120.7 27.1 %copy-start.2 = (bf16[2,64,1024]{2,1,0:T(8,128)(2,1)S(1)}, bf16[2,64,1024]{2,1,0:T(8,128)(2,1)}, u32[]{:S(2)}) copy-start(bf16[2,64,1024]{2,1,0:T(8,128)(2,1)} %a_out.1) | copy-start | bytes 786436
  120.7 41.7 %collective-permute-start.8 = (bf16[512,1024]{1,0:T(8,128)(2,1)}, bf16[512,1024]{1,0:T(8,128)(2,1)}, u32[]{:S(2)}, u32[]{:S(2)}) collective-permute-start(bf16[512,1024]{1,0:T(8,128)(2,1)} %slice.18), channel_id=1, source_target_pairs={{0,128},{128,256},{256,384},{384,0},{1,129},{129,257},{257,385},{3... | collective-permute-start | bytes 3145736 | tf_op jit(solution)/shard_map/ppermute | solution.py:207
  129.5 39.8 %collective-permute-start.9 = (bf16[512,1024]{1,0:T(8,128)(2,1)}, bf16[512,1024]{1,0:T(8,128)(2,1)}, u32[]{:S(2)}, u32[]{:S(2)}) collective-permute-start(bf16[512,1024]{1,0:T(8,128)(2,1)} %slice.19), channel_id=1, source_target_pairs={{0,384},{128,0},{256,128},{384,256},{1,385},{129,1},{257,129},{385... | collective-permute-start | bytes 3145736 | tf_op jit(solution)/shard_map/ppermute | solution.py:207
  208.7 1.3 copy-start.1
Sparse Core Ops, SparseCore 0:
  15.7 36.7 all-gather.3
  210.2 73.7 reduce-scatter.1

commit v4 on v3

v4 whole, which is shorter than its diff:
```python
import jax
import jax.numpy as jnp
from jax import lax
from jax.experimental import pallas as pl
from jax.experimental.pallas import tpu as pltpu
from jax.sharding import Mesh, PartitionSpec as P

BF = jnp.bfloat16
F16 = jnp.float16
F32 = jnp.float32
TOK = 16
TOP = 8
DEST = 16
TEN = 4
RANK = 16
PIECE = 1024
WIDE = 4096
META = 128
ROUTE_AT = 64
GATE_AT = 72
ROWS = 256
TOKS = 128
SCALE_AT = 96
LIFT = 4096.0
def _params(mib):
    return pltpu.CompilerParams(vmem_limit_bytes=mib << 20)


def _matches(meta, z1):
    lane = lax.broadcasted_iota(jnp.int32, (TOKS, META), 1)
    expert = (z1 * 2 + lane % 2) * 8 + (lane // 4) * 2 + (lane // 2) % 2
    expert = jnp.where(lane < DEST, expert, -1).astype(F32)
    return [meta[:, ROUTE_AT + k : ROUTE_AT + k + 1] == expert for k in range(TOP)]


def _spread():
    e = lax.broadcasted_iota(jnp.int32, (META, ROWS), 0)
    j = lax.broadcasted_iota(jnp.int32, (META, ROWS), 1)
    return (e == j // 16).astype(BF)


def _slots(matches):
    named = sum(m.astype(F32) for m in matches)
    row = lax.broadcasted_iota(jnp.int32, (TOKS, TOKS), 0)
    col = lax.broadcasted_iota(jnp.int32, (TOKS, TOKS), 1)
    before = ((row // TOK == col // TOK) & (col < row)).astype(BF)
    rank = jnp.dot(before, named.astype(BF), preferred_element_type=F32)
    seat = named * (rank + 1.0)
    at = jnp.dot(seat.astype(BF), _spread(), preferred_element_type=F32)
    tok = lax.broadcasted_iota(jnp.int32, (TOKS, ROWS), 0)
    slot = lax.broadcasted_iota(jnp.int32, (TOKS, ROWS), 1)
    return (at == (slot % 2 + 1).astype(F32)) & (tok // TOK == (slot % 16) // 2)


def _select_kernel(z_ref, m_ref, t_ref, o_ref):
    slots = _slots(_matches(m_ref[...].reshape(TOKS, META).astype(F32), z_ref[0])).astype(BF)
    t = t_ref[...].reshape(TOKS, t_ref.shape[2])
    out = lax.dot_general(slots, t, (((0,), (0,)), ((), ())), preferred_element_type=F32)
    o_ref[...] = out.astype(BF).reshape(o_ref.shape)


def _select(z1, table):
    width = (WIDE + META) // 3
    return pl.pallas_call(
        _select_kernel,
        grid_spec=pltpu.PrefetchScalarGridSpec(
            num_scalar_prefetch=1,
            grid=(3,),
            in_specs=[
                pl.BlockSpec((8, TOK, META), lambda g, z: (0, 0, WIDE // META)),
                pl.BlockSpec((8, TOK, width), lambda g, z: (0, 0, g)),
            ],
            out_specs=pl.BlockSpec((DEST, 16, width), lambda g, z: (0, 0, g)),
        ),
        out_shape=jax.ShapeDtypeStruct((DEST, 16, WIDE + META), BF),
        compiler_params=_params(24),
        name="select",
    )(z1, table, table)


def _up_kernel(c_ref, x_own, x_other, m_ref, t_ref, w_own, w_other, a_own, a_other, a_out, o_ref, acc, shrink):
    g = pl.program_id(0)
    lanes = (((1,), (1,)), ((), ()))
    more = jnp.dot(x_own[...], w_own[0], preferred_element_type=F32)
    more += jnp.dot(x_other[...], w_other[0], preferred_element_type=F32)
    less = lax.dot_general(x_own[...], a_own[0], lanes, preferred_element_type=F32)
    less += lax.dot_general(x_other[...], a_other[0], lanes, preferred_element_type=F32)

    @pl.when(g == 0)
    def _():
        acc[...] = more
        shrink[...] = less

    @pl.when(g > 0)
    def _():
        acc[...] += more
        shrink[...] += less

    @pl.when(g == 3)
    def _():
        kept = shrink[...] * m_ref[:, :64].astype(F32)
        high = kept.astype(BF)
        low = (kept - high.astype(F32)).astype(BF)
        v = acc[...] + jnp.dot(high, a_out[0], preferred_element_type=F32)
        v += jnp.dot(low, a_out[0], preferred_element_type=F32)
        hidden = (v / (1.0 + jnp.exp(-v))).astype(BF).astype(F32)
        peak = jnp.max(jnp.abs(hidden), axis=1, keepdims=True)
        power = jnp.floor(jnp.log2(jnp.maximum(peak, 1e-30)))
        o_ref[:, :PIECE] = (hidden * jnp.exp2(-power)).astype(BF)
        lane = lax.broadcasted_iota(jnp.int32, (ROWS, META), 1)
        meta = jnp.concatenate([t_ref[...].reshape(TOKS, META), jnp.zeros((ROWS - TOKS, META), BF)], axis=0)
        o_ref[:, PIECE:] = jnp.where(lane == SCALE_AT, power, meta.astype(F32)).astype(BF)


def _up(c, rows, table, w_own, w_other, a_in, a_out):
    own = lambda g, c: (2 * g + c[0])
    other = lambda g, c: (2 * g + 1 - c[0])
    return pl.pallas_call(
        _up_kernel,
        grid_spec=pltpu.PrefetchScalarGridSpec(
            num_scalar_prefetch=1,
            grid=(4,),
            in_specs=[
                pl.BlockSpec((ROWS, 512), lambda g, c: (0, own(g, c))),
                pl.BlockSpec((ROWS, 512), lambda g, c: (0, other(g, c))),
                pl.BlockSpec((ROWS, META), lambda g, c: (0, WIDE // META)),
                pl.BlockSpec((8, TOK, META), lambda g, c: (0, 0, WIDE // META)),
                pl.BlockSpec((1, 512, PIECE), lambda g, c: (g, 0, 0)),
                pl.BlockSpec((1, 512, PIECE), lambda g, c: (g, 0, 0)),
                pl.BlockSpec((1, 64, 512), lambda g, c: (own(g, c), 0, 0)),
                pl.BlockSpec((1, 64, 512), lambda g, c: (other(g, c), 0, 0)),
                pl.BlockSpec((1, 64, PIECE), lambda g, c: (c[0], 0, 0)),
            ],
            out_specs=pl.BlockSpec((ROWS, PIECE + META), lambda g, c: (0, 0)),
            scratch_shapes=[pltpu.VMEM((ROWS, PIECE), F32), pltpu.VMEM((ROWS, 64), F32)],
        ),
        out_shape=jax.ShapeDtypeStruct((ROWS, PIECE + META), BF),
        compiler_params=_params(32),
        name="up",
    )(c, rows, rows, rows, table, w_own, w_other, a_in, a_in, a_out)


def _down_kernel(c_ref, h_ref, m_ref, w_own, w_other, o_ref):
    scale = jnp.exp2(m_ref[0, :, SCALE_AT : SCALE_AT + 1].astype(F32))
    for side, w in ((c_ref[0], w_own[0]), (1 - c_ref[0], w_other[...])):
        cols = pl.ds(pl.multiple_of(side * 512, 512), 512)
        out = jnp.dot(h_ref[0], w, preferred_element_type=F32) * scale
        o_ref[:, :, :, cols] = out.astype(BF).reshape(DEST, 1, 16, 512)


def _down(c, hidden, w, w_other):
    return pl.pallas_call(
        _down_kernel,
        grid_spec=pltpu.PrefetchScalarGridSpec(
            num_scalar_prefetch=1,
            grid=(4,),
            in_specs=[
                pl.BlockSpec((1, ROWS, PIECE), lambda g, c: (g, 0, 0)),
                pl.BlockSpec((1, ROWS, META), lambda g, c: (g, 0, PIECE // META)),
                pl.BlockSpec((1, PIECE, 512), lambda g, c: (c[0], 0, 0)),
                pl.BlockSpec((PIECE, 512), lambda g, c: (0, 0)),
            ],
            out_specs=pl.BlockSpec((DEST, 1, 16, PIECE), lambda g, c: (0, g, 0, 0)),
        ),
        out_shape=jax.ShapeDtypeStruct((DEST, 4, 16, PIECE), BF),
        compiler_params=_params(24),
        name="down",
    )(c, hidden, hidden, w, w_other)


def _combine_kernel(z_ref, m_ref, y_ref, o_ref):
    meta = m_ref[0].astype(F32)
    matches = _matches(meta, z_ref[0])
    gate = sum(jnp.where(m, meta[:, GATE_AT + k : GATE_AT + k + 1], 0.0) for k, m in enumerate(matches))
    gates = jnp.dot(gate.astype(BF), _spread(), preferred_element_type=F32)
    weight = jnp.where(_slots(matches), gates, 0.0).astype(BF)
    out = jnp.dot(weight, y_ref[...].reshape(ROWS, PIECE), preferred_element_type=F32)
    o_ref[...] = out.astype(BF).reshape(8, 1, TOK, PIECE)


def _combine(z1, hidden, back):
    return pl.pallas_call(
        _combine_kernel,
        grid_spec=pltpu.PrefetchScalarGridSpec(
            num_scalar_prefetch=1,
            grid=(4,),
            in_specs=[
                pl.BlockSpec((1, TOKS, META), lambda g, z: (g, 0, PIECE // META)),
                pl.BlockSpec((DEST, 1, 16, PIECE), lambda g, z: (0, g, 0, 0)),
            ],
            out_specs=pl.BlockSpec((8, 1, TOK, PIECE), lambda g, z: (0, g, 0, 0)),
        ),
        out_shape=jax.ShapeDtypeStruct((8, 4, TOK, PIECE), BF),
        compiler_params=_params(24),
        name="combine",
    )(z1, hidden, back)


def _swap(v):
    return lax.ppermute(v, "core", [(0, 1), (1, 0)])


def per_device(tokens, route_ids, gate_weights, tenant_ids, up_weight, down_weight, adapter_in, adapter_out):
    z1 = lax.axis_index("z1").astype(jnp.int32).reshape(1)
    core = lax.axis_index("core").astype(jnp.int32)
    c = core.reshape(1)
    one = lambda w, i: lax.dynamic_index_in_dim(w, i, 0, keepdims=False)

    w_other = _swap(lax.all_gather(one(up_weight, 1 - core), "x", axis=0))
    w_own = lax.all_gather(one(up_weight, core), "x", axis=0)
    down_other = _swap(one(down_weight, 1 - core))

    owner = jnp.arange(TEN * RANK, dtype=jnp.int32) // RANK
    mask = (owner[None, :] == tenant_ids[:, None]).astype(F16)
    meta = jnp.concatenate(
        [mask, route_ids.astype(F16), gate_weights.astype(F16), jnp.zeros((TOK, META - 80), F16)], axis=1
    )
    mine = jnp.concatenate([(tokens.astype(F32) * LIFT).astype(F16), meta], axis=1)
    table = lax.all_gather(mine, "z1", axis=0).astype(F32)
    lift = jnp.where(jnp.arange(WIDE + META) < WIDE, 1.0 / LIFT, 1.0)
    table = (table * lift).astype(BF)
    sending = _select(z1, table)
    arrived = lax.all_to_all(sending, ("y", "core", "z0"), 0, 0, tiled=True).reshape(ROWS, WIDE + META)

    a_in = (adapter_in.transpose(0, 2, 1).astype(F32) * LIFT).astype(F16)
    a_in = lax.all_gather(a_in, ("x", "core"), axis=0)
    a_in = (lax.dynamic_index_in_dim(a_in, core, 1, keepdims=False).astype(F32) / LIFT).astype(BF)

    hidden = _up(c, arrived, table, w_own, w_other, a_in, adapter_out)
    hidden = lax.all_gather(hidden.astype(F16), "x", axis=0).astype(BF)
    out = _down(c, hidden, down_weight, down_other)
    back = lax.all_to_all(out, ("y", "core", "z0"), 0, 0, tiled=True)
    partial = _combine(z1, hidden, back)
    mixed = lax.psum_scatter(partial, "z1", scatter_dimension=0, tiled=True).reshape(4, TOK, PIECE)
    home = lax.all_to_all(mixed, "x", 0, 0, tiled=True)
    return home.transpose(1, 0, 2).reshape(TOK, WIDE)


def solution(mesh):
    fine = Mesh(mesh.devices.reshape(4, 2, 8, 2, 4), ("x", "core", "z1", "z0", "y"))
    dp, ex = ("x", "core"), ("z1", "z0", "y")
    every = dp + ex
    placed = (
        P(every, None),
        P(every, None),
        P(every, None),
        P(every),
        P(ex, dp, None),
        P(ex, None, dp),
        P(ex, dp, None),
        P(ex, None, None),
    )
    return jax.shard_map(per_device, mesh=fine, in_specs=placed, out_specs=P(every, None), check_vma=False)
```

time: 292 us -> 272 us (0.932)
  the two profiles are of different devices: /device:TPU:4 before, /device:TPU:1 now
where the time goes in v4:
time: 272 us; the launch traced here: 268 us
  blocking collectives  118 us (43%)
  waiting for transfers between devices  90.4 us (33%)
  Pallas kernels  17.1 us (6%)
  starting transfers between devices  15.9 us (6%)
  between operations  13.3 us (5%)
  local copies, waits for them, and re-layouts  12.1 us (4%)
    reduce_scatter x1, waiting for transfers between devices, per_device(): lax.psum_scatter(partial, 'z1', scatter_dimension=0, tiled=True)  46.8 us
    all_gather x1, blocking collectives, per_device(): table = lax.all_gather(mine, 'z1', axis=0).astype(F32)  38 us
    all_gather x1, waiting for transfers between devices, per_device(): w_own = lax.all_gather(one(up_weight, core), 'x', axis=0)  36.3 us
    all_to_all x1, blocking collectives, per_device(): back = lax.all_to_all(out, ('y', 'core', 'z0'), 0, 0, tiled=True)  33.1 us
    all_gather x1, blocking collectives, per_device(): hidden = lax.all_gather(hidden.astype(F16), 'x', axis=0).astype(BF)  22.4 us
    all_gather x1, blocking collectives, per_device(): a_in = lax.all_gather(a_in, ('x', 'core'), axis=0)  14.2 us
    all_to_all x1, starting transfers between devices, per_device(): lax.all_to_all(sending, ('y', 'core', 'z0'), 0, 0, tiled=True)  11.2 us
    all_to_all x1, blocking collectives, per_device(): home = lax.all_to_all(mixed, 'x', 0, 0, tiled=True)  9.87 us
  transfers between devices with their start and end apart: 6, of which 3 were waited for; matrix products, arithmetic and copies ran while one was open for 2% of the time, Pallas kernels for 3%

profile of v4, /device:TPU:1, one launch (start us, length us, event | category | flops | bytes accessed | tf_op | source)
XLA Modules:
  0.0 268.3 jit_solution(11005245929823905391)
XLA Ops:
  6.5 0.0 all-gather.11.cloned.1.call-start
  6.5 3.1 %constant_dynamic-slice_fusion = (bf16[1,512,1024]{2,1,0:T(8,128)(2,1)}, bf16[1,512,1024]{2,1,0:T(8,128)(2,1)}) fusion(bf16[2,512,1024]{2,1,0:T(8,128)(2,1)} %param.12, s32[]{:T(128)S(6)} %select_n.31, s32[]{:T(128)S(6)} %select_n.30), kind=kLoop, calls=%fused_computation.12 | loop fusion | bytes 4194312 | tf_op jit(solution)/shard_map/jit(dynamic_index_in_dim)/dynamic_slice | solution.py:207
  9.6 0.0 all-gather.11.cloned.1.call-update
  9.7 0.0 copy-done.7
  9.7 0.1 copy.15
  9.8 0.0 copy-done.8
  9.8 0.1 copy.16
  9.9 0.0 copy-done.9
  9.9 0.1 compare_convert_fusion
  10.0 0.0 copy-done.5
  10.0 0.1 concatenate.3
  10.1 38.0 %all-gather.13 = f16[128,4224]{1,0:T(8,128)(2,1)S(1)} all-gather(f16[16,4224]{1,0:T(8,128)(2,1)S(1)} %concatenate.3), channel_id=2, replica_groups=mesh['x'=4,'core'=2,'z1'=8,'z0'=2,'y'=4] {'z1'}, dimensions={0}, use_global_device_ids=true | all-gather | bytes 1216512 | tf_op jit(solution)/shard_map/all_gather | solution.py:219
  48.2 0.2 fusion.m_ref.t_ref
  48.4 2.7 %select.9 = bf16[16,16,4224]{2,1,0:T(8,128)(2,1)S(1)} custom-call(s32[1]{0:T(128)} %bitcast.z_ref, bf16[8,16,4224]{2,1,0:T(8,128)(2,1)S(1)} %fusion.m_ref.t_ref, bf16[8,16,4224]{2,1,0:T(8,128)(2,1)S(1)} %fusion.m_ref.t_ref), custom_call_target="tpu_custom_call" | custom-call | tf_op jit(solution)/shard_map/select/pallas_call | solution.py:64
  51.1 0.0 copy-start
  51.1 1.3 copy-done
  52.4 11.2 %all-to-all-start = ((bf16[16,16,4224]{2,1,0:T(8,128)(2,1)}), bf16[16,16,4224]{2,1,0:T(8,128)(2,1)S(1)}, u32[]{:S(2)}, u32[]{:S(2)}) async-start(bf16[16,16,4224]{2,1,0:T(8,128)(2,1)} %copy-done), calls=%async_computation | async-start | bytes 4325376 | tf_op jit(solution)/shard_map/all_to_all | solution.py:223
  63.7 0.0 all-gather.9.cloned.1.call-start
  63.7 0.7 all-gather.9.cloned.1.call-update
  64.4 0.0 copy-start.4
  64.4 0.0 reduce-scatter.2.cloned.1.call-start
  64.5 6.6 %all-gather.11.cloned.1.call-done = bf16[4,512,1024]{2,1,0:T(8,128)(2,1)} async-done(((bf16[1,512,1024]{2,1,0:T(8,128)(2,1)}), bf16[4,512,1024]{2,1,0:T(8,128)(2,1)}) %all-gather.11.cloned.1.call-update) | async-done | bytes 4194320 | tf_op jit(solution)/shard_map/all_gather | solution.py:209
  71.0 2.7 %collective-permute-start = (bf16[4,512,1024]{2,1,0:T(8,128)(2,1)}, bf16[4,512,1024]{2,1,0:T(8,128)(2,1)}, u32[]{:S(2)}, u32[]{:S(2)}) collective-permute-start(bf16[4,512,1024]{2,1,0:T(8,128)(2,1)} %all-gather.11.cloned.1.call-done), channel_id=1, source_target_pairs={{0,64},{64,0},{1,65},{65,1},{2,66},{66,2},{3,67},{67,3},{4,68},{68... | collective-permute-start | bytes 12582920 | tf_op jit(solution)/shard_map/ppermute | solution.py:200
  73.8 2.3 dynamic-slice_bitcast_fusion
  76.1 1.9 collective-permute-start.1
  78.0 0.0 copy-done.6
  78.0 14.2 %all-gather.12 = f16[16,64,512]{2,1,0:T(8,128)(2,1)S(1)} all-gather(f16[2,64,512]{2,1,0:T(8,128)(2,1)S(1)} %fusion.2), channel_id=3, replica_groups=mesh['x'=4,'core'=2,'z1'=8,'z0'=2,'y'=4] {'x','core'}, dimensions={0}, use_global_device_ids=true | all-gather | bytes 1179648 | tf_op jit(solution)/shard_map/all_gather | solution.py:226
  92.3 0.9 fusion.1.a_own.a_other
  93.2 36.3 %all-gather.9.cloned.1.call-done.w_own = bf16[4,512,1024]{2,1,0:T(8,128)(2,1)} async-done(((bf16[1,512,1024]{2,1,0:T(8,128)(2,1)}), bf16[4,512,1024]{2,1,0:T(8,128)(2,1)}) %all-gather.9.cloned.1.call-update) | async-done | bytes 4194320 | tf_op jit(solution)/shard_map/all_gather | solution.py:210
  129.5 0.0 all-to-all-done
  129.5 0.0 collective-permute-done.w_other
  129.5 0.0 copy-done.4
  129.5 0.0 copy-start.2
  129.5 1.0 copy-done.2
  130.6 2.2 copy-done.3
  132.8 6.4 %up.1 = bf16[256,1152]{1,0:T(8,128)(2,1)S(1)} custom-call(s32[1]{0:T(128)} %bitcast.1.c_ref, bf16[256,4224]{1,0:T(8,128)(2,1)S(1)} %bitcast.22, bf16[256,4224]{1,0:T(8,128)(2,1)S(1)} %bitcast.23, bf16[256,4224]{1,0:T(8,128)(2,1)S(1)} %bitcast.24, bf16[8,16,4224]{2,1,0:T(8,128)(2,1)S(1)} %fusion.m_ref.t_ref, bf16[4,512,1024]{2,1,0:T(8,128)(2,1)S(1)} %copy-done.3, ...), custom_call_target="tpu_custom_call" | custom-call | tf_op jit(solution)/shard_map/up/pallas_call | solution.py:118
  139.2 0.1 convert_element_type.59
  139.3 22.4 %all-gather.14 = f16[1024,1152]{1,0:T(8,128)(2,1)S(1)} all-gather(f16[256,1152]{1,0:T(8,128)(2,1)S(1)} %convert_element_type.59), channel_id=4, replica_groups=mesh['x'=4,'core'=2,'z1'=8,'z0'=2,'y'=4] {'x'}, dimensions={0}, use_global_device_ids=true | all-gather | bytes 2949120 | tf_op jit(solution)/shard_map/all_gather | solution.py:230
  161.7 0.3 convert_element_type.62
  162.0 0.0 collective-permute-done.1.w_other
  162.0 1.2 copy-done.1
  163.3 4.4 %down.1 = bf16[16,4,16,1024]{3,2,1,0:T(8,128)(2,1)S(1)} custom-call(s32[1]{0:T(128)} %bitcast.1.c_ref, bf16[4,256,1152]{2,1,0:T(8,128)(2,1)S(1)} %bitcast.19, bf16[4,256,1152]{2,1,0:T(8,128)(2,1)S(1)} %bitcast.20, bf16[2,1024,512]{2,1,0:T(8,128)(2,1)S(1)} %copy-done.1, bf16[1024,512]{1,0:T(8,128)(2,1)} %collective-permute-done.1.w_other), custom_call_target="tpu_custom_call" | custom-call | tf_op jit(solution)/shard_map/down/pallas_call | solution.py:152
  167.7 33.1 %all_to_all.15.y_ref = bf16[16,4,16,1024]{3,2,1,0:T(8,128)(2,1)S(1)} all-to-all(bf16[16,4,16,1024]{3,2,1,0:T(8,128)(2,1)S(1)} %down.1), channel_id=1, replica_groups=mesh['x'=4,'core'=2,'z1'=8,'z0'=2,'y'=4] {'y','core','z0'}, dimensions={0} | all-to-all | bytes 4194304 | tf_op jit(solution)/shard_map/all_to_all | solution.py:232
  200.9 3.5 %combine.1 = bf16[8,4,16,1024]{3,2,1,0:T(8,128)(2,1)} custom-call(s32[1]{0:T(128)} %bitcast.z_ref, bf16[4,256,1152]{2,1,0:T(8,128)(2,1)S(1)} %bitcast.21, bf16[16,4,16,1024]{3,2,1,0:T(8,128)(2,1)S(1)} %all_to_all.15.y_ref), custom_call_target="tpu_custom_call" | custom-call | tf_op jit(solution)/shard_map/combine/pallas_call | solution.py:182
  204.4 0.0 reduce-scatter.2.cloned.1.call-update
  204.4 46.8 %reduce-scatter.2.cloned.1.call-done = bf16[1,4,16,1024]{3,2,1,0:T(8,128)(2,1)} async-done(((bf16[8,4,16,1024]{3,2,1,0:T(8,128)(2,1)}), bf16[1,4,16,1024]{3,2,1,0:T(8,128)(2,1)}) %reduce-scatter.2.cloned.1.call-update) | async-done | bytes 131088 | tf_op jit(solution)/shard_map/reduce_scatter | solution.py:234
  251.2 9.9 %all_to_all.16 = bf16[4,16,1024]{2,1,0:T(8,128)(2,1)S(1)} all-to-all(bf16[4,16,1024]{2,1,0:T(8,128)(2,1)} %bitcast.28), channel_id=1, replica_groups=mesh['x'=4,'core'=2,'z1'=8,'z0'=2,'y'=4] {'x'}, dimensions={0} | all-to-all | bytes 262144 | tf_op jit(solution)/shard_map/all_to_all | solution.py:235
  261.1 0.7 copy.20
  (14 shorter events, 0.1 us)
Async XLA Ops:
  6.5 64.5 %all-gather.11.cloned.1.call-start = ((), (), s32[]{:S(2)}) async-start(), calls=%async_computation.5 | async-start | bytes 5242880 | tf_op jit(solution)/shard_map/all_gather | solution.py:209
  6.5 3.1 %copy-start.7 = (s32[16,8]{0,1:T(8,128)S(1)}, s32[16,8]{0,1:T(8,128)}, u32[]{:S(2)}) copy-start(s32[16,8]{0,1:T(8,128)} %param.9) | copy-start | bytes 1540
  6.5 3.2 %copy-start.8 = (f32[16,8]{0,1:T(8,128)S(1)}, f32[16,8]{0,1:T(8,128)}, u32[]{:S(2)}) copy-start(f32[16,8]{0,1:T(8,128)} %param.10) | copy-start | bytes 1540
  6.5 3.3 %copy-start.9 = (s32[16]{0:T(128)S(1)}, s32[16]{0:T(128)}, u32[]{:S(2)}) copy-start(s32[16]{0:T(128)} %param.11) | copy-start | bytes 196
  6.5 3.4 %copy-start.5 = (bf16[16,4096]{1,0:T(8,128)(2,1)S(1)}, bf16[16,4096]{1,0:T(8,128)(2,1)}, u32[]{:S(2)}) copy-start(bf16[16,4096]{1,0:T(8,128)(2,1)} %param.8) | copy-start | bytes 393220
  51.1 1.3 copy-start
  52.4 77.1 %all-to-all-start = ((bf16[16,16,4224]{2,1,0:T(8,128)(2,1)}), bf16[16,16,4224]{2,1,0:T(8,128)(2,1)S(1)}, u32[]{:S(2)}, u32[]{:S(2)}) async-start(bf16[16,16,4224]{2,1,0:T(8,128)(2,1)} %copy-done), calls=%async_computation | async-start | bytes 4325376 | tf_op jit(solution)/shard_map/all_to_all | solution.py:223
  63.7 65.9 %all-gather.9.cloned.1.call-start = ((), (), s32[]{:S(2)}) async-start(), calls=%async_computation.4 | async-start | bytes 5242880 | tf_op jit(solution)/shard_map/all_gather | solution.py:210
  64.4 65.1 %copy-start.4 = (bf16[2,64,1024]{2,1,0:T(8,128)(2,1)S(1)}, bf16[2,64,1024]{2,1,0:T(8,128)(2,1)}, u32[]{:S(2)}) copy-start(bf16[2,64,1024]{2,1,0:T(8,128)(2,1)} %a_out.1) | copy-start | bytes 786436
  64.4 186.8 %reduce-scatter.2.cloned.1.call-start = ((), (), s32[]{:S(2)}) async-start(), calls=%async_computation.6 | async-start | bytes 1179648 | tf_op jit(solution)/shard_map/reduce_scatter | solution.py:234
  71.0 6.9 %copy-start.6 = (bf16[2,512,64]{1,2,0:T(8,128)(2,1)S(1)}, bf16[2,512,64]{1,2,0:T(8,128)(2,1)}, u32[]{:S(2)}) copy-start(bf16[2,512,64]{1,2,0:T(8,128)(2,1)} %param.14) | copy-start | bytes 393220
  71.0 58.5 %collective-permute-start = (bf16[4,512,1024]{2,1,0:T(8,128)(2,1)}, bf16[4,512,1024]{2,1,0:T(8,128)(2,1)}, u32[]{:S(2)}, u32[]{:S(2)}) collective-permute-start(bf16[4,512,1024]{2,1,0:T(8,128)(2,1)} %all-gather.11.cloned.1.call-done), channel_id=1, source_target_pairs={{0,64},{64,0},{1,65},{65,1},{2,66},{66,2},{3,67},{67,3},{4,68},{68... | collective-permute-start | bytes 12582920 | tf_op jit(solution)/shard_map/ppermute | solution.py:200
  76.1 86.0 %collective-permute-start.1 = (bf16[1024,512]{1,0:T(8,128)(2,1)}, bf16[1024,512]{1,0:T(8,128)(2,1)}, u32[]{:S(2)}, u32[]{:S(2)}) collective-permute-start(bf16[1024,512]{1,0:T(8,128)(2,1)} %dynamic-slice_bitcast_fusion), channel_id=1, source_target_pairs={{0,64},{64,0},{1,65},{65,1},{2,66},{66,2},{3,67},{67,3},{4,68},{68... | collective-permute-start | bytes 3145736 | tf_op jit(solution)/shard_map/ppermute | solution.py:200
  129.5 1.0 copy-start.2
  130.6 2.2 copy-start.3
  161.7 1.6 copy-start.1
Sparse Core Ops, SparseCore 0:
  9.8 61.2 all-gather.10
  73.1 56.3 all-gather.8
  204.5 46.6 reduce-scatter.1

commit v5 on v4

--- a/solution.py
+++ b/solution.py
@@ -52,14 +52,15 @@
     return (at == (slot % 2 + 1).astype(F32)) & (tok // TOK == (slot % 16) // 2)
 
 
-def _select_kernel(z_ref, m_ref, t_ref, o_ref):
+def _select_kernel(z_ref, m_ref, t_ref, *rest):
+    o_ref = rest[-1]
     slots = _slots(_matches(m_ref[...].reshape(TOKS, META).astype(F32), z_ref[0])).astype(BF)
     t = t_ref[...].reshape(TOKS, t_ref.shape[2])
     out = lax.dot_general(slots, t, (((0,), (0,)), ((), ())), preferred_element_type=F32)
     o_ref[...] = out.astype(BF).reshape(o_ref.shape)
 
 
-def _select(z1, table):
+def _select(z1, table, after):
     width = (WIDE + META) // 3
     return pl.pallas_call(
         _select_kernel,
@@ -69,32 +70,46 @@
             in_specs=[
                 pl.BlockSpec((8, TOK, META), lambda g, z: (0, 0, WIDE // META)),
                 pl.BlockSpec((8, TOK, width), lambda g, z: (0, 0, g)),
-            ],
+            ]
+            + [pl.BlockSpec(memory_space=pl.ANY) for _ in after],
             out_specs=pl.BlockSpec((DEST, 16, width), lambda g, z: (0, 0, g)),
         ),
         out_shape=jax.ShapeDtypeStruct((DEST, 16, WIDE + META), BF),
         compiler_params=_params(24),
         name="select",
-    )(z1, table, table)
-
-
-def _up_kernel(c_ref, x_own, x_other, m_ref, t_ref, w_own, w_other, a_own, a_other, a_out, o_ref, acc, shrink):
+    )(z1, table, table, *after)
+
+
+def _around(g, x):
+    return lax.rem(x + jnp.where(g == 0, 0, jnp.where(g == 1, 3, jnp.where(g == 2, 1, 2))), 4)
+
+
+def _up_kernel(at, x_ref, m_ref, t_ref, mid, left, right, far_low, far_high, a_low, a_high, a_out, o_ref, acc, shrink):
     g = pl.program_id(0)
     lanes = (((1,), (1,)), ((), ()))
-    more = jnp.dot(x_own[...], w_own[0], preferred_element_type=F32)
-    more += jnp.dot(x_other[...], w_other[0], preferred_element_type=F32)
-    less = lax.dot_general(x_own[...], a_own[0], lanes, preferred_element_type=F32)
-    less += lax.dot_general(x_other[...], a_other[0], lanes, preferred_element_type=F32)
 
     @pl.when(g == 0)
     def _():
-        acc[...] = more
-        shrink[...] = less
-
-    @pl.when(g > 0)
-    def _():
-        acc[...] += more
-        shrink[...] += less
+        acc[...] = jnp.dot(x_ref[...], mid[...], preferred_element_type=F32)
+        shrink[...] = jnp.zeros_like(shrink)
+
+    @pl.when(g == 1)
+    def _():
+        acc[...] += jnp.dot(x_ref[...], left[...], preferred_element_type=F32)
+
+    @pl.when(g == 2)
+    def _():
+        acc[...] += jnp.dot(x_ref[...], right[...], preferred_element_type=F32)
+
+    @pl.when(g == 3)
+    def _():
+        far = jnp.dot(x_ref[:, :512], far_low[...], preferred_element_type=F32)
+        far += jnp.dot(x_ref[:, 512:], far_high[...], preferred_element_type=F32)
+        acc[...] += far
+
+    less = lax.dot_general(x_ref[:, :512], a_low[0], lanes, preferred_element_type=F32)
+    less += lax.dot_general(x_ref[:, 512:], a_high[0], lanes, preferred_element_type=F32)
+    shrink[...] += less
 
     @pl.when(g == 3)
     def _():
@@ -112,32 +127,30 @@
         o_ref[:, PIECE:] = jnp.where(lane == SCALE_AT, power, meta.astype(F32)).astype(BF)
 
 
-def _up(c, rows, table, w_own, w_other, a_in, a_out):
-    own = lambda g, c: (2 * g + c[0])
-    other = lambda g, c: (2 * g + 1 - c[0])
+def _up(at, rows, table, w, a_in, a_out):
     return pl.pallas_call(
         _up_kernel,
         grid_spec=pltpu.PrefetchScalarGridSpec(
             num_scalar_prefetch=1,
             grid=(4,),
             in_specs=[
-                pl.BlockSpec((ROWS, 512), lambda g, c: (0, own(g, c))),
-                pl.BlockSpec((ROWS, 512), lambda g, c: (0, other(g, c))),
-                pl.BlockSpec((ROWS, META), lambda g, c: (0, WIDE // META)),
-                pl.BlockSpec((8, TOK, META), lambda g, c: (0, 0, WIDE // META)),
-                pl.BlockSpec((1, 512, PIECE), lambda g, c: (g, 0, 0)),
-                pl.BlockSpec((1, 512, PIECE), lambda g, c: (g, 0, 0)),
-                pl.BlockSpec((1, 64, 512), lambda g, c: (own(g, c), 0, 0)),
-                pl.BlockSpec((1, 64, 512), lambda g, c: (other(g, c), 0, 0)),
-                pl.BlockSpec((1, 64, PIECE), lambda g, c: (c[0], 0, 0)),
+                pl.BlockSpec((ROWS, PIECE), lambda g, at: (0, _around(g, at[1]))),
+                pl.BlockSpec((ROWS, META), lambda g, at: (0, WIDE // META)),
+                pl.BlockSpec((8, TOK, META), lambda g, at: (0, 0, WIDE // META)),
+            ]
+            + [pl.BlockSpec(p.shape, lambda g, at: (0, 0)) for p in w]
+            + [
+                pl.BlockSpec((1, 64, 512), lambda g, at: (2 * _around(g, at[1]), 0, 0)),
+                pl.BlockSpec((1, 64, 512), lambda g, at: (2 * _around(g, at[1]) + 1, 0, 0)),
+                pl.BlockSpec((1, 64, PIECE), lambda g, at: (at[0], 0, 0)),
             ],
-            out_specs=pl.BlockSpec((ROWS, PIECE + META), lambda g, c: (0, 0)),
+            out_specs=pl.BlockSpec((ROWS, PIECE + META), lambda g, at: (0, 0)),
             scratch_shapes=[pltpu.VMEM((ROWS, PIECE), F32), pltpu.VMEM((ROWS, 64), F32)],
         ),
         out_shape=jax.ShapeDtypeStruct((ROWS, PIECE + META), BF),
         compiler_params=_params(32),
         name="up",
-    )(c, rows, rows, rows, table, w_own, w_other, a_in, a_in, a_out)
+    )(at, rows, rows, table, *w, a_in, a_in, a_out)
 
 
 def _down_kernel(c_ref, h_ref, m_ref, w_own, w_other, o_ref):
@@ -196,6 +209,16 @@
     )(z1, hidden, back)
 
 
+def _shift_x(v, by):
+    return lax.ppermute(v, "x", [(i, (i + by) % 4) for i in range(4)])
+
+
+def _gather_x(w):
+    k = w.shape[0] // 2
+    left, right = _shift_x(w, 1), _shift_x(w, -1)
+    return [w, left, right, _shift_x(left[:k], 1), _shift_x(right[k:], -1)]
+
+
 def _swap(v):
     return lax.ppermute(v, "core", [(0, 1), (1, 0)])
 
@@ -204,10 +227,12 @@
     z1 = lax.axis_index("z1").astype(jnp.int32).reshape(1)
     core = lax.axis_index("core").astype(jnp.int32)
     c = core.reshape(1)
+    at = jnp.stack([core, lax.axis_index("x").astype(jnp.int32)])
     one = lambda w, i: lax.dynamic_index_in_dim(w, i, 0, keepdims=False)
 
-    w_other = _swap(lax.all_gather(one(up_weight, 1 - core), "x", axis=0))
-    w_own = lax.all_gather(one(up_weight, core), "x", axis=0)
+    up_own, up_other = one(up_weight, core), _swap(one(up_weight, 1 - core))
+    first, second = jnp.where(core == 0, up_own, up_other), jnp.where(core == 0, up_other, up_own)
+    w_up = _gather_x(jnp.concatenate([first, second], axis=0))
     down_other = _swap(one(down_weight, 1 - core))
 
     owner = jnp.arange(TEN * RANK, dtype=jnp.int32) // RANK
@@ -219,14 +244,14 @@
     table = lax.all_gather(mine, "z1", axis=0).astype(F32)
     lift = jnp.where(jnp.arange(WIDE + META) < WIDE, 1.0 / LIFT, 1.0)
     table = (table * lift).astype(BF)
-    sending = _select(z1, table)
+    sending = _select(z1, table, w_up[1:3])
     arrived = lax.all_to_all(sending, ("y", "core", "z0"), 0, 0, tiled=True).reshape(ROWS, WIDE + META)
 
     a_in = (adapter_in.transpose(0, 2, 1).astype(F32) * LIFT).astype(F16)
     a_in = lax.all_gather(a_in, ("x", "core"), axis=0)
     a_in = (lax.dynamic_index_in_dim(a_in, core, 1, keepdims=False).astype(F32) / LIFT).astype(BF)
 
-    hidden = _up(c, arrived, table, w_own, w_other, a_in, adapter_out)
+    hidden = _up(at, arrived, table, w_up, a_in, adapter_out)
     hidden = lax.all_gather(hidden.astype(F16), "x", axis=0).astype(BF)
     out = _down(c, hidden, down_weight, down_other)
     back = lax.all_to_all(out, ("y", "core", "z0"), 0, 0, tiled=True)

time: 272 us -> 274 us (level)
  waiting for transfers between devices: 90.4 us -> 63.6 us
  starting transfers between devices: 15.9 us -> 30.1 us
  blocking collectives: 118 us -> 125 us
  other arithmetic: 1.69 us -> 5.18 us
    all_gather x2 -> x0, waiting for transfers between devices: 42.9 us -> none  [the longest x1 36.3 us: per_device(): w_own = lax.all_gather(one(up_weight, core), 'x', axis=0)]
    all_gather x1, blocking collectives: 14.2 us -> 28.9 us  [per_device(): a_in = lax.all_gather(a_in, ('x', 'core'), axis=0)]
    ppermute x0 -> x4, starting transfers between devices: none -> 13.8 us  [_shift_x(): return lax.ppermute(v, 'x', [(i, (i + by) % 4) for i in range(4)])]
    ppermute x0 -> x4, waiting for transfers between devices: none -> 13.6 us  [_shift_x(): return lax.ppermute(v, 'x', [(i, (i + by) % 4) for i in range(4)])]
    all_gather x1, blocking collectives: 38 us -> 30.6 us  [per_device(): table = lax.all_gather(mine, 'z1', axis=0).astype(F32)]
    ppermute x2, starting transfers between devices: 4.61 us -> 11.2 us  [_swap(): return lax.ppermute(v, 'core', [(0, 1), (1, 0)])]
    all_to_all x1, starting transfers between devices: 11.2 us -> 5.03 us  [per_device(): lax.all_to_all(sending, ('y', 'core', 'z0'), 0, 0, tiled=True)]
    slice x0 -> x2, local copies, waits for them, and re-layouts: none -> 4.77 us  [_gather_x(): return [w, left, right, _shift_x(left[:k], 1), _shift_x(right[k:], -1)]]
  transfers between devices with their start and end apart: 6 -> 8, of which waited for: 3 -> 4; matrix products, arithmetic and copies ran while one was open for 2% -> 4% of each run, Pallas kernels for 3% -> 3%
where the time goes in v5:
time: 274 us; the launch traced here: 271 us
  blocking collectives  125 us (46%)
  waiting for transfers between devices  63.6 us (23%)
  starting transfers between devices  30.1 us (11%)
  Pallas kernels  19.1 us (7%)
  local copies, waits for them, and re-layouts  14.5 us (5%)
  between operations  13.6 us (5%)
  other arithmetic  5.18 us (2%)
    reduce_scatter x1, waiting for transfers between devices, per_device(): lax.psum_scatter(partial, 'z1', scatter_dimension=0, tiled=True)  48.7 us
    all_to_all x1, blocking collectives, per_device(): back = lax.all_to_all(out, ('y', 'core', 'z0'), 0, 0, tiled=True)  32.6 us
    all_gather x1, blocking collectives, per_device(): table = lax.all_gather(mine, 'z1', axis=0).astype(F32)  30.6 us
    all_gather x1, blocking collectives, per_device(): a_in = lax.all_gather(a_in, ('x', 'core'), axis=0)  28.9 us
    all_gather x1, blocking collectives, per_device(): hidden = lax.all_gather(hidden.astype(F16), 'x', axis=0).astype(BF)  23.6 us
    ppermute x4, starting transfers between devices, _shift_x(): return lax.ppermute(v, 'x', [(i, (i + by) % 4) for i in range(4)])  13.8 us
    ppermute x4, waiting for transfers between devices, _shift_x(): return lax.ppermute(v, 'x', [(i, (i + by) % 4) for i in range(4)])  13.6 us
    ppermute x2, starting transfers between devices, _swap(): return lax.ppermute(v, 'core', [(0, 1), (1, 0)])  11.2 us
  transfers between devices with their start and end apart: 8, of which 4 were waited for; matrix products, arithmetic and copies ran while one was open for 4% of the time, Pallas kernels for 3%

profile of v5, /device:TPU:1, one launch (start us, length us, event | category | flops | bytes accessed | tf_op | source)
XLA Modules:
  0.0 271.0 jit_solution(13697632244671652560)
XLA Ops:
  6.5 2.4 dynamic-slice_bitcast_fusion.1
  9.0 8.8 %collective-permute-start = (bf16[512,1024]{1,0:T(8,128)(2,1)}, bf16[512,1024]{1,0:T(8,128)(2,1)S(1)}, u32[]{:S(2)}, u32[]{:S(2)}) collective-permute-start(bf16[512,1024]{1,0:T(8,128)(2,1)} %dynamic-slice_bitcast_fusion.1), channel_id=1, source_target_pairs={{0,64},{64,0},{1,65},{65,1},{2,66},{66,2},{3,67},{67,3},{4,68},{68... | collective-permute-start | bytes 3145736 | tf_op jit(solution)/shard_map/ppermute | solution.py:223
  17.8 0.1 copy.15
  17.9 0.1 copy.16
  18.0 0.9 multiply_convert_fusion.2
  18.9 1.3 collective-permute-done
  20.2 0.1 bitcast_select_fusion.1
  20.4 0.0 copy-start.10
  20.4 1.5 pad_maximum_fusion.mid
  21.9 1.9 collective-permute-start.1
  23.8 4.6 %collective-permute-start.2 = (bf16[1024,1024]{1,0:T(8,128)(2,1)}, bf16[1024,1024]{1,0:T(8,128)(2,1)}, u32[]{:S(2)}, u32[]{:S(2)}) collective-permute-start(bf16[1024,1024]{1,0:T(8,128)(2,1)} %pad_maximum_fusion.mid), channel_id=1, source_target_pairs={{0,384},{128,0},{256,128},{384,256},{1,385},{129,1},{257,129},{385... | collective-permute-start | bytes 6291464 | tf_op jit(solution)/shard_map/ppermute | solution.py:213
  28.4 0.1 compare_convert_fusion
  28.5 0.1 concatenate.6
  28.6 30.6 %all-gather.6 = f16[128,4224]{1,0:T(8,128)(2,1)S(1)} all-gather(f16[16,4224]{1,0:T(8,128)(2,1)S(1)} %concatenate.6), channel_id=2, replica_groups=mesh['x'=4,'core'=2,'z1'=8,'z0'=2,'y'=4] {'z1'}, dimensions={0}, use_global_device_ids=true | all-gather | bytes 1216512 | tf_op jit(solution)/shard_map/all_gather | solution.py:244
  59.2 0.2 fusion.m_ref.t_ref
  59.4 12.6 %collective-permute-done.1.rest_0_.left = bf16[1024,1024]{1,0:T(8,128)(2,1)S(1)} collective-permute-done((bf16[1024,1024]{1,0:T(8,128)(2,1)}, bf16[1024,1024]{1,0:T(8,128)(2,1)S(1)}, u32[]{:S(2)}, u32[]{:S(2)}) %collective-permute-start.1) | collective-permute-done | bytes 2097184 | tf_op jit(solution)/shard_map/ppermute | solution.py:213
  72.0 1.0 collective-permute-done.2.rest_1_.right
  73.0 2.7 select.9
  75.7 1.3 copy-done.2
  77.1 5.0 %all-to-all-start = ((bf16[16,16,4224]{2,1,0:T(8,128)(2,1)}), bf16[16,16,4224]{2,1,0:T(8,128)(2,1)S(1)}, u32[]{:S(2)}, u32[]{:S(2)}) async-start(bf16[16,16,4224]{2,1,0:T(8,128)(2,1)} %copy-done.2), calls=%async_computation | async-start | bytes 4325376 | tf_op jit(solution)/shard_map/all_to_all | solution.py:248
  82.1 0.0 reduce-scatter.2.cloned.1.call-start
  82.1 0.0 copy-start.3
  82.1 2.5 slice.8
  84.6 1.9 collective-permute-start.3
  86.5 2.3 slice.9
  88.8 5.4 %collective-permute-start.4 = (bf16[512,1024]{1,0:T(8,128)(2,1)}, bf16[512,1024]{1,0:T(8,128)(2,1)}, u32[]{:S(2)}, u32[]{:S(2)}) collective-permute-start(bf16[512,1024]{1,0:T(8,128)(2,1)} %slice.9), channel_id=1, source_target_pairs={{0,384},{128,0},{256,128},{384,256},{1,385},{129,1},{257,129},{385... | collective-permute-start | bytes 3145736 | tf_op jit(solution)/shard_map/ppermute | solution.py:213
  94.3 1.1 dynamic-slice_bitcast_fusion
  95.4 2.4 collective-permute-start.5
  97.8 0.9 fusion.2
  98.7 28.9 %all-gather.7 = f16[16,64,512]{2,1,0:T(8,128)(2,1)S(1)} all-gather(f16[2,64,512]{2,1,0:T(8,128)(2,1)S(1)} %fusion.2), channel_id=3, replica_groups=mesh['x'=4,'core'=2,'z1'=8,'z0'=2,'y'=4] {'x','core'}, dimensions={0}, use_global_device_ids=true | all-gather | bytes 1179648 | tf_op jit(solution)/shard_map/all_gather | solution.py:251
  127.6 0.1 pad_add_fusion.at
  127.7 0.9 fusion.1.a_low.a_high
  128.6 0.0 collective-permute-done.4.far_high
  128.6 0.0 all-to-all-done
  128.6 1.6 copy-done.1
  130.2 1.0 copy-done.5
  131.2 8.4 %up.1 = bf16[256,1152]{1,0:T(8,128)(2,1)S(1)} custom-call(s32[2]{0:T(128)S(1)} %pad_add_fusion.at, bf16[256,4224]{1,0:T(8,128)(2,1)S(1)} %bitcast.28, bf16[256,4224]{1,0:T(8,128)(2,1)S(1)} %bitcast.29, bf16[8,16,4224]{2,1,0:T(8,128)(2,1)S(1)} %fusion.m_ref.t_ref, bf16[1024,1024]{1,0:T(8,128)(2,1)} %pad_maximum_fusion.mid, bf16[1024,1024]{1,0:T(8,128)(2,1)S(1)} %copy-done.1, ...), custom_call_target="tpu_custom_call" | custom-call | tf_op jit(solution)/shard_map/up/pallas_call | solution.py:131
  139.7 0.1 convert_element_type.59
  139.8 23.6 %all-gather.8 = f16[1024,1152]{1,0:T(8,128)(2,1)S(1)} all-gather(f16[256,1152]{1,0:T(8,128)(2,1)S(1)} %convert_element_type.59), channel_id=4, replica_groups=mesh['x'=4,'core'=2,'z1'=8,'z0'=2,'y'=4] {'x'}, dimensions={0}, use_global_device_ids=true | all-gather | bytes 2949120 | tf_op jit(solution)/shard_map/all_gather | solution.py:255
  163.4 0.3 convert_element_type.62
  163.8 1.2 copy-done.4
  165.0 4.4 %down.1 = bf16[16,4,16,1024]{3,2,1,0:T(8,128)(2,1)S(1)} custom-call(s32[1]{0:T(128)} %bitcast.1.c_ref, bf16[4,256,1152]{2,1,0:T(8,128)(2,1)S(1)} %bitcast.25, bf16[4,256,1152]{2,1,0:T(8,128)(2,1)S(1)} %bitcast.26, bf16[2,1024,512]{2,1,0:T(8,128)(2,1)S(1)} %copy-done.4, bf16[1024,512]{1,0:T(8,128)(2,1)} %collective-permute-done.5.w_other), custom_call_target="tpu_custom_call" | custom-call | tf_op jit(solution)/shard_map/down/pallas_call | solution.py:165
  169.4 32.6 %all_to_all.15.y_ref = bf16[16,4,16,1024]{3,2,1,0:T(8,128)(2,1)S(1)} all-to-all(bf16[16,4,16,1024]{3,2,1,0:T(8,128)(2,1)S(1)} %down.1), channel_id=1, replica_groups=mesh['x'=4,'core'=2,'z1'=8,'z0'=2,'y'=4] {'y','core','z0'}, dimensions={0} | all-to-all | bytes 4194304 | tf_op jit(solution)/shard_map/all_to_all | solution.py:257
  202.0 3.6 %combine.1 = bf16[8,4,16,1024]{3,2,1,0:T(8,128)(2,1)} custom-call(s32[1]{0:T(128)} %bitcast.z_ref, bf16[4,256,1152]{2,1,0:T(8,128)(2,1)S(1)} %bitcast.27, bf16[16,4,16,1024]{3,2,1,0:T(8,128)(2,1)S(1)} %all_to_all.15.y_ref), custom_call_target="tpu_custom_call" | custom-call | tf_op jit(solution)/shard_map/combine/pallas_call | solution.py:195
  205.6 0.0 reduce-scatter.2.cloned.1.call-update
  205.6 48.7 %reduce-scatter.2.cloned.1.call-done = bf16[1,4,16,1024]{3,2,1,0:T(8,128)(2,1)} async-done(((bf16[8,4,16,1024]{3,2,1,0:T(8,128)(2,1)}), bf16[1,4,16,1024]{3,2,1,0:T(8,128)(2,1)}) %reduce-scatter.2.cloned.1.call-update) | async-done | bytes 131088 | tf_op jit(solution)/shard_map/reduce_scatter | solution.py:259
  254.3 9.2 %all_to_all.16 = bf16[4,16,1024]{2,1,0:T(8,128)(2,1)S(1)} all-to-all(bf16[4,16,1024]{2,1,0:T(8,128)(2,1)} %bitcast.33), channel_id=1, replica_groups=mesh['x'=4,'core'=2,'z1'=8,'z0'=2,'y'=4] {'x'}, dimensions={0} | all-to-all | bytes 262144 | tf_op jit(solution)/shard_map/all_to_all | solution.py:260
  263.5 0.7 copy.20
  (23 shorter events, 0.1 us)
Async XLA Ops:
  6.5 13.7 %copy-start.7 = (bf16[2,512,1024]{2,1,0:T(8,128)(2,1)S(1)}, bf16[2,512,1024]{2,1,0:T(8,128)(2,1)}, u32[]{:S(2)}) copy-start(bf16[2,512,1024]{2,1,0:T(8,128)(2,1)} %param.12) | copy-start | bytes 6291460
  6.5 11.2 %copy-start.8 = (s32[16,8]{0,1:T(8,128)S(1)}, s32[16,8]{0,1:T(8,128)}, u32[]{:S(2)}) copy-start(s32[16,8]{0,1:T(8,128)} %param.9) | copy-start | bytes 1540
  6.5 11.3 %copy-start.9 = (f32[16,8]{0,1:T(8,128)S(1)}, f32[16,8]{0,1:T(8,128)}, u32[]{:S(2)}) copy-start(f32[16,8]{0,1:T(8,128)} %param.10) | copy-start | bytes 1540
  9.0 11.3 %collective-permute-start = (bf16[512,1024]{1,0:T(8,128)(2,1)}, bf16[512,1024]{1,0:T(8,128)(2,1)S(1)}, u32[]{:S(2)}, u32[]{:S(2)}) collective-permute-start(bf16[512,1024]{1,0:T(8,128)(2,1)} %dynamic-slice_bitcast_fusion.1), channel_id=1, source_target_pairs={{0,64},{64,0},{1,65},{65,1},{2,66},{66,2},{3,67},{67,3},{4,68},{68... | collective-permute-start | bytes 3145736 | tf_op jit(solution)/shard_map/ppermute | solution.py:223
  20.4 8.0 %copy-start.10 = (s32[16]{0:T(128)S(1)}, s32[16]{0:T(128)}, u32[]{:S(2)}) copy-start(s32[16]{0:T(128)} %param.11) | copy-start | bytes 196
  21.9 50.1 %collective-permute-start.1 = (bf16[1024,1024]{1,0:T(8,128)(2,1)}, bf16[1024,1024]{1,0:T(8,128)(2,1)S(1)}, u32[]{:S(2)}, u32[]{:S(2)}) collective-permute-start(bf16[1024,1024]{1,0:T(8,128)(2,1)} %pad_maximum_fusion.mid), channel_id=1, source_target_pairs={{0,128},{128,256},{256,384},{384,0},{1,129},{129,257},{257,385},{3... | collective-permute-start | bytes 6291464 | tf_op jit(solution)/shard_map/ppermute | solution.py:213
  23.8 49.2 %collective-permute-start.2 = (bf16[1024,1024]{1,0:T(8,128)(2,1)}, bf16[1024,1024]{1,0:T(8,128)(2,1)}, u32[]{:S(2)}, u32[]{:S(2)}) collective-permute-start(bf16[1024,1024]{1,0:T(8,128)(2,1)} %pad_maximum_fusion.mid), channel_id=1, source_target_pairs={{0,384},{128,0},{256,128},{384,256},{1,385},{129,1},{257,129},{385... | collective-permute-start | bytes 6291464 | tf_op jit(solution)/shard_map/ppermute | solution.py:213
  72.0 3.7 %copy-start = (bf16[1024,1024]{1,0:T(8,128)(2,1)}, bf16[1024,1024]{1,0:T(8,128)(2,1)S(1)}, u32[]{:S(2)}) copy-start(bf16[1024,1024]{1,0:T(8,128)(2,1)S(1)} %collective-permute-done.1.rest_0_.left) | copy-start | bytes 6291460
  75.7 1.4 copy-start.2
  77.1 51.5 %all-to-all-start = ((bf16[16,16,4224]{2,1,0:T(8,128)(2,1)}), bf16[16,16,4224]{2,1,0:T(8,128)(2,1)S(1)}, u32[]{:S(2)}, u32[]{:S(2)}) async-start(bf16[16,16,4224]{2,1,0:T(8,128)(2,1)} %copy-done.2), calls=%async_computation | async-start | bytes 4325376 | tf_op jit(solution)/shard_map/all_to_all | solution.py:248
  82.1 172.2 %reduce-scatter.2.cloned.1.call-start = ((), (), s32[]{:S(2)}) async-start(), calls=%async_computation.4 | async-start | bytes 1179648 | tf_op jit(solution)/shard_map/reduce_scatter | solution.py:259
  82.1 12.2 %copy-start.3 = (bf16[2,1024,512]{2,1,0:T(8,128)(2,1)S(1)}, bf16[2,1024,512]{2,1,0:T(8,128)(2,1)}, u32[]{:S(2)}) copy-start(bf16[2,1024,512]{2,1,0:T(8,128)(2,1)} %w_own.1) | copy-start | bytes 6291460
  84.6 43.9 %collective-permute-start.3 = (bf16[512,1024]{1,0:T(8,128)(2,1)}, bf16[512,1024]{1,0:T(8,128)(2,1)}, u32[]{:S(2)}, u32[]{:S(2)}) collective-permute-start(bf16[512,1024]{1,0:T(8,128)(2,1)} %slice.8), channel_id=1, source_target_pairs={{0,128},{128,256},{256,384},{384,0},{1,129},{129,257},{257,385},{3... | collective-permute-start | bytes 3145736 | tf_op jit(solution)/shard_map/ppermute | solution.py:213
  88.8 39.7 %copy-start.6 = (bf16[2,64,1024]{2,1,0:T(8,128)(2,1)S(1)}, bf16[2,64,1024]{2,1,0:T(8,128)(2,1)}, u32[]{:S(2)}) copy-start(bf16[2,64,1024]{2,1,0:T(8,128)(2,1)} %a_out.1) | copy-start | bytes 786436
  88.8 39.7 %collective-permute-start.4 = (bf16[512,1024]{1,0:T(8,128)(2,1)}, bf16[512,1024]{1,0:T(8,128)(2,1)}, u32[]{:S(2)}, u32[]{:S(2)}) collective-permute-start(bf16[512,1024]{1,0:T(8,128)(2,1)} %slice.9), channel_id=1, source_target_pairs={{0,384},{128,0},{256,128},{384,256},{1,385},{129,1},{257,129},{385... | collective-permute-start | bytes 3145736 | tf_op jit(solution)/shard_map/ppermute | solution.py:213
  95.4 68.4 %collective-permute-start.5 = (bf16[1024,512]{1,0:T(8,128)(2,1)}, bf16[1024,512]{1,0:T(8,128)(2,1)}, u32[]{:S(2)}, u32[]{:S(2)}) collective-permute-start(bf16[1024,512]{1,0:T(8,128)(2,1)} %dynamic-slice_bitcast_fusion), channel_id=1, source_target_pairs={{0,64},{64,0},{1,65},{65,1},{2,66},{66,2},{3,67},{67,3},{4,68},{68... | collective-permute-start | bytes 3145736 | tf_op jit(solution)/shard_map/ppermute | solution.py:223
  128.6 1.6 copy-start.1
  130.2 1.0 copy-start.5
  163.4 1.6 copy-start.4
Sparse Core Ops, SparseCore 0:
  205.8 48.4 reduce-scatter.1

commit v6 on v5

--- a/solution.py
+++ b/solution.py
@@ -20,7 +20,6 @@
 GATE_AT = 72
 ROWS = 256
 TOKS = 128
-SCALE_AT = 96
 LIFT = 4096.0
 def _params(mib):
     return pltpu.CompilerParams(vmem_limit_bytes=mib << 20)
@@ -84,7 +83,7 @@
     return lax.rem(x + jnp.where(g == 0, 0, jnp.where(g == 1, 3, jnp.where(g == 2, 1, 2))), 4)
 
 
-def _up_kernel(at, x_ref, m_ref, t_ref, mid, left, right, far_low, far_high, a_low, a_high, a_out, o_ref, acc, shrink):
+def _up_kernel(at, x_ref, m_ref, mid, left, right, far_low, far_high, a_low, a_high, a_out, o_ref, acc, shrink):
     g = pl.program_id(0)
     lanes = (((1,), (1,)), ((), ()))
 
@@ -107,8 +106,8 @@
         far += jnp.dot(x_ref[:, 512:], far_high[...], preferred_element_type=F32)
         acc[...] += far
 
-    less = lax.dot_general(x_ref[:, :512], a_low[0], lanes, preferred_element_type=F32)
-    less += lax.dot_general(x_ref[:, 512:], a_high[0], lanes, preferred_element_type=F32)
+    less = lax.dot_general(x_ref[:, :512], a_low[0, 0], lanes, preferred_element_type=F32)
+    less += lax.dot_general(x_ref[:, 512:], a_high[0, 0], lanes, preferred_element_type=F32)
     shrink[...] += less
 
     @pl.when(g == 3)
@@ -122,12 +121,10 @@
         peak = jnp.max(jnp.abs(hidden), axis=1, keepdims=True)
         power = jnp.floor(jnp.log2(jnp.maximum(peak, 1e-30)))
         o_ref[:, :PIECE] = (hidden * jnp.exp2(-power)).astype(BF)
-        lane = lax.broadcasted_iota(jnp.int32, (ROWS, META), 1)
-        meta = jnp.concatenate([t_ref[...].reshape(TOKS, META), jnp.zeros((ROWS - TOKS, META), BF)], axis=0)
-        o_ref[:, PIECE:] = jnp.where(lane == SCALE_AT, power, meta.astype(F32)).astype(BF)
-
-
-def _up(at, rows, table, w, a_in, a_out):
+        o_ref[:, PIECE:] = jnp.broadcast_to(power, (ROWS, META)).astype(BF)
+
+
+def _up(at, rows, w, a_in, a_out):
     return pl.pallas_call(
         _up_kernel,
         grid_spec=pltpu.PrefetchScalarGridSpec(
@@ -136,12 +133,11 @@
             in_specs=[
                 pl.BlockSpec((ROWS, PIECE), lambda g, at: (0, _around(g, at[1]))),
                 pl.BlockSpec((ROWS, META), lambda g, at: (0, WIDE // META)),
-                pl.BlockSpec((8, TOK, META), lambda g, at: (0, 0, WIDE // META)),
             ]
             + [pl.BlockSpec(p.shape, lambda g, at: (0, 0)) for p in w]
             + [
-                pl.BlockSpec((1, 64, 512), lambda g, at: (2 * _around(g, at[1]), 0, 0)),
-                pl.BlockSpec((1, 64, 512), lambda g, at: (2 * _around(g, at[1]) + 1, 0, 0)),
+                pl.BlockSpec((1, 1, 64, 512), lambda g, at: (2 * _around(g, at[1]), at[0], 0, 0)),
+                pl.BlockSpec((1, 1, 64, 512), lambda g, at: (2 * _around(g, at[1]) + 1, at[0], 0, 0)),
                 pl.BlockSpec((1, 64, PIECE), lambda g, at: (at[0], 0, 0)),
             ],
             out_specs=pl.BlockSpec((ROWS, PIECE + META), lambda g, at: (0, 0)),
@@ -150,15 +146,15 @@
         out_shape=jax.ShapeDtypeStruct((ROWS, PIECE + META), BF),
         compiler_params=_params(32),
         name="up",
-    )(at, rows, rows, table, *w, a_in, a_in, a_out)
+    )(at, rows, rows, *w, a_in, a_in, a_out)
 
 
 def _down_kernel(c_ref, h_ref, m_ref, w_own, w_other, o_ref):
-    scale = jnp.exp2(m_ref[0, :, SCALE_AT : SCALE_AT + 1].astype(F32))
+    scale = jnp.exp2(m_ref[0, :, :1].astype(F32))
     for side, w in ((c_ref[0], w_own[0]), (1 - c_ref[0], w_other[...])):
         cols = pl.ds(pl.multiple_of(side * 512, 512), 512)
         out = jnp.dot(h_ref[0], w, preferred_element_type=F32) * scale
-        o_ref[:, :, :, cols] = out.astype(BF).reshape(DEST, 1, 16, 512)
+        o_ref[:, :, :, cols] = out.astype(BF).reshape(1, DEST, 16, 512)
 
 
 def _down(c, hidden, w, w_other):
@@ -173,40 +169,44 @@
                 pl.BlockSpec((1, PIECE, 512), lambda g, c: (c[0], 0, 0)),
                 pl.BlockSpec((PIECE, 512), lambda g, c: (0, 0)),
             ],
-            out_specs=pl.BlockSpec((DEST, 1, 16, PIECE), lambda g, c: (0, g, 0, 0)),
-        ),
-        out_shape=jax.ShapeDtypeStruct((DEST, 4, 16, PIECE), BF),
+            out_specs=pl.BlockSpec((1, DEST, 16, PIECE), lambda g, c: (g, 0, 0, 0)),
+        ),
+        out_shape=jax.ShapeDtypeStruct((4, DEST, 16, PIECE), BF),
         compiler_params=_params(24),
         name="down",
     )(c, hidden, hidden, w, w_other)
 
 
-def _combine_kernel(z_ref, m_ref, y_ref, o_ref):
-    meta = m_ref[0].astype(F32)
-    matches = _matches(meta, z_ref[0])
-    gate = sum(jnp.where(m, meta[:, GATE_AT + k : GATE_AT + k + 1], 0.0) for k, m in enumerate(matches))
-    gates = jnp.dot(gate.astype(BF), _spread(), preferred_element_type=F32)
-    weight = jnp.where(_slots(matches), gates, 0.0).astype(BF)
-    out = jnp.dot(weight, y_ref[...].reshape(ROWS, PIECE), preferred_element_type=F32)
-    o_ref[...] = out.astype(BF).reshape(8, 1, TOK, PIECE)
-
-
-def _combine(z1, hidden, back):
+def _combine_kernel(z_ref, m_ref, y_ref, o_ref, weight):
+    @pl.when(pl.program_id(0) == 0)
+    def _():
+        meta = m_ref[...].reshape(TOKS, META).astype(F32)
+        matches = _matches(meta, z_ref[0])
+        gate = sum(jnp.where(m, meta[:, GATE_AT + k : GATE_AT + k + 1], 0.0) for k, m in enumerate(matches))
+        gates = jnp.dot(gate.astype(BF), _spread(), preferred_element_type=F32)
+        weight[...] = jnp.where(_slots(matches), gates, 0.0).astype(BF)
+
+    out = jnp.dot(weight[...], y_ref[...].reshape(ROWS, PIECE), preferred_element_type=F32)
+    o_ref[...] = out.astype(BF)
+
+
+def _combine(z1, table, back):
     return pl.pallas_call(
         _combine_kernel,
         grid_spec=pltpu.PrefetchScalarGridSpec(
             num_scalar_prefetch=1,
             grid=(4,),
             in_specs=[
-                pl.BlockSpec((1, TOKS, META), lambda g, z: (g, 0, PIECE // META)),
-                pl.BlockSpec((DEST, 1, 16, PIECE), lambda g, z: (0, g, 0, 0)),
+                pl.BlockSpec((8, TOK, META), lambda g, z: (0, 0, WIDE // META)),
+                pl.BlockSpec((1, DEST, 16, PIECE), lambda g, z: (g, 0, 0, 0)),
             ],
-            out_specs=pl.BlockSpec((8, 1, TOK, PIECE), lambda g, z: (0, g, 0, 0)),
-        ),
-        out_shape=jax.ShapeDtypeStruct((8, 4, TOK, PIECE), BF),
+            out_specs=pl.BlockSpec((TOKS, PIECE), lambda g, z: (0, g)),
+            scratch_shapes=[pltpu.VMEM((TOKS, ROWS), BF)],
+        ),
+        out_shape=jax.ShapeDtypeStruct((TOKS, WIDE), BF),
         compiler_params=_params(24),
         name="combine",
-    )(z1, hidden, back)
+    )(z1, table, back)
 
 
 def _shift_x(v, by):
@@ -233,6 +233,7 @@
     up_own, up_other = one(up_weight, core), _swap(one(up_weight, 1 - core))
     first, second = jnp.where(core == 0, up_own, up_other), jnp.where(core == 0, up_other, up_own)
     w_up = _gather_x(jnp.concatenate([first, second], axis=0))
+    a_in = lax.all_gather(adapter_in.transpose(0, 2, 1), ("x", "core"), axis=0)
     down_other = _swap(one(down_weight, 1 - core))
 
     owner = jnp.arange(TEN * RANK, dtype=jnp.int32) // RANK
@@ -244,21 +245,15 @@
     table = lax.all_gather(mine, "z1", axis=0).astype(F32)
     lift = jnp.where(jnp.arange(WIDE + META) < WIDE, 1.0 / LIFT, 1.0)
     table = (table * lift).astype(BF)
-    sending = _select(z1, table, w_up[1:3])
+    sending = _select(z1, table, w_up[1:3] + [a_in])
     arrived = lax.all_to_all(sending, ("y", "core", "z0"), 0, 0, tiled=True).reshape(ROWS, WIDE + META)
 
-    a_in = (adapter_in.transpose(0, 2, 1).astype(F32) * LIFT).astype(F16)
-    a_in = lax.all_gather(a_in, ("x", "core"), axis=0)
-    a_in = (lax.dynamic_index_in_dim(a_in, core, 1, keepdims=False).astype(F32) / LIFT).astype(BF)
-
-    hidden = _up(at, arrived, table, w_up, a_in, adapter_out)
+    hidden = _up(at, arrived, w_up, a_in, adapter_out)
     hidden = lax.all_gather(hidden.astype(F16), "x", axis=0).astype(BF)
     out = _down(c, hidden, down_weight, down_other)
-    back = lax.all_to_all(out, ("y", "core", "z0"), 0, 0, tiled=True)
-    partial = _combine(z1, hidden, back)
-    mixed = lax.psum_scatter(partial, "z1", scatter_dimension=0, tiled=True).reshape(4, TOK, PIECE)
-    home = lax.all_to_all(mixed, "x", 0, 0, tiled=True)
-    return home.transpose(1, 0, 2).reshape(TOK, WIDE)
+    back = lax.all_to_all(out.reshape(64, 16, PIECE), ("x", "y", "core", "z0"), 0, 0, tiled=True)
+    partial = _combine(z1, table, back.reshape(4, DEST, 16, PIECE))
+    return lax.psum_scatter(partial, "z1", scatter_dimension=0, tiled=True)
 
 
 def solution(mesh):

time: 274 us -> 260 us (0.949)
  blocking collectives: 125 us -> 91.2 us
  waiting for transfers between devices: 63.6 us -> 87 us
    all_gather x1 -> x0, blocking collectives: 28.9 us -> none  [per_device(): a_in = lax.all_gather(a_in, ('x', 'core'), axis=0)]
    ppermute x4, waiting for transfers between devices: 13.6 us -> 36.8 us  [_shift_x(): return lax.ppermute(v, 'x', [(i, (i + by) % 4) for i in range(4)])]
    all_to_all x2 -> x1, blocking collectives: 41.8 us -> 38.3 us  [per_device(): lax.all_to_all(out.reshape(64, 16, PIECE), ('x', 'y', 'core', 'z0'), 0, 0...]
    unnamed x22 -> x26, local copies, waits for them, and re-layouts: 5.24 us -> 6.66 us
  transfers between devices with their start and end apart: 8 -> 9, of which waited for: 4 -> 6; matrix products, arithmetic and copies ran while one was open for 4% -> 3% of each run, Pallas kernels for 3% -> 3%
where the time goes in v6:
time: 260 us; the launch traced here: 258 us
  blocking collectives  91.2 us (35%)
  waiting for transfers between devices  87 us (33%)
  starting transfers between devices  30.1 us (12%)
  Pallas kernels  18 us (7%)
  local copies, waits for them, and re-layouts  15.2 us (6%)
  between operations  13.6 us (5%)
    reduce_scatter x1, waiting for transfers between devices, per_device(): return lax.psum_scatter(partial, 'z1', scatter_dimension=0, tiled=True)  47.7 us
    all_to_all x1, blocking collectives, per_device(): lax.all_to_all(out.reshape(64, 16, PIECE), ('x', 'y', 'core', 'z0'), 0, 0...  38.3 us
    ppermute x4, waiting for transfers between devices, _shift_x(): return lax.ppermute(v, 'x', [(i, (i + by) % 4) for i in range(4)])  36.8 us
    all_gather x1, blocking collectives, per_device(): table = lax.all_gather(mine, 'z1', axis=0).astype(F32)  30.4 us
    all_gather x1, blocking collectives, per_device(): hidden = lax.all_gather(hidden.astype(F16), 'x', axis=0).astype(BF)  22.5 us
    ppermute x4, starting transfers between devices, _shift_x(): return lax.ppermute(v, 'x', [(i, (i + by) % 4) for i in range(4)])  13.8 us
    ppermute x2, starting transfers between devices, _swap(): return lax.ppermute(v, 'core', [(0, 1), (1, 0)])  11.2 us
    pallas_call x1, Pallas kernels, _up(): pl.pallas_call(_up_kernel, grid_spec=pltpu.PrefetchScalarGridSpec(num_sca...  8.41 us
  transfers between devices with their start and end apart: 9, of which 6 were waited for; matrix products, arithmetic and copies ran while one was open for 3% of the time, Pallas kernels for 3%

profile of v6, /device:TPU:1, one launch (start us, length us, event | category | flops | bytes accessed | tf_op | source)
XLA Modules:
  0.0 257.6 jit_solution(16977852150894064634)
XLA Ops:
  6.5 2.5 dynamic-slice_bitcast_fusion.1
  9.0 8.8 %collective-permute-start = (bf16[512,1024]{1,0:T(8,128)(2,1)}, bf16[512,1024]{1,0:T(8,128)(2,1)S(1)}, u32[]{:S(2)}, u32[]{:S(2)}) collective-permute-start(bf16[512,1024]{1,0:T(8,128)(2,1)} %dynamic-slice_bitcast_fusion.1), channel_id=1, source_target_pairs={{0,64},{64,0},{1,65},{65,1},{2,66},{66,2},{3,67},{67,3},{4,68},{68... | collective-permute-start | bytes 3145736 | tf_op jit(solution)/shard_map/ppermute | solution.py:223
  17.8 0.0 all-gather.7.cloned.1.call-update
  17.9 2.4 collective-permute-done
  20.3 0.1 bitcast_select_fusion.1
  20.4 0.0 copy-start.12
  20.4 0.0 copy-start.10
  20.4 0.0 copy-start.11
  20.4 1.5 pad_maximum_fusion.mid
  21.9 1.9 collective-permute-start.1
  23.8 4.6 %collective-permute-start.2 = (bf16[1024,1024]{1,0:T(8,128)(2,1)}, bf16[1024,1024]{1,0:T(8,128)(2,1)}, u32[]{:S(2)}, u32[]{:S(2)}) collective-permute-start(bf16[1024,1024]{1,0:T(8,128)(2,1)} %pad_maximum_fusion.mid), channel_id=1, source_target_pairs={{0,384},{128,0},{256,128},{384,256},{1,385},{129,1},{257,129},{385... | collective-permute-start | bytes 6291464 | tf_op jit(solution)/shard_map/ppermute | solution.py:213
  28.4 0.1 compare_convert_fusion
  28.5 0.1 copy.11
  28.6 0.1 copy.12
  28.7 0.1 concatenate.6
  28.8 30.4 %all-gather.8 = f16[128,4224]{1,0:T(8,128)(2,1)S(1)} all-gather(f16[16,4224]{1,0:T(8,128)(2,1)S(1)} %concatenate.6), channel_id=2, replica_groups=mesh['x'=4,'core'=2,'z1'=8,'z0'=2,'y'=4] {'z1'}, dimensions={0}, use_global_device_ids=true | all-gather | bytes 1216512 | tf_op jit(solution)/shard_map/all_gather | solution.py:245
  59.3 0.2 fusion.m_ref.t_ref
  59.4 0.0 all-gather.7.cloned.1.call-done
  59.5 16.8 %collective-permute-done.1.rest_0_.left = bf16[1024,1024]{1,0:T(8,128)(2,1)S(1)} collective-permute-done((bf16[1024,1024]{1,0:T(8,128)(2,1)}, bf16[1024,1024]{1,0:T(8,128)(2,1)S(1)}, u32[]{:S(2)}, u32[]{:S(2)}) %collective-permute-start.1) | collective-permute-done | bytes 2097184 | tf_op jit(solution)/shard_map/ppermute | solution.py:213
  76.3 1.0 collective-permute-done.2.rest_1_.right
  77.2 1.2 copy-done.2
  78.5 2.7 %select.9 = bf16[16,16,4224]{2,1,0:T(8,128)(2,1)S(1)} custom-call(s32[1]{0:T(128)} %bitcast.z_ref, bf16[8,16,4224]{2,1,0:T(8,128)(2,1)S(1)} %fusion.m_ref.t_ref, bf16[8,16,4224]{2,1,0:T(8,128)(2,1)S(1)} %fusion.m_ref.t_ref, bf16[1024,1024]{1,0:T(8,128)(2,1)S(1)} %collective-permute-done.1.rest_0_.left, ...), custom_call_target="tpu_custom_call" | custom-call | tf_op jit(solution)/shard_map/select/pallas_call | solution.py:64
  81.2 1.3 copy-done.4
  82.5 5.0 %all-to-all-start = ((bf16[16,16,4224]{2,1,0:T(8,128)(2,1)}), bf16[16,16,4224]{2,1,0:T(8,128)(2,1)S(1)}, u32[]{:S(2)}, u32[]{:S(2)}) async-start(bf16[16,16,4224]{2,1,0:T(8,128)(2,1)} %copy-done.4), calls=%async_computation | async-start | bytes 4325376 | tf_op jit(solution)/shard_map/all_to_all | solution.py:249
  87.6 0.0 reduce-scatter.2.cloned.1.call-start
  87.6 0.0 copy-start.5
  87.6 2.4 slice.8
  90.0 2.0 collective-permute-start.3
  92.1 2.3 slice.9
  94.4 5.3 %collective-permute-start.4 = (bf16[512,1024]{1,0:T(8,128)(2,1)}, bf16[512,1024]{1,0:T(8,128)(2,1)}, u32[]{:S(2)}, u32[]{:S(2)}) collective-permute-start(bf16[512,1024]{1,0:T(8,128)(2,1)} %slice.9), channel_id=1, source_target_pairs={{0,384},{128,0},{256,128},{384,256},{1,385},{129,1},{257,129},{385... | collective-permute-start | bytes 3145736 | tf_op jit(solution)/shard_map/ppermute | solution.py:213
  99.7 1.1 dynamic-slice_bitcast_fusion
  100.8 2.4 collective-permute-start.5
  103.2 0.1 pad_add_fusion.at
  103.3 15.9 %collective-permute-done.3.far_low = bf16[512,1024]{1,0:T(8,128)(2,1)} collective-permute-done((bf16[512,1024]{1,0:T(8,128)(2,1)}, bf16[512,1024]{1,0:T(8,128)(2,1)}, u32[]{:S(2)}, u32[]{:S(2)}) %collective-permute-start.3) | collective-permute-done | bytes 1048608 | tf_op jit(solution)/shard_map/ppermute | solution.py:213
  119.2 3.1 %collective-permute-done.4.far_high = bf16[512,1024]{1,0:T(8,128)(2,1)} collective-permute-done((bf16[512,1024]{1,0:T(8,128)(2,1)}, bf16[512,1024]{1,0:T(8,128)(2,1)}, u32[]{:S(2)}, u32[]{:S(2)}) %collective-permute-start.4) | collective-permute-done | bytes 1048608 | tf_op jit(solution)/shard_map/ppermute | solution.py:213
  122.3 0.0 all-to-all-done
  122.4 1.6 copy-done.1
  124.0 1.2 copy-done.3
  125.2 8.4 %up.1 = bf16[256,1152]{1,0:T(8,128)(2,1)S(1)} custom-call(s32[2]{0:T(128)S(1)} %pad_add_fusion.at, bf16[256,4224]{1,0:T(8,128)(2,1)S(1)} %bitcast.20, bf16[256,4224]{1,0:T(8,128)(2,1)S(1)} %bitcast.21, bf16[1024,1024]{1,0:T(8,128)(2,1)} %pad_maximum_fusion.mid, bf16[1024,1024]{1,0:T(8,128)(2,1)S(1)} %copy-done.1, ...), custom_call_target="tpu_custom_call" | custom-call | tf_op jit(solution)/shard_map/up/pallas_call | solution.py:128
  133.6 0.1 convert_element_type.34
  133.7 22.5 %all-gather.9 = f16[1024,1152]{1,0:T(8,128)(2,1)S(1)} all-gather(f16[256,1152]{1,0:T(8,128)(2,1)S(1)} %convert_element_type.34), channel_id=4, replica_groups=mesh['x'=4,'core'=2,'z1'=8,'z0'=2,'y'=4] {'x'}, dimensions={0}, use_global_device_ids=true | all-gather | bytes 2949120 | tf_op jit(solution)/shard_map/all_gather | solution.py:252
  156.2 0.3 convert_element_type.37
  156.6 1.2 copy-done.6
  157.8 4.3 %down.1 = bf16[4,16,16,1024]{3,2,1,0:T(8,128)(2,1)S(1)} custom-call(s32[1]{0:T(128)} %bitcast.2.c_ref, bf16[4,256,1152]{2,1,0:T(8,128)(2,1)S(1)} %bitcast.18, bf16[4,256,1152]{2,1,0:T(8,128)(2,1)S(1)} %bitcast.19, bf16[2,1024,512]{2,1,0:T(8,128)(2,1)S(1)} %copy-done.6, bf16[1024,512]{1,0:T(8,128)(2,1)} %collective-permute-done.5.w_other), custom_call_target="tpu_custom_call" | custom-call | tf_op jit(solution)/shard_map/down/pallas_call | solution.py:161
  162.1 38.3 %all_to_all.10 = bf16[64,16,1024]{2,1,0:T(8,128)(2,1)S(1)} all-to-all(bf16[64,16,1024]{2,1,0:T(8,128)(2,1)S(1)} %bitcast.25), channel_id=1, replica_groups=mesh['x'=4,'core'=2,'z1'=8,'z0'=2,'y'=4] {'x','y','core','z0'}, dimensions={0} | all-to-all | bytes 4194304 | tf_op jit(solution)/shard_map/all_to_all | solution.py:254
  200.4 2.6 %combine.1 = bf16[128,4096]{1,0:T(8,128)(2,1)} custom-call(s32[1]{0:T(128)} %bitcast.z_ref, bf16[8,16,4224]{2,1,0:T(8,128)(2,1)S(1)} %fusion.m_ref.t_ref, bf16[4,16,16,1024]{3,2,1,0:T(8,128)(2,1)S(1)} %bitcast.26), custom_call_target="tpu_custom_call" | custom-call | tf_op jit(solution)/shard_map/combine/pallas_call | solution.py:194
  203.0 0.0 reduce-scatter.2.cloned.1.call-update
  203.0 47.7 %reduce-scatter.2.cloned.1.call-done = bf16[16,4096]{1,0:T(8,128)(2,1)} async-done(((bf16[128,4096]{1,0:T(8,128)(2,1)}), bf16[16,4096]{1,0:T(8,128)(2,1)}) %reduce-scatter.2.cloned.1.call-update) | async-done | bytes 131088 | tf_op jit(solution)/shard_map/reduce_scatter | solution.py:256
  (25 shorter events, 0.1 us)
Async XLA Ops:
  6.5 13.7 %copy-start.8 = (bf16[2,512,1024]{2,1,0:T(8,128)(2,1)S(1)}, bf16[2,512,1024]{2,1,0:T(8,128)(2,1)}, u32[]{:S(2)}) copy-start(bf16[2,512,1024]{2,1,0:T(8,128)(2,1)} %param.12) | copy-start | bytes 6291460
  6.5 11.3 %copy-start.9 = (bf16[16,4096]{1,0:T(8,128)(2,1)S(1)}, bf16[16,4096]{1,0:T(8,128)(2,1)}, u32[]{:S(2)}) copy-start(bf16[16,4096]{1,0:T(8,128)(2,1)} %param.8) | copy-start | bytes 393220
  6.5 52.9 %all-gather.7.cloned.1.call-start = ((), (), s32[]{:S(2)}) async-start(), calls=%async_computation.4 | async-start | bytes 1179648 | tf_op jit(solution)/shard_map/all_gather | solution.py:236
  9.0 11.3 %collective-permute-start = (bf16[512,1024]{1,0:T(8,128)(2,1)}, bf16[512,1024]{1,0:T(8,128)(2,1)S(1)}, u32[]{:S(2)}, u32[]{:S(2)}) collective-permute-start(bf16[512,1024]{1,0:T(8,128)(2,1)} %dynamic-slice_bitcast_fusion.1), channel_id=1, source_target_pairs={{0,64},{64,0},{1,65},{65,1},{2,66},{66,2},{3,67},{67,3},{4,68},{68... | collective-permute-start | bytes 3145736 | tf_op jit(solution)/shard_map/ppermute | solution.py:223
  20.4 8.0 %copy-start.12 = (s32[16]{0:T(128)S(1)}, s32[16]{0:T(128)}, u32[]{:S(2)}) copy-start(s32[16]{0:T(128)} %param.11) | copy-start | bytes 196
  20.4 8.1 %copy-start.10 = (s32[16,8]{0,1:T(8,128)S(1)}, s32[16,8]{0,1:T(8,128)}, u32[]{:S(2)}) copy-start(s32[16,8]{0,1:T(8,128)} %param.9) | copy-start | bytes 1540
  20.4 8.2 %copy-start.11 = (f32[16,8]{0,1:T(8,128)S(1)}, f32[16,8]{0,1:T(8,128)}, u32[]{:S(2)}) copy-start(f32[16,8]{0,1:T(8,128)} %param.10) | copy-start | bytes 1540
  21.9 54.4 %collective-permute-start.1 = (bf16[1024,1024]{1,0:T(8,128)(2,1)}, bf16[1024,1024]{1,0:T(8,128)(2,1)S(1)}, u32[]{:S(2)}, u32[]{:S(2)}) collective-permute-start(bf16[1024,1024]{1,0:T(8,128)(2,1)} %pad_maximum_fusion.mid), channel_id=1, source_target_pairs={{0,128},{128,256},{256,384},{384,0},{1,129},{129,257},{257,385},{3... | collective-permute-start | bytes 6291464 | tf_op jit(solution)/shard_map/ppermute | solution.py:213
  23.8 53.4 %collective-permute-start.2 = (bf16[1024,1024]{1,0:T(8,128)(2,1)}, bf16[1024,1024]{1,0:T(8,128)(2,1)}, u32[]{:S(2)}, u32[]{:S(2)}) collective-permute-start(bf16[1024,1024]{1,0:T(8,128)(2,1)} %pad_maximum_fusion.mid), channel_id=1, source_target_pairs={{0,384},{128,0},{256,128},{384,256},{1,385},{129,1},{257,129},{385... | collective-permute-start | bytes 6291464 | tf_op jit(solution)/shard_map/ppermute | solution.py:213
  76.3 4.9 %copy-start = (bf16[1024,1024]{1,0:T(8,128)(2,1)}, bf16[1024,1024]{1,0:T(8,128)(2,1)S(1)}, u32[]{:S(2)}) copy-start(bf16[1024,1024]{1,0:T(8,128)(2,1)S(1)} %collective-permute-done.1.rest_0_.left) | copy-start | bytes 6291460
  77.2 1.2 copy-start.2
  81.2 1.4 copy-start.4
  82.5 39.8 %all-to-all-start = ((bf16[16,16,4224]{2,1,0:T(8,128)(2,1)}), bf16[16,16,4224]{2,1,0:T(8,128)(2,1)S(1)}, u32[]{:S(2)}, u32[]{:S(2)}) async-start(bf16[16,16,4224]{2,1,0:T(8,128)(2,1)} %copy-done.4), calls=%async_computation | async-start | bytes 4325376 | tf_op jit(solution)/shard_map/all_to_all | solution.py:249
  87.6 163.1 %reduce-scatter.2.cloned.1.call-start = ((), (), s32[]{:S(2)}) async-start(), calls=%async_computation.3 | async-start | bytes 1179648 | tf_op jit(solution)/shard_map/reduce_scatter | solution.py:256
  87.6 12.1 %copy-start.5 = (bf16[2,1024,512]{2,1,0:T(8,128)(2,1)S(1)}, bf16[2,1024,512]{2,1,0:T(8,128)(2,1)}, u32[]{:S(2)}) copy-start(bf16[2,1024,512]{2,1,0:T(8,128)(2,1)} %w_own.1) | copy-start | bytes 6291460
  90.0 32.3 %copy-start.7 = (bf16[2,64,1024]{2,1,0:T(8,128)(2,1)S(1)}, bf16[2,64,1024]{2,1,0:T(8,128)(2,1)}, u32[]{:S(2)}) copy-start(bf16[2,64,1024]{2,1,0:T(8,128)(2,1)} %a_out.1) | copy-start | bytes 786436
  90.0 29.1 %collective-permute-start.3 = (bf16[512,1024]{1,0:T(8,128)(2,1)}, bf16[512,1024]{1,0:T(8,128)(2,1)}, u32[]{:S(2)}, u32[]{:S(2)}) collective-permute-start(bf16[512,1024]{1,0:T(8,128)(2,1)} %slice.8), channel_id=1, source_target_pairs={{0,128},{128,256},{256,384},{384,0},{1,129},{129,257},{257,385},{3... | collective-permute-start | bytes 3145736 | tf_op jit(solution)/shard_map/ppermute | solution.py:213
  94.4 28.0 %collective-permute-start.4 = (bf16[512,1024]{1,0:T(8,128)(2,1)}, bf16[512,1024]{1,0:T(8,128)(2,1)}, u32[]{:S(2)}, u32[]{:S(2)}) collective-permute-start(bf16[512,1024]{1,0:T(8,128)(2,1)} %slice.9), channel_id=1, source_target_pairs={{0,384},{128,0},{256,128},{384,256},{1,385},{129,1},{257,129},{385... | collective-permute-start | bytes 3145736 | tf_op jit(solution)/shard_map/ppermute | solution.py:213
  100.8 55.8 %collective-permute-start.5 = (bf16[1024,512]{1,0:T(8,128)(2,1)}, bf16[1024,512]{1,0:T(8,128)(2,1)}, u32[]{:S(2)}, u32[]{:S(2)}) collective-permute-start(bf16[1024,512]{1,0:T(8,128)(2,1)} %dynamic-slice_bitcast_fusion), channel_id=1, source_target_pairs={{0,64},{64,0},{1,65},{65,1},{2,66},{66,2},{3,67},{67,3},{4,68},{68... | collective-permute-start | bytes 3145736 | tf_op jit(solution)/shard_map/ppermute | solution.py:223
  122.4 1.6 copy-start.1
  123.9 1.2 copy-start.3
  156.2 1.6 copy-start.6
Sparse Core Ops, SparseCore 0:
  17.9 32.1 all-gather.6
  203.1 47.5 reduce-scatter.1

commit v7 on v6

--- a/solution.py
+++ b/solution.py
@@ -79,48 +79,40 @@
     )(z1, table, table, *after)
 
 
-def _around(g, x):
-    return lax.rem(x + jnp.where(g == 0, 0, jnp.where(g == 1, 3, jnp.where(g == 2, 1, 2))), 4)
-
-
-def _up_kernel(at, x_ref, m_ref, mid, left, right, far_low, far_high, a_low, a_high, a_out, o_ref, acc, shrink):
+HELD = ((0, 0, 768), (0, 768, 256), (3, 0, 768), (3, 768, 256), (1, 256, 768), (1, 0, 256), (2, 0, 512), (2, 512, 512))
+
+
+def _up_kernel(at, x_ref, *refs):
+    w = refs[: len(HELD)]
+    a_in, a_out, o_ref, high, low, hidden = refs[len(HELD) :]
     g = pl.program_id(0)
-    lanes = (((1,), (1,)), ((), ()))
 
     @pl.when(g == 0)
     def _():
-        acc[...] = jnp.dot(x_ref[...], mid[...], preferred_element_type=F32)
-        shrink[...] = jnp.zeros_like(shrink)
-
-    @pl.when(g == 1)
-    def _():
-        acc[...] += jnp.dot(x_ref[...], left[...], preferred_element_type=F32)
-
-    @pl.when(g == 2)
-    def _():
-        acc[...] += jnp.dot(x_ref[...], right[...], preferred_element_type=F32)
+        kept = jnp.zeros((ROWS, 64), F32)
+        for i in range(8):
+            part = x_ref[:, i * 512 : i * 512 + 512]
+            kept += lax.dot_general(part, a_in[i, 0], (((1,), (1,)), ((), ())), preferred_element_type=F32)
+        kept *= x_ref[:, WIDE : WIDE + 64].astype(F32)
+        high[...] = kept.astype(BF)
+        low[...] = (kept - high[...].astype(F32)).astype(BF)
+
+    v = jnp.dot(high[...], a_out[0], preferred_element_type=F32)
+    v += jnp.dot(low[...], a_out[0], preferred_element_type=F32)
+    for ref, (away, start, size) in zip(w, HELD):
+        first = pl.multiple_of(lax.rem(at[1] + away, 4) * PIECE + start, 256)
+        v += jnp.dot(x_ref[:, pl.ds(first, size)], ref[...], preferred_element_type=F32)
+    hidden[g] = (v / (1.0 + jnp.exp(-v))).astype(BF).astype(F32)
 
     @pl.when(g == 3)
     def _():
-        far = jnp.dot(x_ref[:, :512], far_low[...], preferred_element_type=F32)
-        far += jnp.dot(x_ref[:, 512:], far_high[...], preferred_element_type=F32)
-        acc[...] += far
-
-    less = lax.dot_general(x_ref[:, :512], a_low[0, 0], lanes, preferred_element_type=F32)
-    less += lax.dot_general(x_ref[:, 512:], a_high[0, 0], lanes, preferred_element_type=F32)
-    shrink[...] += less
-
-    @pl.when(g == 3)
-    def _():
-        kept = shrink[...] * m_ref[:, :64].astype(F32)
-        high = kept.astype(BF)
-        low = (kept - high.astype(F32)).astype(BF)
-        v = acc[...] + jnp.dot(high, a_out[0], preferred_element_type=F32)
-        v += jnp.dot(low, a_out[0], preferred_element_type=F32)
-        hidden = (v / (1.0 + jnp.exp(-v))).astype(BF).astype(F32)
-        peak = jnp.max(jnp.abs(hidden), axis=1, keepdims=True)
+        peak = jnp.max(jnp.abs(hidden[0]), axis=1, keepdims=True)
+        for i in range(1, 4):
+            peak = jnp.maximum(peak, jnp.max(jnp.abs(hidden[i]), axis=1, keepdims=True))
         power = jnp.floor(jnp.log2(jnp.maximum(peak, 1e-30)))
-        o_ref[:, :PIECE] = (hidden * jnp.exp2(-power)).astype(BF)
+        scale = jnp.exp2(-power)
+        for i in range(4):
+            o_ref[:, i * 256 : i * 256 + 256] = (hidden[i] * scale).astype(BF)
         o_ref[:, PIECE:] = jnp.broadcast_to(power, (ROWS, META)).astype(BF)
 
 
@@ -130,23 +122,23 @@
         grid_spec=pltpu.PrefetchScalarGridSpec(
             num_scalar_prefetch=1,
             grid=(4,),
-            in_specs=[
-                pl.BlockSpec((ROWS, PIECE), lambda g, at: (0, _around(g, at[1]))),
-                pl.BlockSpec((ROWS, META), lambda g, at: (0, WIDE // META)),
-            ]
-            + [pl.BlockSpec(p.shape, lambda g, at: (0, 0)) for p in w]
+            in_specs=[pl.BlockSpec((ROWS, WIDE + META), lambda g, at: (0, 0))]
+            + [pl.BlockSpec((p.shape[0], 256), lambda g, at: (0, g)) for p in w]
             + [
-                pl.BlockSpec((1, 1, 64, 512), lambda g, at: (2 * _around(g, at[1]), at[0], 0, 0)),
-                pl.BlockSpec((1, 1, 64, 512), lambda g, at: (2 * _around(g, at[1]) + 1, at[0], 0, 0)),
-                pl.BlockSpec((1, 64, PIECE), lambda g, at: (at[0], 0, 0)),
+                pl.BlockSpec((8, 1, 64, 512), lambda g, at: (0, at[0], 0, 0)),
+                pl.BlockSpec((1, 64, 256), lambda g, at: (at[0], 0, g)),
             ],
             out_specs=pl.BlockSpec((ROWS, PIECE + META), lambda g, at: (0, 0)),
-            scratch_shapes=[pltpu.VMEM((ROWS, PIECE), F32), pltpu.VMEM((ROWS, 64), F32)],
+            scratch_shapes=[
+                pltpu.VMEM((ROWS, 64), BF),
+                pltpu.VMEM((ROWS, 64), BF),
+                pltpu.VMEM((4, ROWS, 256), F32),
+            ],
         ),
         out_shape=jax.ShapeDtypeStruct((ROWS, PIECE + META), BF),
         compiler_params=_params(32),
         name="up",
-    )(at, rows, rows, *w, a_in, a_in, a_out)
+    )(at, rows, *w, a_in, a_out)
 
 
 def _down_kernel(c_ref, h_ref, m_ref, w_own, w_other, o_ref):
@@ -213,10 +205,12 @@
     return lax.ppermute(v, "x", [(i, (i + by) % 4) for i in range(4)])
 
 
-def _gather_x(w):
-    k = w.shape[0] // 2
-    left, right = _shift_x(w, 1), _shift_x(w, -1)
-    return [w, left, right, _shift_x(left[:k], 1), _shift_x(right[k:], -1)]
+def _gather_x(first, second):
+    wide, tail = jnp.concatenate([first, second[:256]], axis=0), second[256:]
+    broad, head = jnp.concatenate([first[256:], second], axis=0), first[:256]
+    left, right = _shift_x(wide, 1), _shift_x(broad, -1)
+    far = [_shift_x(left[:512], 1), _shift_x(right[256:], -1)]
+    return [wide, tail, left, _shift_x(tail, 1), right, _shift_x(head, -1)] + far
 
 
 def _swap(v):
@@ -232,7 +226,7 @@
 
     up_own, up_other = one(up_weight, core), _swap(one(up_weight, 1 - core))
     first, second = jnp.where(core == 0, up_own, up_other), jnp.where(core == 0, up_other, up_own)
-    w_up = _gather_x(jnp.concatenate([first, second], axis=0))
+    w_up = _gather_x(first, second)
     a_in = lax.all_gather(adapter_in.transpose(0, 2, 1), ("x", "core"), axis=0)
     down_other = _swap(one(down_weight, 1 - core))
 
@@ -245,7 +239,7 @@
     table = lax.all_gather(mine, "z1", axis=0).astype(F32)
     lift = jnp.where(jnp.arange(WIDE + META) < WIDE, 1.0 / LIFT, 1.0)
     table = (table * lift).astype(BF)
-    sending = _select(z1, table, w_up[1:3] + [a_in])
+    sending = _select(z1, table, [w_up[2], w_up[4], a_in])
     arrived = lax.all_to_all(sending, ("y", "core", "z0"), 0, 0, tiled=True).reshape(ROWS, WIDE + META)
 
     hidden = _up(at, arrived, w_up, a_in, adapter_out)

time: 260 us -> 259 us (level)
  starting transfers between devices: 30.1 us -> 34.7 us
  waiting for transfers between devices: 87 us -> 83.4 us
    ppermute x4 -> x6, starting transfers between devices: 13.8 us -> 17.6 us  [_shift_x(): return lax.ppermute(v, 'x', [(i, (i + by) % 4) for i in range(4)])]
    ppermute x4 -> x6, waiting for transfers between devices: 36.8 us -> 34.5 us  [_shift_x(): return lax.ppermute(v, 'x', [(i, (i + by) % 4) for i in range(4)])]
    unnamed x26 -> x22, local copies, waits for them, and re-layouts: 6.66 us -> 5.04 us
  transfers between devices with their start and end apart: 9 -> 11, of which waited for: 6 -> 5; matrix products, arithmetic and copies ran while one was open for 3% -> 4% of each run, Pallas kernels for 3% -> 3%
where the time goes in v7:
time: 259 us; the launch traced here: 256 us
  blocking collectives  90 us (35%)
  waiting for transfers between devices  83.4 us (32%)
  starting transfers between devices  34.7 us (13%)
  Pallas kernels  17.4 us (7%)
  between operations  13.7 us (5%)
  local copies, waits for them, and re-layouts  13.1 us (5%)
  other arithmetic  3.54 us (1%)
    reduce_scatter x1, waiting for transfers between devices, per_device(): return lax.psum_scatter(partial, 'z1', scatter_dimension=0, tiled=True)  46.8 us
    all_to_all x1, blocking collectives, per_device(): lax.all_to_all(out.reshape(64, 16, PIECE), ('x', 'y', 'core', 'z0'), 0, 0...  36.8 us
    ppermute x6, waiting for transfers between devices, _shift_x(): return lax.ppermute(v, 'x', [(i, (i + by) % 4) for i in range(4)])  34.5 us
    all_gather x1, blocking collectives, per_device(): table = lax.all_gather(mine, 'z1', axis=0).astype(F32)  31.6 us
    all_gather x1, blocking collectives, per_device(): hidden = lax.all_gather(hidden.astype(F16), 'x', axis=0).astype(BF)  21.7 us
    ppermute x6, starting transfers between devices, _shift_x(): return lax.ppermute(v, 'x', [(i, (i + by) % 4) for i in range(4)])  17.6 us
    ppermute x2, starting transfers between devices, _swap(): return lax.ppermute(v, 'core', [(0, 1), (1, 0)])  11.7 us
    pallas_call x1, Pallas kernels, _up(): pl.pallas_call(_up_kernel, grid_spec=pltpu.PrefetchScalarGridSpec(num_sca...  7.73 us
  transfers between devices with their start and end apart: 11, of which 5 were waited for; matrix products, arithmetic and copies ran while one was open for 4% of the time, Pallas kernels for 3%

profile of v7, /device:TPU:1, one launch (start us, length us, event | category | flops | bytes accessed | tf_op | source)
XLA Modules:
  0.0 255.8 jit_solution(4833630254795711171)
XLA Ops:
  6.5 0.0 all-gather.7.cloned.1.call-start
  6.6 2.5 dynamic-slice_bitcast_fusion.1
  9.1 8.8 %collective-permute-start = (bf16[512,1024]{1,0:T(8,128)(2,1)}, bf16[512,1024]{1,0:T(8,128)(2,1)S(1)}, u32[]{:S(2)}, u32[]{:S(2)}) collective-permute-start(bf16[512,1024]{1,0:T(8,128)(2,1)} %dynamic-slice_bitcast_fusion.1), channel_id=1, source_target_pairs={{0,64},{64,0},{1,65},{65,1},{2,66},{66,2},{3,67},{67,3},{4,68},{68... | collective-permute-start | bytes 3145736 | tf_op jit(solution)/shard_map/ppermute | solution.py:217
  17.8 0.0 all-gather.7.cloned.1.call-update
  17.9 0.1 compare_convert_fusion
  18.0 0.1 copy.11
  18.1 0.1 copy.12
  18.2 0.1 concatenate.9
  18.3 2.0 collective-permute-done
  20.3 0.1 bitcast_select_fusion.1
  20.5 0.9 fusion.2
  21.3 0.1 fusion.3
  21.4 1.3 pad_maximum_fusion.1
  22.7 1.9 collective-permute-start.2
  24.6 1.3 pad_maximum_fusion.refs_0_
  25.9 3.4 %collective-permute-start.1 = (bf16[768,1024]{1,0:T(8,128)(2,1)}, bf16[768,1024]{1,0:T(8,128)(2,1)}, u32[]{:S(2)}, u32[]{:S(2)}) collective-permute-start(bf16[768,1024]{1,0:T(8,128)(2,1)} %pad_maximum_fusion.refs_0_), channel_id=1, source_target_pairs={{0,128},{128,256},{256,384},{384,0},{1,129},{129,257},{257,385},{3... | collective-permute-start | bytes 4718600 | tf_op jit(solution)/shard_map/ppermute | solution.py:205
  29.3 31.6 %all-gather.8 = f16[128,4224]{1,0:T(8,128)(2,1)S(1)} all-gather(f16[16,4224]{1,0:T(8,128)(2,1)S(1)} %concatenate.9), channel_id=2, replica_groups=mesh['x'=4,'core'=2,'z1'=8,'z0'=2,'y'=4] {'z1'}, dimensions={0}, use_global_device_ids=true | all-gather | bytes 1216512 | tf_op jit(solution)/shard_map/all_gather | solution.py:239
  60.8 0.2 fusion.m_ref.t_ref
  61.0 0.0 all-gather.7.cloned.1.call-done
  61.0 3.7 %collective-permute-done.2.rest_1_.refs_4_ = bf16[768,1024]{1,0:T(8,128)(2,1)S(1)} collective-permute-done((bf16[768,1024]{1,0:T(8,128)(2,1)}, bf16[768,1024]{1,0:T(8,128)(2,1)S(1)}, u32[]{:S(2)}, u32[]{:S(2)}) %collective-permute-start.2) | collective-permute-done | bytes 1572896 | tf_op jit(solution)/shard_map/ppermute | solution.py:205
  64.7 4.4 %collective-permute-done.1.rest_0_.refs_2_ = bf16[768,1024]{1,0:T(8,128)(2,1)} collective-permute-done((bf16[768,1024]{1,0:T(8,128)(2,1)}, bf16[768,1024]{1,0:T(8,128)(2,1)}, u32[]{:S(2)}, u32[]{:S(2)}) %collective-permute-start.1) | collective-permute-done | bytes 1572896 | tf_op jit(solution)/shard_map/ppermute | solution.py:205
  69.1 1.2 copy-done.3
  70.4 2.7 %select.9 = bf16[16,16,4224]{2,1,0:T(8,128)(2,1)S(1)} custom-call(s32[1]{0:T(128)} %bitcast.z_ref, bf16[8,16,4224]{2,1,0:T(8,128)(2,1)S(1)} %fusion.m_ref.t_ref, bf16[8,16,4224]{2,1,0:T(8,128)(2,1)S(1)} %fusion.m_ref.t_ref, bf16[768,1024]{1,0:T(8,128)(2,1)} %collective-permute-done.1.rest_0_.refs_2_, ...), custom_call_target="tpu_custom_call" | custom-call | tf_op jit(solution)/shard_map/select/pallas_call | solution.py:64
  73.1 1.3 copy-done
  74.4 5.4 %all-to-all-start = ((bf16[16,16,4224]{2,1,0:T(8,128)(2,1)}), bf16[16,16,4224]{2,1,0:T(8,128)(2,1)}, u32[]{:S(2)}, u32[]{:S(2)}) async-start(bf16[16,16,4224]{2,1,0:T(8,128)(2,1)} %copy-done), calls=%async_computation | async-start | bytes 4325376 | tf_op jit(solution)/shard_map/all_to_all | solution.py:243
  79.8 0.0 reduce-scatter.2.cloned.1.call-start
  79.8 0.0 copy-start.1
  79.9 1.1 slice.29
  80.9 3.9 %collective-permute-start.6 = (bf16[512,1024]{1,0:T(8,128)(2,1)}, bf16[512,1024]{1,0:T(8,128)(2,1)}, u32[]{:S(2)}, u32[]{:S(2)}) collective-permute-start(bf16[512,1024]{1,0:T(8,128)(2,1)} %slice.29), channel_id=1, source_target_pairs={{0,384},{128,0},{256,128},{384,256},{1,385},{129,1},{257,129},{385... | collective-permute-start | bytes 3145736 | tf_op jit(solution)/shard_map/ppermute | solution.py:205
  84.9 2.3 slice.28
  87.1 1.9 collective-permute-start.5
  89.0 1.9 collective-permute-start.3
  91.0 4.6 %collective-permute-start.4 = (bf16[256,1024]{1,0:T(8,128)(2,1)}, bf16[256,1024]{1,0:T(8,128)(2,1)}, u32[]{:S(2)}, u32[]{:S(2)}) collective-permute-start(bf16[256,1024]{1,0:T(8,128)(2,1)} %get-tuple-element.7), channel_id=1, source_target_pairs={{0,384},{128,0},{256,128},{384,256},{1,385},{129,1},{257,129},{385... | collective-permute-start | bytes 1572872 | tf_op jit(solution)/shard_map/ppermute | solution.py:205
  95.6 1.1 dynamic-slice_bitcast_fusion
  96.6 2.9 %collective-permute-start.7 = (bf16[1024,512]{1,0:T(8,128)(2,1)}, bf16[1024,512]{1,0:T(8,128)(2,1)}, u32[]{:S(2)}, u32[]{:S(2)}) collective-permute-start(bf16[1024,512]{1,0:T(8,128)(2,1)} %dynamic-slice_bitcast_fusion), channel_id=1, source_target_pairs={{0,64},{64,0},{1,65},{65,1},{2,66},{66,2},{3,67},{67,3},{4,68},{68... | collective-permute-start | bytes 3145736 | tf_op jit(solution)/shard_map/ppermute | solution.py:217
  99.6 0.1 pad_add_fusion.at
  99.6 26.4 %collective-permute-done.3.refs_3_ = bf16[256,1024]{1,0:T(8,128)(2,1)} collective-permute-done((bf16[256,1024]{1,0:T(8,128)(2,1)S(1)}, bf16[256,1024]{1,0:T(8,128)(2,1)}, u32[]{:S(2)}, u32[]{:S(2)}) %collective-permute-start.3) | collective-permute-done | bytes 524320 | tf_op jit(solution)/shard_map/ppermute | solution.py:205
  126.1 1.2 copy-done.4
  127.3 7.7 %up.1 = bf16[256,1152]{1,0:T(8,128)(2,1)S(1)} custom-call(s32[2]{0:T(128)S(1)} %pad_add_fusion.at, bf16[256,4224]{1,0:T(8,128)(2,1)} %bitcast.8.x_ref, bf16[768,1024]{1,0:T(8,128)(2,1)} %pad_maximum_fusion.refs_0_, bf16[256,1024]{1,0:T(8,128)(2,1)S(1)} %get-tuple-element.9.refs_1_, bf16[768,1024]{1,0:T(8,128)(2,1)} %collective-permute-done.1.rest_0_.refs_2_, ...), custom_call_target="tpu_custom_call" | custom-call | tf_op jit(solution)/shard_map/up/pallas_call | solution.py:120
  135.1 0.1 convert_element_type.34
  135.2 21.7 %all-gather.9 = f16[1024,1152]{1,0:T(8,128)(2,1)S(1)} all-gather(f16[256,1152]{1,0:T(8,128)(2,1)S(1)} %convert_element_type.34), channel_id=4, replica_groups=mesh['x'=4,'core'=2,'z1'=8,'z0'=2,'y'=4] {'x'}, dimensions={0}, use_global_device_ids=true | all-gather | bytes 2949120 | tf_op jit(solution)/shard_map/all_gather | solution.py:246
  156.9 0.3 convert_element_type.37
  157.2 1.2 copy-done.2
  158.5 4.3 %down.1 = bf16[4,16,16,1024]{3,2,1,0:T(8,128)(2,1)S(1)} custom-call(s32[1]{0:T(128)} %bitcast.2.c_ref, bf16[4,256,1152]{2,1,0:T(8,128)(2,1)S(1)} %bitcast.18, bf16[4,256,1152]{2,1,0:T(8,128)(2,1)S(1)} %bitcast.19, bf16[2,1024,512]{2,1,0:T(8,128)(2,1)S(1)} %copy-done.2, bf16[1024,512]{1,0:T(8,128)(2,1)} %collective-permute-done.7.w_other), custom_call_target="tpu_custom_call" | custom-call | tf_op jit(solution)/shard_map/down/pallas_call | solution.py:153
  162.8 36.8 %all_to_all.10 = bf16[64,16,1024]{2,1,0:T(8,128)(2,1)S(1)} all-to-all(bf16[64,16,1024]{2,1,0:T(8,128)(2,1)S(1)} %bitcast.20), channel_id=1, replica_groups=mesh['x'=4,'core'=2,'z1'=8,'z0'=2,'y'=4] {'x','y','core','z0'}, dimensions={0} | all-to-all | bytes 4194304 | tf_op jit(solution)/shard_map/all_to_all | solution.py:248
  199.5 2.6 %combine.1 = bf16[128,4096]{1,0:T(8,128)(2,1)} custom-call(s32[1]{0:T(128)} %bitcast.z_ref, bf16[8,16,4224]{2,1,0:T(8,128)(2,1)S(1)} %fusion.m_ref.t_ref, bf16[4,16,16,1024]{3,2,1,0:T(8,128)(2,1)S(1)} %bitcast.21), custom_call_target="tpu_custom_call" | custom-call | tf_op jit(solution)/shard_map/combine/pallas_call | solution.py:186
  202.2 0.0 reduce-scatter.2.cloned.1.call-update
  202.2 46.8 %reduce-scatter.2.cloned.1.call-done = bf16[16,4096]{1,0:T(8,128)(2,1)} async-done(((bf16[128,4096]{1,0:T(8,128)(2,1)}), bf16[16,4096]{1,0:T(8,128)(2,1)}) %reduce-scatter.2.cloned.1.call-update) | async-done | bytes 131088 | tf_op jit(solution)/shard_map/reduce_scatter | solution.py:250
  (28 shorter events, 0.1 us)
Async XLA Ops:
  6.5 13.8 %copy-start.6 = (bf16[2,512,1024]{2,1,0:T(8,128)(2,1)S(1)}, bf16[2,512,1024]{2,1,0:T(8,128)(2,1)}, u32[]{:S(2)}) copy-start(bf16[2,512,1024]{2,1,0:T(8,128)(2,1)} %param.12) | copy-start | bytes 6291460
  6.5 11.3 %copy-start.10 = (s32[16]{0:T(128)S(1)}, s32[16]{0:T(128)}, u32[]{:S(2)}) copy-start(s32[16]{0:T(128)} %param.11) | copy-start | bytes 196
  6.5 11.4 %copy-start.8 = (s32[16,8]{0,1:T(8,128)S(1)}, s32[16,8]{0,1:T(8,128)}, u32[]{:S(2)}) copy-start(s32[16,8]{0,1:T(8,128)} %param.9) | copy-start | bytes 1540
  6.5 11.5 %copy-start.9 = (f32[16,8]{0,1:T(8,128)S(1)}, f32[16,8]{0,1:T(8,128)}, u32[]{:S(2)}) copy-start(f32[16,8]{0,1:T(8,128)} %param.10) | copy-start | bytes 1540
  6.5 11.6 %copy-start.7 = (bf16[16,4096]{1,0:T(8,128)(2,1)S(1)}, bf16[16,4096]{1,0:T(8,128)(2,1)}, u32[]{:S(2)}) copy-start(bf16[16,4096]{1,0:T(8,128)(2,1)} %param.8) | copy-start | bytes 393220
  6.5 54.5 %all-gather.7.cloned.1.call-start = ((), (), s32[]{:S(2)}) async-start(), calls=%async_computation.4 | async-start | bytes 1179648 | tf_op jit(solution)/shard_map/all_gather | solution.py:230
  9.1 11.3 %collective-permute-start = (bf16[512,1024]{1,0:T(8,128)(2,1)}, bf16[512,1024]{1,0:T(8,128)(2,1)S(1)}, u32[]{:S(2)}, u32[]{:S(2)}) collective-permute-start(bf16[512,1024]{1,0:T(8,128)(2,1)} %dynamic-slice_bitcast_fusion.1), channel_id=1, source_target_pairs={{0,64},{64,0},{1,65},{65,1},{2,66},{66,2},{3,67},{67,3},{4,68},{68... | collective-permute-start | bytes 3145736 | tf_op jit(solution)/shard_map/ppermute | solution.py:217
  22.7 42.0 %collective-permute-start.2 = (bf16[768,1024]{1,0:T(8,128)(2,1)}, bf16[768,1024]{1,0:T(8,128)(2,1)S(1)}, u32[]{:S(2)}, u32[]{:S(2)}) collective-permute-start(bf16[768,1024]{1,0:T(8,128)(2,1)} %pad_maximum_fusion.1), channel_id=1, source_target_pairs={{0,384},{128,0},{256,128},{384,256},{1,385},{129,1},{257,129},{385... | collective-permute-start | bytes 4718600 | tf_op jit(solution)/shard_map/ppermute | solution.py:205
  25.9 43.2 %collective-permute-start.1 = (bf16[768,1024]{1,0:T(8,128)(2,1)}, bf16[768,1024]{1,0:T(8,128)(2,1)}, u32[]{:S(2)}, u32[]{:S(2)}) collective-permute-start(bf16[768,1024]{1,0:T(8,128)(2,1)} %pad_maximum_fusion.refs_0_), channel_id=1, source_target_pairs={{0,128},{128,256},{256,384},{384,0},{1,129},{129,257},{257,385},{3... | collective-permute-start | bytes 4718600 | tf_op jit(solution)/shard_map/ppermute | solution.py:205
  69.1 1.2 copy-start.3
  73.1 1.3 copy-start
  74.4 51.7 %all-to-all-start = ((bf16[16,16,4224]{2,1,0:T(8,128)(2,1)}), bf16[16,16,4224]{2,1,0:T(8,128)(2,1)}, u32[]{:S(2)}, u32[]{:S(2)}) async-start(bf16[16,16,4224]{2,1,0:T(8,128)(2,1)} %copy-done), calls=%async_computation | async-start | bytes 4325376 | tf_op jit(solution)/shard_map/all_to_all | solution.py:243
  79.8 169.2 %reduce-scatter.2.cloned.1.call-start = ((), (), s32[]{:S(2)}) async-start(), calls=%async_computation.3 | async-start | bytes 1179648 | tf_op jit(solution)/shard_map/reduce_scatter | solution.py:250
  79.8 15.7 %copy-start.1 = (bf16[2,1024,512]{2,1,0:T(8,128)(2,1)S(1)}, bf16[2,1024,512]{2,1,0:T(8,128)(2,1)}, u32[]{:S(2)}) copy-start(bf16[2,1024,512]{2,1,0:T(8,128)(2,1)} %w_own.1) | copy-start | bytes 6291460
  80.9 45.2 %copy-start.5 = (bf16[2,64,1024]{2,1,0:T(8,128)(2,1)S(1)}, bf16[2,64,1024]{2,1,0:T(8,128)(2,1)}, u32[]{:S(2)}) copy-start(bf16[2,64,1024]{2,1,0:T(8,128)(2,1)} %refs_9_.1) | copy-start | bytes 786436
  80.9 45.1 %collective-permute-start.6 = (bf16[512,1024]{1,0:T(8,128)(2,1)}, bf16[512,1024]{1,0:T(8,128)(2,1)}, u32[]{:S(2)}, u32[]{:S(2)}) collective-permute-start(bf16[512,1024]{1,0:T(8,128)(2,1)} %slice.29), channel_id=1, source_target_pairs={{0,384},{128,0},{256,128},{384,256},{1,385},{129,1},{257,129},{385... | collective-permute-start | bytes 3145736 | tf_op jit(solution)/shard_map/ppermute | solution.py:205
  87.1 38.9 %collective-permute-start.5 = (bf16[512,1024]{1,0:T(8,128)(2,1)}, bf16[512,1024]{1,0:T(8,128)(2,1)}, u32[]{:S(2)}, u32[]{:S(2)}) collective-permute-start(bf16[512,1024]{1,0:T(8,128)(2,1)} %slice.28), channel_id=1, source_target_pairs={{0,128},{128,256},{256,384},{384,0},{1,129},{129,257},{257,385},{3... | collective-permute-start | bytes 3145736 | tf_op jit(solution)/shard_map/ppermute | solution.py:205
  89.0 37.0 %collective-permute-start.3 = (bf16[256,1024]{1,0:T(8,128)(2,1)S(1)}, bf16[256,1024]{1,0:T(8,128)(2,1)}, u32[]{:S(2)}, u32[]{:S(2)}) collective-permute-start(bf16[256,1024]{1,0:T(8,128)(2,1)S(1)} %get-tuple-element.9.refs_1_), channel_id=1, source_target_pairs={{0,128},{128,256},{256,384},{384,0},{1,129},{129,257},{257,385},{3... | collective-permute-start | bytes 1572872 | tf_op jit(solution)/shard_map/ppermute | solution.py:205
  91.0 35.1 %collective-permute-start.4 = (bf16[256,1024]{1,0:T(8,128)(2,1)}, bf16[256,1024]{1,0:T(8,128)(2,1)}, u32[]{:S(2)}, u32[]{:S(2)}) collective-permute-start(bf16[256,1024]{1,0:T(8,128)(2,1)} %get-tuple-element.7), channel_id=1, source_target_pairs={{0,384},{128,0},{256,128},{384,256},{1,385},{129,1},{257,129},{385... | collective-permute-start | bytes 1572872 | tf_op jit(solution)/shard_map/ppermute | solution.py:205
  96.6 60.6 %collective-permute-start.7 = (bf16[1024,512]{1,0:T(8,128)(2,1)}, bf16[1024,512]{1,0:T(8,128)(2,1)}, u32[]{:S(2)}, u32[]{:S(2)}) collective-permute-start(bf16[1024,512]{1,0:T(8,128)(2,1)} %dynamic-slice_bitcast_fusion), channel_id=1, source_target_pairs={{0,64},{64,0},{1,65},{65,1},{2,66},{66,2},{3,67},{67,3},{4,68},{68... | collective-permute-start | bytes 3145736 | tf_op jit(solution)/shard_map/ppermute | solution.py:217
  126.1 1.2 copy-start.4
  156.9 1.6 copy-start.2
Sparse Core Ops, SparseCore 0:
  18.0 32.1 all-gather.6
  202.3 46.6 reduce-scatter.1

commit v8 on v7

--- a/solution.py
+++ b/solution.py
@@ -79,12 +79,22 @@
     )(z1, table, table, *after)
 
 
-HELD = ((0, 0, 768), (0, 768, 256), (3, 0, 768), (3, 768, 256), (1, 256, 768), (1, 0, 256), (2, 0, 512), (2, 512, 512))
+HELD = (
+    (0, 0, 256, 0, 0, 0),
+    (0, 256, 512, 0, 1, 0),
+    (1, 0, 256, 3, 0, 0),
+    (1, 256, 512, 3, 1, 0),
+    (2, 0, 256, 1, 0, 0),
+    (2, 256, 512, 1, 1, 0),
+    (3, 0, 256, 2, 0, 0),
+    (3, 256, 128, 2, 1, 0),
+    (4, 0, 384, 2, 1, 128),
+)
 
 
 def _up_kernel(at, x_ref, *refs):
-    w = refs[: len(HELD)]
-    a_in, a_out, o_ref, high, low, hidden = refs[len(HELD) :]
+    w = refs[:5]
+    w_own, a_in, a_out, o_ref, high, low, hidden = refs[5:]
     g = pl.program_id(0)
 
     @pl.when(g == 0)
@@ -99,9 +109,13 @@
 
     v = jnp.dot(high[...], a_out[0], preferred_element_type=F32)
     v += jnp.dot(low[...], a_out[0], preferred_element_type=F32)
-    for ref, (away, start, size) in zip(w, HELD):
-        first = pl.multiple_of(lax.rem(at[1] + away, 4) * PIECE + start, 256)
-        v += jnp.dot(x_ref[:, pl.ds(first, size)], ref[...], preferred_element_type=F32)
+    for held, row, size, away, side, start in HELD:
+        core = at[0] if side == 0 else 1 - at[0]
+        first = pl.multiple_of(lax.rem(at[1] + away, 4) * PIECE + core * 512 + start, 128)
+        v += jnp.dot(x_ref[:, pl.ds(first, size)], w[held][row : row + size], preferred_element_type=F32)
+    for i in range(4):
+        first = pl.multiple_of(i * PIECE + at[0] * 512 + 256, 128)
+        v += jnp.dot(x_ref[:, pl.ds(first, 256)], w_own[i], preferred_element_type=F32)
     hidden[g] = (v / (1.0 + jnp.exp(-v))).astype(BF).astype(F32)
 
     @pl.when(g == 3)
@@ -116,7 +130,7 @@
         o_ref[:, PIECE:] = jnp.broadcast_to(power, (ROWS, META)).astype(BF)
 
 
-def _up(at, rows, w, a_in, a_out):
+def _up(at, rows, w_own, w, a_in, a_out):
     return pl.pallas_call(
         _up_kernel,
         grid_spec=pltpu.PrefetchScalarGridSpec(
@@ -125,6 +139,7 @@
             in_specs=[pl.BlockSpec((ROWS, WIDE + META), lambda g, at: (0, 0))]
             + [pl.BlockSpec((p.shape[0], 256), lambda g, at: (0, g)) for p in w]
             + [
+                pl.BlockSpec((4, 256, 256), lambda g, at: (0, 0, g)),
                 pl.BlockSpec((8, 1, 64, 512), lambda g, at: (0, at[0], 0, 0)),
                 pl.BlockSpec((1, 64, 256), lambda g, at: (at[0], 0, g)),
             ],
@@ -138,7 +153,7 @@
         out_shape=jax.ShapeDtypeStruct((ROWS, PIECE + META), BF),
         compiler_params=_params(32),
         name="up",
-    )(at, rows, *w, a_in, a_out)
+    )(at, rows, *w, w_own, a_in, a_out)
 
 
 def _down_kernel(c_ref, h_ref, m_ref, w_own, w_other, o_ref):
@@ -205,12 +220,9 @@
     return lax.ppermute(v, "x", [(i, (i + by) % 4) for i in range(4)])
 
 
-def _gather_x(first, second):
-    wide, tail = jnp.concatenate([first, second[:256]], axis=0), second[256:]
-    broad, head = jnp.concatenate([first[256:], second], axis=0), first[:256]
-    left, right = _shift_x(wide, 1), _shift_x(broad, -1)
-    far = [_shift_x(left[:512], 1), _shift_x(right[256:], -1)]
-    return [wide, tail, left, _shift_x(tail, 1), right, _shift_x(head, -1)] + far
+def _gather_x(w):
+    left, right = _shift_x(w, 1), _shift_x(w, -1)
+    return [w, left, right, _shift_x(left[:384], 1), _shift_x(right[384:], -1)]
 
 
 def _swap(v):
@@ -225,8 +237,8 @@
     one = lambda w, i: lax.dynamic_index_in_dim(w, i, 0, keepdims=False)
 
     up_own, up_other = one(up_weight, core), _swap(one(up_weight, 1 - core))
-    first, second = jnp.where(core == 0, up_own, up_other), jnp.where(core == 0, up_other, up_own)
-    w_up = _gather_x(first, second)
+    w_own = lax.all_gather(up_own[256:], "x", axis=0)
+    w_up = _gather_x(jnp.concatenate([up_own[:256], up_other], axis=0))
     a_in = lax.all_gather(adapter_in.transpose(0, 2, 1), ("x", "core"), axis=0)
     down_other = _swap(one(down_weight, 1 - core))
 
@@ -239,10 +251,10 @@
     table = lax.all_gather(mine, "z1", axis=0).astype(F32)
     lift = jnp.where(jnp.arange(WIDE + META) < WIDE, 1.0 / LIFT, 1.0)
     table = (table * lift).astype(BF)
-    sending = _select(z1, table, [w_up[2], w_up[4], a_in])
+    sending = _select(z1, table, w_up[1:3] + [w_own])
     arrived = lax.all_to_all(sending, ("y", "core", "z0"), 0, 0, tiled=True).reshape(ROWS, WIDE + META)
 
-    hidden = _up(at, arrived, w_up, a_in, adapter_out)
+    hidden = _up(at, arrived, w_own, w_up, a_in, adapter_out)
     hidden = lax.all_gather(hidden.astype(F16), "x", axis=0).astype(BF)
     out = _down(c, hidden, down_weight, down_other)
     back = lax.all_to_all(out.reshape(64, 16, PIECE), ("x", "y", "core", "z0"), 0, 0, tiled=True)

time: 259 us -> 268 us (1.035)
  local copies, waits for them, and re-layouts: 13.1 us -> 21.2 us
  waiting for transfers between devices: 83.4 us -> 90.1 us
  starting transfers between devices: 34.7 us -> 30.7 us
    all_gather x1, waiting for transfers between devices: 0.02 us -> 20.9 us  [per_device(): a_in = lax.all_gather(adapter_in.transpose(0, 2, 1), ('x', 'core'), axis=0)]
    ppermute x6 -> x4, waiting for transfers between devices: 34.5 us -> 19.3 us  [_shift_x(): return lax.ppermute(v, 'x', [(i, (i + by) % 4) for i in range(4)])]
    unnamed x22 -> x34, local copies, waits for them, and re-layouts: 5.04 us -> 13.4 us
    ppermute x6 -> x4, starting transfers between devices: 17.6 us -> 13.7 us  [_shift_x(): return lax.ppermute(v, 'x', [(i, (i + by) % 4) for i in range(4)])]
  transfers between devices with their start and end apart: 11 -> 10, of which waited for: 5 -> 5; matrix products, arithmetic and copies ran while one was open for 4% -> 3% of each run, Pallas kernels for 3% -> 3%
where the time goes in v8:
time: 268 us; the launch traced here: 265 us
  waiting for transfers between devices  90.1 us (34%)
  blocking collectives  89.1 us (33%)
  starting transfers between devices  30.7 us (11%)
  local copies, waits for them, and re-layouts  21.2 us (8%)
  Pallas kernels  17.1 us (6%)
  between operations  15.1 us (6%)
    reduce_scatter x1, waiting for transfers between devices, per_device(): return lax.psum_scatter(partial, 'z1', scatter_dimension=0, tiled=True)  48.2 us
    all_to_all x1, blocking collectives, per_device(): lax.all_to_all(out.reshape(64, 16, PIECE), ('x', 'y', 'core', 'z0'), 0, 0...  35.8 us
    all_gather x1, blocking collectives, per_device(): table = lax.all_gather(mine, 'z1', axis=0).astype(F32)  30.5 us
    all_gather x1, blocking collectives, per_device(): hidden = lax.all_gather(hidden.astype(F16), 'x', axis=0).astype(BF)  22.9 us
    all_gather x1, waiting for transfers between devices, per_device(): a_in = lax.all_gather(adapter_in.transpose(0, 2, 1), ('x', 'core'), axis=0)  20.9 us
    ppermute x4, waiting for transfers between devices, _shift_x(): return lax.ppermute(v, 'x', [(i, (i + by) % 4) for i in range(4)])  19.3 us
    ppermute x4, starting transfers between devices, _shift_x(): return lax.ppermute(v, 'x', [(i, (i + by) % 4) for i in range(4)])  13.7 us
    unnamed x34, local copies, waits for them, and re-layouts  13.4 us
  transfers between devices with their start and end apart: 10, of which 5 were waited for; matrix products, arithmetic and copies ran while one was open for 3% of the time, Pallas kernels for 3%

profile of v8, /device:TPU:1, one launch (start us, length us, event | category | flops | bytes accessed | tf_op | source)
XLA Modules:
  0.0 265.5 jit_solution(6524489712202838088)
XLA Ops:
  7.4 2.4 dynamic-slice_bitcast_fusion.1
  9.8 8.8 %collective-permute-start = (bf16[512,1024]{1,0:T(8,128)(2,1)}, bf16[512,1024]{1,0:T(8,128)(2,1)}, u32[]{:S(2)}, u32[]{:S(2)}) collective-permute-start(bf16[512,1024]{1,0:T(8,128)(2,1)} %dynamic-slice_bitcast_fusion.1), channel_id=1, source_target_pairs={{0,64},{64,0},{1,65},{65,1},{2,66},{66,2},{3,67},{67,3},{4,68},{68... | collective-permute-start | bytes 3145736 | tf_op jit(solution)/shard_map/ppermute | solution.py:229
  18.6 0.9 constant_dynamic-slice_fusion
  19.5 0.0 all-gather.8.cloned.1.call-update
  19.6 0.1 compare_convert_fusion
  19.6 0.1 copy.11
  19.7 0.1 copy.12
  19.9 0.1 concatenate.6
  20.0 1.2 collective-permute-done
  21.2 1.3 pad_maximum_fusion.refs_0_
  22.6 1.9 collective-permute-start.1
  24.5 4.6 %collective-permute-start.2 = (bf16[768,1024]{1,0:T(8,128)(2,1)S(1)}, bf16[768,1024]{1,0:T(8,128)(2,1)S(1)}, u32[]{:S(2)}, u32[]{:S(2)}) collective-permute-start(bf16[768,1024]{1,0:T(8,128)(2,1)S(1)} %pad_maximum_fusion.refs_0_), channel_id=1, source_target_pairs={{0,384},{128,0},{256,128},{384,256},{1,385},{129,1},{257,129},{385... | collective-permute-start | bytes 4718600 | tf_op jit(solution)/shard_map/ppermute | solution.py:220
  29.1 30.5 %all-gather.11 = f16[128,4224]{1,0:T(8,128)(2,1)S(1)} all-gather(f16[16,4224]{1,0:T(8,128)(2,1)S(1)} %concatenate.6), channel_id=2, replica_groups=mesh['x'=4,'core'=2,'z1'=8,'z0'=2,'y'=4] {'z1'}, dimensions={0}, use_global_device_ids=true | all-gather | bytes 1216512 | tf_op jit(solution)/shard_map/all_gather | solution.py:251
  59.5 0.2 fusion.m_ref.t_ref
  59.7 18.4 %collective-permute-done.1.rest_0_.refs_1_ = bf16[768,1024]{1,0:T(8,128)(2,1)S(1)} collective-permute-done((bf16[768,1024]{1,0:T(8,128)(2,1)S(1)}, bf16[768,1024]{1,0:T(8,128)(2,1)S(1)}, u32[]{:S(2)}, u32[]{:S(2)}) %collective-permute-start.1) | collective-permute-done | bytes 1572896 | tf_op jit(solution)/shard_map/ppermute | solution.py:220
  78.1 0.9 collective-permute-done.2.rest_1_.refs_2_
  79.0 1.2 copy-done
  80.2 1.4 copy-done.1
  81.6 1.6 copy-done.5
  83.2 2.7 %select.9 = bf16[16,16,4224]{2,1,0:T(8,128)(2,1)S(1)} custom-call(s32[1]{0:T(128)} %bitcast.z_ref, bf16[8,16,4224]{2,1,0:T(8,128)(2,1)S(1)} %fusion.m_ref.t_ref, bf16[8,16,4224]{2,1,0:T(8,128)(2,1)S(1)} %fusion.m_ref.t_ref, bf16[768,1024]{1,0:T(8,128)(2,1)S(1)} %collective-permute-done.1.rest_0_.refs_1_, bf16[768,1024]{1,0:T(8,128)(2,1)S(1)} %copy-done.1, ...), custom_call_target="tpu_custom_call" | custom-call | tf_op jit(solution)/shard_map/select/pallas_call | solution.py:64
  85.9 1.4 copy-done.4
  87.3 5.7 %all-to-all-start = ((bf16[16,16,4224]{2,1,0:T(8,128)(2,1)}), bf16[16,16,4224]{2,1,0:T(8,128)(2,1)}, u32[]{:S(2)}, u32[]{:S(2)}) async-start(bf16[16,16,4224]{2,1,0:T(8,128)(2,1)} %copy-done.4), calls=%async_computation | async-start | bytes 4325376 | tf_op jit(solution)/shard_map/all_to_all | solution.py:255
  93.0 0.0 all-gather.10.cloned.1.call-start
  93.0 0.5 all-gather.10.cloned.1.call-update
  93.5 0.0 reduce-scatter.2.cloned.1.call-start
  93.6 0.9 slice.21
  94.5 1.9 collective-permute-start.3
  96.5 0.9 slice.22
  97.4 5.3 %collective-permute-start.4 = (bf16[384,1024]{1,0:T(8,128)(2,1)}, bf16[384,1024]{1,0:T(8,128)(2,1)}, u32[]{:S(2)}, u32[]{:S(2)}) collective-permute-start(bf16[384,1024]{1,0:T(8,128)(2,1)} %slice.22), channel_id=1, source_target_pairs={{0,384},{128,0},{256,128},{384,256},{1,385},{129,1},{257,129},{385... | collective-permute-start | bytes 2359304 | tf_op jit(solution)/shard_map/ppermute | solution.py:220
  102.7 2.3 dynamic-slice_bitcast_fusion
  105.0 2.4 collective-permute-start.5
  107.5 0.1 pad_add_fusion.at
  107.6 20.9 %all-gather.10.cloned.1.call-done = bf16[16,64,512]{2,1,0:T(8,128)(2,1)} async-done(((bf16[2,64,512]{2,1,0:T(8,128)(2,1)}), bf16[16,64,512]{2,1,0:T(8,128)(2,1)}) %all-gather.10.cloned.1.call-update) | async-done | bytes 1048592 | tf_op jit(solution)/shard_map/all_gather | solution.py:242
  128.5 1.4 copy-done.3
  129.9 1.6 copy-done.6
  131.5 1.4 copy-done.8
  132.9 1.2 copy-done.10
  134.1 0.9 copy-done.11
  135.1 7.5 %up.1 = bf16[256,1152]{1,0:T(8,128)(2,1)S(1)} custom-call(s32[2]{0:T(128)S(1)} %pad_add_fusion.at, bf16[256,4224]{1,0:T(8,128)(2,1)} %bitcast.6.x_ref, bf16[768,1024]{1,0:T(8,128)(2,1)S(1)} %copy-done.8, bf16[768,1024]{1,0:T(8,128)(2,1)S(1)} %collective-permute-done.1.rest_0_.refs_1_, bf16[768,1024]{1,0:T(8,128)(2,1)S(1)} %copy-done.3, ...), custom_call_target="tpu_custom_call" | custom-call | tf_op jit(solution)/shard_map/up/pallas_call | solution.py:134
  142.5 0.1 convert_element_type.34
  142.7 22.9 %all-gather.12 = f16[1024,1152]{1,0:T(8,128)(2,1)S(1)} all-gather(f16[256,1152]{1,0:T(8,128)(2,1)S(1)} %convert_element_type.34), channel_id=4, replica_groups=mesh['x'=4,'core'=2,'z1'=8,'z0'=2,'y'=4] {'x'}, dimensions={0}, use_global_device_ids=true | all-gather | bytes 2949120 | tf_op jit(solution)/shard_map/all_gather | solution.py:258
  165.5 0.3 convert_element_type.37
  165.9 1.2 copy-done.9
  167.1 4.3 %down.1 = bf16[4,16,16,1024]{3,2,1,0:T(8,128)(2,1)S(1)} custom-call(s32[1]{0:T(128)} %bitcast.2.c_ref, bf16[4,256,1152]{2,1,0:T(8,128)(2,1)S(1)} %bitcast.17, bf16[4,256,1152]{2,1,0:T(8,128)(2,1)S(1)} %bitcast.18, bf16[2,1024,512]{2,1,0:T(8,128)(2,1)S(1)} %copy-done.9, bf16[1024,512]{1,0:T(8,128)(2,1)} %collective-permute-done.5.w_other), custom_call_target="tpu_custom_call" | custom-call | tf_op jit(solution)/shard_map/down/pallas_call | solution.py:168
  171.4 35.8 %all_to_all.10 = bf16[64,16,1024]{2,1,0:T(8,128)(2,1)S(1)} all-to-all(bf16[64,16,1024]{2,1,0:T(8,128)(2,1)S(1)} %bitcast.19), channel_id=1, replica_groups=mesh['x'=4,'core'=2,'z1'=8,'z0'=2,'y'=4] {'x','y','core','z0'}, dimensions={0} | all-to-all | bytes 4194304 | tf_op jit(solution)/shard_map/all_to_all | solution.py:260
  207.2 2.6 combine.1
  209.8 0.0 reduce-scatter.2.cloned.1.call-update
  209.8 48.2 %reduce-scatter.2.cloned.1.call-done = bf16[16,4096]{1,0:T(8,128)(2,1)} async-done(((bf16[128,4096]{1,0:T(8,128)(2,1)}), bf16[16,4096]{1,0:T(8,128)(2,1)}) %reduce-scatter.2.cloned.1.call-update) | async-done | bytes 131088 | tf_op jit(solution)/shard_map/reduce_scatter | solution.py:262
  (36 shorter events, 0.1 us)
Async XLA Ops:
  7.4 11.2 %copy-start.12 = (bf16[2,512,1024]{2,1,0:T(8,128)(2,1)S(1)}, bf16[2,512,1024]{2,1,0:T(8,128)(2,1)}, u32[]{:S(2)}) copy-start(bf16[2,512,1024]{2,1,0:T(8,128)(2,1)} %param.12) | copy-start | bytes 6291460
  7.4 72.8 %all-gather.8.cloned.1.call-start = ((), (), s32[]{:S(2)}) async-start(), calls=%async_computation.3 | async-start | bytes 2621440 | tf_op jit(solution)/shard_map/all_gather | solution.py:240
  7.4 12.2 %copy-start.16 = (s32[16]{0:T(128)S(1)}, s32[16]{0:T(128)}, u32[]{:S(2)}) copy-start(s32[16]{0:T(128)} %param.11) | copy-start | bytes 196
  7.4 12.3 %copy-start.14 = (s32[16,8]{0,1:T(8,128)S(1)}, s32[16,8]{0,1:T(8,128)}, u32[]{:S(2)}) copy-start(s32[16,8]{0,1:T(8,128)} %param.9) | copy-start | bytes 1540
  7.4 12.4 %copy-start.15 = (f32[16,8]{0,1:T(8,128)S(1)}, f32[16,8]{0,1:T(8,128)}, u32[]{:S(2)}) copy-start(f32[16,8]{0,1:T(8,128)} %param.10) | copy-start | bytes 1540
  7.4 12.4 %copy-start.13 = (bf16[16,4096]{1,0:T(8,128)(2,1)S(1)}, bf16[16,4096]{1,0:T(8,128)(2,1)}, u32[]{:S(2)}) copy-start(bf16[16,4096]{1,0:T(8,128)(2,1)} %param.8) | copy-start | bytes 393220
  9.8 11.4 %collective-permute-start = (bf16[512,1024]{1,0:T(8,128)(2,1)}, bf16[512,1024]{1,0:T(8,128)(2,1)}, u32[]{:S(2)}, u32[]{:S(2)}) collective-permute-start(bf16[512,1024]{1,0:T(8,128)(2,1)} %dynamic-slice_bitcast_fusion.1), channel_id=1, source_target_pairs={{0,64},{64,0},{1,65},{65,1},{2,66},{66,2},{3,67},{67,3},{4,68},{68... | collective-permute-start | bytes 3145736 | tf_op jit(solution)/shard_map/ppermute | solution.py:229
  22.6 55.6 %copy-start.7 = (bf16[768,1024]{1,0:T(8,128)(2,1)}, bf16[768,1024]{1,0:T(8,128)(2,1)S(1)}, u32[]{:S(2)}) copy-start(bf16[768,1024]{1,0:T(8,128)(2,1)S(1)} %pad_maximum_fusion.refs_0_) | copy-start | bytes 4718596
  22.6 55.6 %collective-permute-start.1 = (bf16[768,1024]{1,0:T(8,128)(2,1)S(1)}, bf16[768,1024]{1,0:T(8,128)(2,1)S(1)}, u32[]{:S(2)}, u32[]{:S(2)}) collective-permute-start(bf16[768,1024]{1,0:T(8,128)(2,1)S(1)} %pad_maximum_fusion.refs_0_), channel_id=1, source_target_pairs={{0,128},{128,256},{256,384},{384,0},{1,129},{129,257},{257,385},{3... | collective-permute-start | bytes 4718600 | tf_op jit(solution)/shard_map/ppermute | solution.py:220
  24.5 54.5 %collective-permute-start.2 = (bf16[768,1024]{1,0:T(8,128)(2,1)S(1)}, bf16[768,1024]{1,0:T(8,128)(2,1)S(1)}, u32[]{:S(2)}, u32[]{:S(2)}) collective-permute-start(bf16[768,1024]{1,0:T(8,128)(2,1)S(1)} %pad_maximum_fusion.refs_0_), channel_id=1, source_target_pairs={{0,384},{128,0},{256,128},{384,256},{1,385},{129,1},{257,129},{385... | collective-permute-start | bytes 4718600 | tf_op jit(solution)/shard_map/ppermute | solution.py:220
  79.0 1.2 copy-start
  80.2 1.4 copy-start.1
  81.6 1.6 copy-start.5
  85.9 1.4 copy-start.4
  87.3 41.2 %all-to-all-start = ((bf16[16,16,4224]{2,1,0:T(8,128)(2,1)}), bf16[16,16,4224]{2,1,0:T(8,128)(2,1)}, u32[]{:S(2)}, u32[]{:S(2)}) async-start(bf16[16,16,4224]{2,1,0:T(8,128)(2,1)} %copy-done.4), calls=%async_computation | async-start | bytes 4325376 | tf_op jit(solution)/shard_map/all_to_all | solution.py:255
  93.0 35.5 %all-gather.10.cloned.1.call-start = ((), (), s32[]{:S(2)}) async-start(), calls=%async_computation.5 | async-start | bytes 1179648 | tf_op jit(solution)/shard_map/all_gather | solution.py:242
  93.5 164.5 %reduce-scatter.2.cloned.1.call-start = ((), (), s32[]{:S(2)}) async-start(), calls=%async_computation.4 | async-start | bytes 1179648 | tf_op jit(solution)/shard_map/reduce_scatter | solution.py:262
  93.6 2.9 %copy-start.2 = (bf16[768,1024]{1,0:T(8,128)(2,1)S(1)}, bf16[768,1024]{1,0:T(8,128)(2,1)}, u32[]{:S(2)}) copy-start(bf16[768,1024]{1,0:T(8,128)(2,1)} %copy-done) | copy-start | bytes 4718596
  94.5 33.9 %collective-permute-start.3 = (bf16[384,1024]{1,0:T(8,128)(2,1)}, bf16[384,1024]{1,0:T(8,128)(2,1)S(1)}, u32[]{:S(2)}, u32[]{:S(2)}) collective-permute-start(bf16[384,1024]{1,0:T(8,128)(2,1)} %slice.21), channel_id=1, source_target_pairs={{0,128},{128,256},{256,384},{384,0},{1,129},{129,257},{257,385},{3... | collective-permute-start | bytes 2359304 | tf_op jit(solution)/shard_map/ppermute | solution.py:220
  97.4 31.1 %collective-permute-start.4 = (bf16[384,1024]{1,0:T(8,128)(2,1)}, bf16[384,1024]{1,0:T(8,128)(2,1)}, u32[]{:S(2)}, u32[]{:S(2)}) collective-permute-start(bf16[384,1024]{1,0:T(8,128)(2,1)} %slice.22), channel_id=1, source_target_pairs={{0,384},{128,0},{256,128},{384,256},{1,385},{129,1},{257,129},{385... | collective-permute-start | bytes 2359304 | tf_op jit(solution)/shard_map/ppermute | solution.py:220
  105.0 60.8 %collective-permute-start.5 = (bf16[1024,512]{1,0:T(8,128)(2,1)}, bf16[1024,512]{1,0:T(8,128)(2,1)}, u32[]{:S(2)}, u32[]{:S(2)}) collective-permute-start(bf16[1024,512]{1,0:T(8,128)(2,1)} %dynamic-slice_bitcast_fusion), channel_id=1, source_target_pairs={{0,64},{64,0},{1,65},{65,1},{2,66},{66,2},{3,67},{67,3},{4,68},{68... | collective-permute-start | bytes 3145736 | tf_op jit(solution)/shard_map/ppermute | solution.py:229
  128.5 1.4 copy-start.3
  129.9 1.6 copy-start.6
  131.5 1.4 copy-start.8
  132.9 1.2 copy-start.10
  134.1 0.9 copy-start.11
  165.5 1.6 copy-start.9
Sparse Core Ops, SparseCore 0:
  19.7 54.2 all-gather.7
Sparse Core Ops, SparseCore 1:
  95.6 32.8 all-gather.9
  209.9 48.1 reduce-scatter.1

commit v9 on v7

--- a/solution.py
+++ b/solution.py
@@ -51,16 +51,33 @@
     return (at == (slot % 2 + 1).astype(F32)) & (tok // TOK == (slot % 16) // 2)
 
 
-def _select_kernel(z_ref, m_ref, t_ref, *rest):
-    o_ref = rest[-1]
+def _select_kernel(z_ref, m_ref, t_ref, left, right, after, o_ref, low, high, sem):
+    g = pl.program_id(0)
+    copies = (
+        pltpu.make_async_copy(left.at[pl.ds(0, 512)], low, sem.at[0]),
+        pltpu.make_async_copy(right.at[pl.ds(512, 512)], high, sem.at[1]),
+    )
+
+    @pl.when(g == 0)
+    def _():
+        for copy in copies:
+            copy.start()
+
     slots = _slots(_matches(m_ref[...].reshape(TOKS, META).astype(F32), z_ref[0])).astype(BF)
     t = t_ref[...].reshape(TOKS, t_ref.shape[2])
     out = lax.dot_general(slots, t, (((0,), (0,)), ((), ())), preferred_element_type=F32)
     o_ref[...] = out.astype(BF).reshape(o_ref.shape)
 
-
-def _select(z1, table, after):
+    @pl.when(g == 2)
+    def _():
+        for copy in copies:
+            copy.wait()
+
+
+def _select(z1, table, left, right, after):
     width = (WIDE + META) // 3
+    anywhere = pl.BlockSpec(memory_space=pl.ANY)
+    half = jax.ShapeDtypeStruct((512, PIECE), BF)
     return pl.pallas_call(
         _select_kernel,
         grid_spec=pltpu.PrefetchScalarGridSpec(
@@ -69,17 +86,20 @@
             in_specs=[
                 pl.BlockSpec((8, TOK, META), lambda g, z: (0, 0, WIDE // META)),
                 pl.BlockSpec((8, TOK, width), lambda g, z: (0, 0, g)),
-            ]
-            + [pl.BlockSpec(memory_space=pl.ANY) for _ in after],
-            out_specs=pl.BlockSpec((DEST, 16, width), lambda g, z: (0, 0, g)),
-        ),
-        out_shape=jax.ShapeDtypeStruct((DEST, 16, WIDE + META), BF),
-        compiler_params=_params(24),
+                anywhere,
+                anywhere,
+                anywhere,
+            ],
+            out_specs=[pl.BlockSpec((DEST, 16, width), lambda g, z: (0, 0, g)), anywhere, anywhere],
+            scratch_shapes=[pltpu.SemaphoreType.DMA((2,))],
+        ),
+        out_shape=[jax.ShapeDtypeStruct((DEST, 16, WIDE + META), BF), half, half],
+        compiler_params=_params(56),
         name="select",
-    )(z1, table, table, *after)
-
-
-HELD = ((0, 0, 768), (0, 768, 256), (3, 0, 768), (3, 768, 256), (1, 256, 768), (1, 0, 256), (2, 0, 512), (2, 512, 512))
+    )(z1, table, table, left, right, after)
+
+
+HELD = ((0, 0, 1024), (3, 0, 1024), (1, 0, 1024), (2, 0, 512), (2, 512, 512))
 
 
 def _up_kernel(at, x_ref, *refs):
@@ -136,7 +156,7 @@
             ],
         ),
         out_shape=jax.ShapeDtypeStruct((ROWS, PIECE + META), BF),
-        compiler_params=_params(32),
+        compiler_params=_params(56),
         name="up",
     )(at, rows, *w, a_in, a_out)
 
@@ -164,7 +184,7 @@
             out_specs=pl.BlockSpec((1, DEST, 16, PIECE), lambda g, c: (g, 0, 0, 0)),
         ),
         out_shape=jax.ShapeDtypeStruct((4, DEST, 16, PIECE), BF),
-        compiler_params=_params(24),
+        compiler_params=_params(56),
         name="down",
     )(c, hidden, hidden, w, w_other)
 
@@ -196,21 +216,13 @@
             scratch_shapes=[pltpu.VMEM((TOKS, ROWS), BF)],
         ),
         out_shape=jax.ShapeDtypeStruct((TOKS, WIDE), BF),
-        compiler_params=_params(24),
+        compiler_params=_params(56),
         name="combine",
     )(z1, table, back)
 
 
 def _shift_x(v, by):
     return lax.ppermute(v, "x", [(i, (i + by) % 4) for i in range(4)])
-
-
-def _gather_x(first, second):
-    wide, tail = jnp.concatenate([first, second[:256]], axis=0), second[256:]
-    broad, head = jnp.concatenate([first[256:], second], axis=0), first[:256]
-    left, right = _shift_x(wide, 1), _shift_x(broad, -1)
-    far = [_shift_x(left[:512], 1), _shift_x(right[256:], -1)]
-    return [wide, tail, left, _shift_x(tail, 1), right, _shift_x(head, -1)] + far
 
 
 def _swap(v):
@@ -226,7 +238,8 @@
 
     up_own, up_other = one(up_weight, core), _swap(one(up_weight, 1 - core))
     first, second = jnp.where(core == 0, up_own, up_other), jnp.where(core == 0, up_other, up_own)
-    w_up = _gather_x(first, second)
+    block = jnp.concatenate([first, second], axis=0)
+    left, right = _shift_x(block, 1), _shift_x(block, -1)
     a_in = lax.all_gather(adapter_in.transpose(0, 2, 1), ("x", "core"), axis=0)
     down_other = _swap(one(down_weight, 1 - core))
 
@@ -239,7 +252,8 @@
     table = lax.all_gather(mine, "z1", axis=0).astype(F32)
     lift = jnp.where(jnp.arange(WIDE + META) < WIDE, 1.0 / LIFT, 1.0)
     table = (table * lift).astype(BF)
-    sending = _select(z1, table, [w_up[2], w_up[4], a_in])
+    sending, low, high = _select(z1, table, left, right, a_in)
+    w_up = [block, left, right, _shift_x(low, 1), _shift_x(high, -1)]
     arrived = lax.all_to_all(sending, ("y", "core", "z0"), 0, 0, tiled=True).reshape(ROWS, WIDE + META)
 
     hidden = _up(at, arrived, w_up, a_in, adapter_out)

time: 259 us -> 320 us (1.24)
  Pallas kernels: 17.4 us -> 86 us
  local copies, waits for them, and re-layouts: 13.1 us -> 7.4 us
  starting transfers between devices: 34.7 us -> 30.1 us
    pallas_call x1, Pallas kernels: 2.7 us -> 66.5 us  [_select(): pl.pallas_call(_select_kernel, grid_spec=pltpu.PrefetchScalarGridSpec(num...]
    slice x4 -> x0, local copies, waits for them, and re-layouts: 4.29 us -> none  [the longest x2 3.34 us: _gather_x(): far = [_shift_x(left[:512], 1), _shift_x(right[256:], -1)]]
    ppermute x6 -> x4, starting transfers between devices: 17.6 us -> 13.8 us  [_shift_x(): return lax.ppermute(v, 'x', [(i, (i + by) % 4) for i in range(4)])]
    ppermute x6 -> x4, waiting for transfers between devices: 34.5 us -> 33.7 us  [_shift_x(): return lax.ppermute(v, 'x', [(i, (i + by) % 4) for i in range(4)])]
  transfers between devices with their start and end apart: 11 -> 9, of which waited for: 5 -> 6; matrix products, arithmetic and copies ran while one was open for 4% -> 2% of each run, Pallas kernels for 3% -> 3%
where the time goes in v9:
time: 320 us; the launch traced here: 316 us
  blocking collectives  91.6 us (29%)
  Pallas kernels  86 us (27%)
  waiting for transfers between devices  82.4 us (26%)
  starting transfers between devices  30.1 us (9%)
  between operations  13.6 us (4%)
  local copies, waits for them, and re-layouts  7.4 us (2%)
  other arithmetic  5.34 us (2%)
    pallas_call x1, Pallas kernels, _select(): pl.pallas_call(_select_kernel, grid_spec=pltpu.PrefetchScalarGridSpec(num...  66.5 us
    reduce_scatter x1, waiting for transfers between devices, per_device(): return lax.psum_scatter(partial, 'z1', scatter_dimension=0, tiled=True)  46.3 us
    all_to_all x1, blocking collectives, per_device(): lax.all_to_all(out.reshape(64, 16, PIECE), ('x', 'y', 'core', 'z0'), 0, 0...  38.5 us
    ppermute x4, waiting for transfers between devices, _shift_x(): return lax.ppermute(v, 'x', [(i, (i + by) % 4) for i in range(4)])  33.7 us
    all_gather x1, blocking collectives, per_device(): table = lax.all_gather(mine, 'z1', axis=0).astype(F32)  30.5 us
    all_gather x1, blocking collectives, per_device(): hidden = lax.all_gather(hidden.astype(F16), 'x', axis=0).astype(BF)  22.6 us
    ppermute x4, starting transfers between devices, _shift_x(): return lax.ppermute(v, 'x', [(i, (i + by) % 4) for i in range(4)])  13.8 us
    ppermute x2, starting transfers between devices, _swap(): return lax.ppermute(v, 'core', [(0, 1), (1, 0)])  11.2 us
  transfers between devices with their start and end apart: 9, of which 6 were waited for; matrix products, arithmetic and copies ran while one was open for 2% of the time, Pallas kernels for 3%

profile of v9, /device:TPU:1, one launch (start us, length us, event | category | flops | bytes accessed | tf_op | source)
XLA Modules:
  0.0 316.5 jit_solution(2840563788216002260)
XLA Ops:
  6.5 0.0 all-gather.7.cloned.1.call-start
  6.5 2.4 dynamic-slice_bitcast_fusion.1
  9.0 8.8 %collective-permute-start = (bf16[512,1024]{1,0:T(8,128)(2,1)}, bf16[512,1024]{1,0:T(8,128)(2,1)S(1)}, u32[]{:S(2)}, u32[]{:S(2)}) collective-permute-start(bf16[512,1024]{1,0:T(8,128)(2,1)} %dynamic-slice_bitcast_fusion.1), channel_id=1, source_target_pairs={{0,64},{64,0},{1,65},{65,1},{2,66},{66,2},{3,67},{67,3},{4,68},{68... | collective-permute-start | bytes 3145736 | tf_op jit(solution)/shard_map/ppermute | solution.py:229
  17.8 0.0 all-gather.7.cloned.1.call-update
  17.8 0.0 copy-done.4
  17.8 2.4 collective-permute-done
  20.2 0.0 copy-done.2
  20.2 0.1 bitcast_select_fusion.1
  20.4 0.0 copy-start.7
  20.4 0.0 copy-start.5
  20.4 0.0 copy-start.6
  20.4 0.2 pad_maximum_fusion.refs_0_
  20.6 0.0 copy-start.1
  20.6 1.9 collective-permute-start.1
  22.5 4.6 %collective-permute-start.2 = (bf16[1024,1024]{1,0:T(8,128)(2,1)S(1)}, bf16[1024,1024]{1,0:T(8,128)(2,1)}, u32[]{:S(2)}, u32[]{:S(2)}) collective-permute-start(bf16[1024,1024]{1,0:T(8,128)(2,1)S(1)} %pad_maximum_fusion.refs_0_), channel_id=1, source_target_pairs={{0,384},{128,0},{256,128},{384,256},{1,385},{129,1},{257,129},{385... | collective-permute-start | bytes 6291464 | tf_op jit(solution)/shard_map/ppermute | solution.py:225
  27.1 0.0 copy-done.7
  27.1 0.1 compare_convert_fusion
  27.2 0.1 copy.11
  27.3 0.1 copy.12
  27.4 0.1 concatenate.6
  27.5 30.5 %all-gather.8 = f16[128,4224]{1,0:T(8,128)(2,1)S(1)} all-gather(f16[16,4224]{1,0:T(8,128)(2,1)S(1)} %concatenate.6), channel_id=2, replica_groups=mesh['x'=4,'core'=2,'z1'=8,'z0'=2,'y'=4] {'z1'}, dimensions={0}, use_global_device_ids=true | all-gather | bytes 1216512 | tf_op jit(solution)/shard_map/all_gather | solution.py:252
  58.0 1.3 fusion.m_ref.t_ref
  59.3 15.6 %collective-permute-done.1.left.refs_1_ = bf16[1024,1024]{1,0:T(8,128)(2,1)} collective-permute-done((bf16[1024,1024]{1,0:T(8,128)(2,1)S(1)}, bf16[1024,1024]{1,0:T(8,128)(2,1)}, u32[]{:S(2)}, u32[]{:S(2)}) %collective-permute-start.1) | collective-permute-done | bytes 2097184 | tf_op jit(solution)/shard_map/ppermute | solution.py:225
  74.9 0.8 collective-permute-done.2.right.refs_2_
  75.6 66.5 %select.9 = (bf16[16,16,4224]{2,1,0:T(8,128)(2,1)}, bf16[512,1024]{1,0:T(8,128)(2,1)}, bf16[512,1024]{1,0:T(8,128)(2,1)}) custom-call(s32[1]{0:T(128)} %bitcast.z_ref, bf16[8,16,4224]{2,1,0:T(8,128)(2,1)} %fusion.m_ref.t_ref, bf16[8,16,4224]{2,1,0:T(8,128)(2,1)} %fusion.m_ref.t_ref, bf16[1024,1024]{1,0:T(8,128)(2,1)} %collective-permute-done.1.left.refs_1_, ...), custom_call_target="tpu_custom_call" | custom-call | tf_op jit(solution)/shard_map/select/pallas_call | solution.py:81
  142.2 0.0 copy-done.1
  142.2 5.1 %all-to-all-start = ((bf16[16,16,4224]{2,1,0:T(8,128)(2,1)}), bf16[16,16,4224]{2,1,0:T(8,128)(2,1)S(1)}, u32[]{:S(2)}, u32[]{:S(2)}) async-start(bf16[16,16,4224]{2,1,0:T(8,128)(2,1)} %get-tuple-element.8), calls=%async_computation | async-start | bytes 4325376 | tf_op jit(solution)/shard_map/all_to_all | solution.py:257
  147.2 0.0 reduce-scatter.2.cloned.1.call-start
  147.3 1.9 collective-permute-start.3
  149.2 5.4 %collective-permute-start.4 = (bf16[512,1024]{1,0:T(8,128)(2,1)}, bf16[512,1024]{1,0:T(8,128)(2,1)}, u32[]{:S(2)}, u32[]{:S(2)}) collective-permute-start(bf16[512,1024]{1,0:T(8,128)(2,1)} %get-tuple-element.10), channel_id=1, source_target_pairs={{0,384},{128,0},{256,128},{384,256},{1,385},{129,1},{257,129},{385... | collective-permute-start | bytes 3145736 | tf_op jit(solution)/shard_map/ppermute | solution.py:225
  154.6 2.3 dynamic-slice_bitcast_fusion
  156.9 2.4 collective-permute-start.5
  159.3 0.7 pad_add_fusion.at
  160.0 16.4 %collective-permute-done.3.refs_3_ = bf16[512,1024]{1,0:T(8,128)(2,1)} collective-permute-done((bf16[512,1024]{1,0:T(8,128)(2,1)}, bf16[512,1024]{1,0:T(8,128)(2,1)}, u32[]{:S(2)}, u32[]{:S(2)}) %collective-permute-start.3) | collective-permute-done | bytes 1048608 | tf_op jit(solution)/shard_map/ppermute | solution.py:225
  176.4 0.9 collective-permute-done.4.refs_4_
  177.3 0.0 all-to-all-done
  177.3 1.4 copy-done
  178.6 9.0 %up.1 = bf16[256,1152]{1,0:T(8,128)(2,1)} custom-call(s32[2]{0:T(128)} %pad_add_fusion.at, bf16[256,4224]{1,0:T(8,128)(2,1)} %bitcast.20, bf16[1024,1024]{1,0:T(8,128)(2,1)} %copy-done.1, bf16[1024,1024]{1,0:T(8,128)(2,1)} %collective-permute-done.1.left.refs_1_, bf16[1024,1024]{1,0:T(8,128)(2,1)} %collective-permute-done.2.right.refs_2_, ...), custom_call_target="tpu_custom_call" | custom-call | tf_op jit(solution)/shard_map/up/pallas_call | solution.py:140
  187.7 1.2 convert_element_type.34
  188.8 22.6 %all-gather.9 = f16[1024,1152]{1,0:T(8,128)(2,1)S(1)} all-gather(f16[256,1152]{1,0:T(8,128)(2,1)S(1)} %convert_element_type.34), channel_id=4, replica_groups=mesh['x'=4,'core'=2,'z1'=8,'z0'=2,'y'=4] {'x'}, dimensions={0}, use_global_device_ids=true | all-gather | bytes 2949120 | tf_op jit(solution)/shard_map/all_gather | solution.py:260
  211.4 1.8 convert_element_type.37
  213.2 0.0 collective-permute-done.5.w_other
  213.2 1.0 copy-done.3
  214.2 6.0 %down.1 = bf16[4,16,16,1024]{3,2,1,0:T(8,128)(2,1)} custom-call(s32[1]{0:T(128)} %bitcast.2.c_ref, bf16[4,256,1152]{2,1,0:T(8,128)(2,1)} %bitcast.18, bf16[4,256,1152]{2,1,0:T(8,128)(2,1)} %bitcast.19, bf16[2,1024,512]{2,1,0:T(8,128)(2,1)} %w_own.1, bf16[1024,512]{1,0:T(8,128)(2,1)} %copy-done.3), custom_call_target="tpu_custom_call" | custom-call | tf_op jit(solution)/shard_map/down/pallas_call | solution.py:173
  220.2 38.5 %all_to_all.10 = bf16[64,16,1024]{2,1,0:T(8,128)(2,1)} all-to-all(bf16[64,16,1024]{2,1,0:T(8,128)(2,1)} %bitcast.21), channel_id=1, replica_groups=mesh['x'=4,'core'=2,'z1'=8,'z0'=2,'y'=4] {'x','y','core','z0'}, dimensions={0} | all-to-all | bytes 4194304 | tf_op jit(solution)/shard_map/all_to_all | solution.py:262
  258.8 4.5 %combine.1 = bf16[128,4096]{1,0:T(8,128)(2,1)} custom-call(s32[1]{0:T(128)} %bitcast.z_ref, bf16[8,16,4224]{2,1,0:T(8,128)(2,1)} %fusion.m_ref.t_ref, bf16[4,16,16,1024]{3,2,1,0:T(8,128)(2,1)} %bitcast.22), custom_call_target="tpu_custom_call" | custom-call | tf_op jit(solution)/shard_map/combine/pallas_call | solution.py:206
  263.3 0.0 reduce-scatter.2.cloned.1.call-update
  263.3 46.3 %reduce-scatter.2.cloned.1.call-done = bf16[16,4096]{1,0:T(8,128)(2,1)} async-done(((bf16[128,4096]{1,0:T(8,128)(2,1)}), bf16[16,4096]{1,0:T(8,128)(2,1)}) %reduce-scatter.2.cloned.1.call-update) | async-done | bytes 131088 | tf_op jit(solution)/shard_map/reduce_scatter | solution.py:264
  (13 shorter events, 0.1 us)
Async XLA Ops:
  6.5 13.7 %copy-start.2 = (bf16[2,512,1024]{2,1,0:T(8,128)(2,1)S(1)}, bf16[2,512,1024]{2,1,0:T(8,128)(2,1)}, u32[]{:S(2)}) copy-start(bf16[2,512,1024]{2,1,0:T(8,128)(2,1)} %param.12) | copy-start | bytes 6291460
  6.5 11.3 %copy-start.4 = (bf16[16,4096]{1,0:T(8,128)(2,1)S(1)}, bf16[16,4096]{1,0:T(8,128)(2,1)}, u32[]{:S(2)}) copy-start(bf16[16,4096]{1,0:T(8,128)(2,1)} %param.8) | copy-start | bytes 393220
  6.5 52.7 %all-gather.7.cloned.1.call-start = ((), (), s32[]{:S(2)}) async-start(), calls=%async_computation.4 | async-start | bytes 1179648 | tf_op jit(solution)/shard_map/all_gather | solution.py:243
  9.0 11.3 %collective-permute-start = (bf16[512,1024]{1,0:T(8,128)(2,1)}, bf16[512,1024]{1,0:T(8,128)(2,1)S(1)}, u32[]{:S(2)}, u32[]{:S(2)}) collective-permute-start(bf16[512,1024]{1,0:T(8,128)(2,1)} %dynamic-slice_bitcast_fusion.1), channel_id=1, source_target_pairs={{0,64},{64,0},{1,65},{65,1},{2,66},{66,2},{3,67},{67,3},{4,68},{68... | collective-permute-start | bytes 3145736 | tf_op jit(solution)/shard_map/ppermute | solution.py:229
  20.4 6.8 %copy-start.7 = (s32[16]{0:T(128)S(1)}, s32[16]{0:T(128)}, u32[]{:S(2)}) copy-start(s32[16]{0:T(128)} %param.11) | copy-start | bytes 196
  20.4 6.8 %copy-start.5 = (s32[16,8]{0,1:T(8,128)S(1)}, s32[16,8]{0,1:T(8,128)}, u32[]{:S(2)}) copy-start(s32[16,8]{0,1:T(8,128)} %param.9) | copy-start | bytes 1540
  20.4 6.9 %copy-start.6 = (f32[16,8]{0,1:T(8,128)S(1)}, f32[16,8]{0,1:T(8,128)}, u32[]{:S(2)}) copy-start(f32[16,8]{0,1:T(8,128)} %param.10) | copy-start | bytes 1540
  20.6 121.6 %copy-start.1 = (bf16[1024,1024]{1,0:T(8,128)(2,1)}, bf16[1024,1024]{1,0:T(8,128)(2,1)S(1)}, u32[]{:S(2)}) copy-start(bf16[1024,1024]{1,0:T(8,128)(2,1)S(1)} %pad_maximum_fusion.refs_0_) | copy-start | bytes 6291460
  20.6 54.3 %collective-permute-start.1 = (bf16[1024,1024]{1,0:T(8,128)(2,1)S(1)}, bf16[1024,1024]{1,0:T(8,128)(2,1)}, u32[]{:S(2)}, u32[]{:S(2)}) collective-permute-start(bf16[1024,1024]{1,0:T(8,128)(2,1)S(1)} %pad_maximum_fusion.refs_0_), channel_id=1, source_target_pairs={{0,128},{128,256},{256,384},{384,0},{1,129},{129,257},{257,385},{3... | collective-permute-start | bytes 6291464 | tf_op jit(solution)/shard_map/ppermute | solution.py:225
  22.5 53.1 %collective-permute-start.2 = (bf16[1024,1024]{1,0:T(8,128)(2,1)S(1)}, bf16[1024,1024]{1,0:T(8,128)(2,1)}, u32[]{:S(2)}, u32[]{:S(2)}) collective-permute-start(bf16[1024,1024]{1,0:T(8,128)(2,1)S(1)} %pad_maximum_fusion.refs_0_), channel_id=1, source_target_pairs={{0,384},{128,0},{256,128},{384,256},{1,385},{129,1},{257,129},{385... | collective-permute-start | bytes 6291464 | tf_op jit(solution)/shard_map/ppermute | solution.py:225
  142.2 35.1 %all-to-all-start = ((bf16[16,16,4224]{2,1,0:T(8,128)(2,1)}), bf16[16,16,4224]{2,1,0:T(8,128)(2,1)S(1)}, u32[]{:S(2)}, u32[]{:S(2)}) async-start(bf16[16,16,4224]{2,1,0:T(8,128)(2,1)} %get-tuple-element.8), calls=%async_computation | async-start | bytes 4325376 | tf_op jit(solution)/shard_map/all_to_all | solution.py:257
  147.2 162.4 %reduce-scatter.2.cloned.1.call-start = ((), (), s32[]{:S(2)}) async-start(), calls=%async_computation.3 | async-start | bytes 1179648 | tf_op jit(solution)/shard_map/reduce_scatter | solution.py:264
  147.3 29.1 %collective-permute-start.3 = (bf16[512,1024]{1,0:T(8,128)(2,1)}, bf16[512,1024]{1,0:T(8,128)(2,1)}, u32[]{:S(2)}, u32[]{:S(2)}) collective-permute-start(bf16[512,1024]{1,0:T(8,128)(2,1)} %get-tuple-element.9), channel_id=1, source_target_pairs={{0,128},{128,256},{256,384},{384,0},{1,129},{129,257},{257,385},{3... | collective-permute-start | bytes 3145736 | tf_op jit(solution)/shard_map/ppermute | solution.py:225
  149.2 28.1 %collective-permute-start.4 = (bf16[512,1024]{1,0:T(8,128)(2,1)}, bf16[512,1024]{1,0:T(8,128)(2,1)}, u32[]{:S(2)}, u32[]{:S(2)}) collective-permute-start(bf16[512,1024]{1,0:T(8,128)(2,1)} %get-tuple-element.10), channel_id=1, source_target_pairs={{0,384},{128,0},{256,128},{384,256},{1,385},{129,1},{257,129},{385... | collective-permute-start | bytes 3145736 | tf_op jit(solution)/shard_map/ppermute | solution.py:225
  156.9 56.3 %collective-permute-start.5 = (bf16[1024,512]{1,0:T(8,128)(2,1)}, bf16[1024,512]{1,0:T(8,128)(2,1)S(1)}, u32[]{:S(2)}, u32[]{:S(2)}) collective-permute-start(bf16[1024,512]{1,0:T(8,128)(2,1)} %dynamic-slice_bitcast_fusion), channel_id=1, source_target_pairs={{0,64},{64,0},{1,65},{65,1},{2,66},{66,2},{3,67},{67,3},{4,68},{68... | collective-permute-start | bytes 3145736 | tf_op jit(solution)/shard_map/ppermute | solution.py:229
  177.3 1.4 copy-start
  213.2 1.0 copy-start.3
Sparse Core Ops, SparseCore 0:
  17.9 32.1 all-gather.6
  263.4 46.1 reduce-scatter.1

commit v10 on v9

--- a/solution.py
+++ b/solution.py
@@ -51,32 +51,21 @@
     return (at == (slot % 2 + 1).astype(F32)) & (tok // TOK == (slot % 16) // 2)
 
 
-def _select_kernel(z_ref, m_ref, t_ref, left, right, after, o_ref, low, high, sem):
-    g = pl.program_id(0)
-    copies = (
-        pltpu.make_async_copy(left.at[pl.ds(0, 512)], low, sem.at[0]),
-        pltpu.make_async_copy(right.at[pl.ds(512, 512)], high, sem.at[1]),
-    )
-
-    @pl.when(g == 0)
-    def _():
-        for copy in copies:
-            copy.start()
-
+def _select_kernel(z_ref, m_ref, t_ref, left, right, after, o_ref, low, high):
     slots = _slots(_matches(m_ref[...].reshape(TOKS, META).astype(F32), z_ref[0])).astype(BF)
     t = t_ref[...].reshape(TOKS, t_ref.shape[2])
     out = lax.dot_general(slots, t, (((0,), (0,)), ((), ())), preferred_element_type=F32)
     o_ref[...] = out.astype(BF).reshape(o_ref.shape)
 
-    @pl.when(g == 2)
-    def _():
-        for copy in copies:
-            copy.wait()
+    @pl.when(pl.program_id(0) == 0)
+    def _():
+        low[...] = left[...]
+        high[...] = right[...]
 
 
 def _select(z1, table, left, right, after):
     width = (WIDE + META) // 3
-    anywhere = pl.BlockSpec(memory_space=pl.ANY)
+    upper = pl.BlockSpec((512, PIECE), lambda g, z: (0, 0))
     half = jax.ShapeDtypeStruct((512, PIECE), BF)
     return pl.pallas_call(
         _select_kernel,
@@ -86,15 +75,14 @@
             in_specs=[
                 pl.BlockSpec((8, TOK, META), lambda g, z: (0, 0, WIDE // META)),
                 pl.BlockSpec((8, TOK, width), lambda g, z: (0, 0, g)),
-                anywhere,
-                anywhere,
-                anywhere,
-            ],
-            out_specs=[pl.BlockSpec((DEST, 16, width), lambda g, z: (0, 0, g)), anywhere, anywhere],
-            scratch_shapes=[pltpu.SemaphoreType.DMA((2,))],
+                upper,
+                pl.BlockSpec((512, PIECE), lambda g, z: (1, 0)),
+                pl.BlockSpec(memory_space=pl.ANY),
+            ],
+            out_specs=[pl.BlockSpec((DEST, 16, width), lambda g, z: (0, 0, g)), upper, upper],
         ),
         out_shape=[jax.ShapeDtypeStruct((DEST, 16, WIDE + META), BF), half, half],
-        compiler_params=_params(56),
+        compiler_params=_params(24),
         name="select",
     )(z1, table, table, left, right, after)
 
@@ -156,7 +144,7 @@
             ],
         ),
         out_shape=jax.ShapeDtypeStruct((ROWS, PIECE + META), BF),
-        compiler_params=_params(56),
+        compiler_params=_params(28),
         name="up",
     )(at, rows, *w, a_in, a_out)
 
@@ -184,7 +172,7 @@
             out_specs=pl.BlockSpec((1, DEST, 16, PIECE), lambda g, c: (g, 0, 0, 0)),
         ),
         out_shape=jax.ShapeDtypeStruct((4, DEST, 16, PIECE), BF),
-        compiler_params=_params(56),
+        compiler_params=_params(28),
         name="down",
     )(c, hidden, hidden, w, w_other)
 
@@ -216,7 +204,7 @@
             scratch_shapes=[pltpu.VMEM((TOKS, ROWS), BF)],
         ),
         out_shape=jax.ShapeDtypeStruct((TOKS, WIDE), BF),
-        compiler_params=_params(56),
+        compiler_params=_params(28),
         name="combine",
     )(z1, table, back)
 

time: 320 us -> 256 us (0.80)
  Pallas kernels: 86 us -> 18.4 us
  local copies, waits for them, and re-layouts: 7.4 us -> 13.7 us
  other arithmetic: 5.34 us -> 1.17 us
    pallas_call x1, Pallas kernels: 66.5 us -> 4.42 us  [_select(): pl.pallas_call(_select_kernel, grid_spec=pltpu.PrefetchScalarGridSpec(num...]
    unnamed x16 -> x28, local copies, waits for them, and re-layouts: 2.41 us -> 8.62 us
  transfers between devices with their start and end apart: 9 -> 9, of which waited for: 6 -> 6; matrix products, arithmetic and copies ran while one was open for 2% -> 1% of each run, Pallas kernels for 3% -> 3%
where the time goes in v10:
time: 256 us; the launch traced here: 253 us
  blocking collectives  91.3 us (36%)
  waiting for transfers between devices  84.4 us (33%)
  starting transfers between devices  30.2 us (12%)
  Pallas kernels  18.4 us (7%)
  local copies, waits for them, and re-layouts  13.7 us (5%)
  between operations  13.6 us (5%)
    reduce_scatter x1, waiting for transfers between devices, per_device(): return lax.psum_scatter(partial, 'z1', scatter_dimension=0, tiled=True)  46.7 us
    all_to_all x1, blocking collectives, per_device(): lax.all_to_all(out.reshape(64, 16, PIECE), ('x', 'y', 'core', 'z0'), 0, 0...  38.2 us
    ppermute x4, waiting for transfers between devices, _shift_x(): return lax.ppermute(v, 'x', [(i, (i + by) % 4) for i in range(4)])  35.3 us
    all_gather x1, blocking collectives, per_device(): table = lax.all_gather(mine, 'z1', axis=0).astype(F32)  30.5 us
    all_gather x1, blocking collectives, per_device(): hidden = lax.all_gather(hidden.astype(F16), 'x', axis=0).astype(BF)  22.6 us
    ppermute x4, starting transfers between devices, _shift_x(): return lax.ppermute(v, 'x', [(i, (i + by) % 4) for i in range(4)])  14 us
    ppermute x2, starting transfers between devices, _swap(): return lax.ppermute(v, 'core', [(0, 1), (1, 0)])  11.2 us
    unnamed x28, local copies, waits for them, and re-layouts  8.62 us
  transfers between devices with their start and end apart: 9, of which 6 were waited for; matrix products, arithmetic and copies ran while one was open for 1% of the time, Pallas kernels for 3%

profile of v10, /device:TPU:1, one launch (start us, length us, event | category | flops | bytes accessed | tf_op | source)
XLA Modules:
  0.0 252.8 jit_solution(7637158504166764474)
XLA Ops:
  6.5 2.5 dynamic-slice_bitcast_fusion.1
  9.0 8.8 %collective-permute-start = (bf16[512,1024]{1,0:T(8,128)(2,1)}, bf16[512,1024]{1,0:T(8,128)(2,1)S(1)}, u32[]{:S(2)}, u32[]{:S(2)}) collective-permute-start(bf16[512,1024]{1,0:T(8,128)(2,1)} %dynamic-slice_bitcast_fusion.1), channel_id=1, source_target_pairs={{0,64},{64,0},{1,65},{65,1},{2,66},{66,2},{3,67},{67,3},{4,68},{68... | collective-permute-start | bytes 3145736 | tf_op jit(solution)/shard_map/ppermute | solution.py:217
  17.8 0.0 all-gather.7.cloned.1.call-update
  17.9 2.4 collective-permute-done
  20.3 0.1 bitcast_select_fusion.1
  20.4 0.0 copy-start.13
  20.4 0.0 copy-start.11
  20.4 0.0 copy-start.12
  20.4 0.2 pad_maximum_fusion.refs_0_
  20.6 1.9 collective-permute-start.1
  22.6 4.6 %collective-permute-start.2 = (bf16[1024,1024]{1,0:T(8,128)(2,1)S(1)}, bf16[1024,1024]{1,0:T(8,128)(2,1)}, u32[]{:S(2)}, u32[]{:S(2)}) collective-permute-start(bf16[1024,1024]{1,0:T(8,128)(2,1)S(1)} %pad_maximum_fusion.refs_0_), channel_id=1, source_target_pairs={{0,384},{128,0},{256,128},{384,256},{1,385},{129,1},{257,129},{385... | collective-permute-start | bytes 6291464 | tf_op jit(solution)/shard_map/ppermute | solution.py:213
  27.2 0.1 compare_convert_fusion
  27.3 0.1 copy.11
  27.4 0.1 copy.12
  27.4 0.1 concatenate.6
  27.6 30.5 %all-gather.8 = f16[128,4224]{1,0:T(8,128)(2,1)S(1)} all-gather(f16[16,4224]{1,0:T(8,128)(2,1)S(1)} %concatenate.6), channel_id=2, replica_groups=mesh['x'=4,'core'=2,'z1'=8,'z0'=2,'y'=4] {'z1'}, dimensions={0}, use_global_device_ids=true | all-gather | bytes 1216512 | tf_op jit(solution)/shard_map/all_gather | solution.py:240
  58.0 0.2 fusion.m_ref.t_ref
  58.2 0.0 all-gather.7.cloned.1.call-done
  58.2 16.7 %collective-permute-done.1.left.refs_1_ = bf16[1024,1024]{1,0:T(8,128)(2,1)} collective-permute-done((bf16[1024,1024]{1,0:T(8,128)(2,1)S(1)}, bf16[1024,1024]{1,0:T(8,128)(2,1)}, u32[]{:S(2)}, u32[]{:S(2)}) %collective-permute-start.1) | collective-permute-done | bytes 2097184 | tf_op jit(solution)/shard_map/ppermute | solution.py:213
  74.9 0.8 collective-permute-done.2.right.refs_2_
  75.7 1.2 copy-done.3
  76.9 4.4 %select.9 = (bf16[16,16,4224]{2,1,0:T(8,128)(2,1)S(1)}, bf16[512,1024]{1,0:T(8,128)(2,1)S(1)}, bf16[512,1024]{1,0:T(8,128)(2,1)S(1)}) custom-call(s32[1]{0:T(128)} %bitcast.z_ref, bf16[8,16,4224]{2,1,0:T(8,128)(2,1)S(1)} %fusion.m_ref.t_ref, bf16[8,16,4224]{2,1,0:T(8,128)(2,1)S(1)} %fusion.m_ref.t_ref, ...), custom_call_target="tpu_custom_call" | custom-call | tf_op jit(solution)/shard_map/select/pallas_call | solution.py:70
  81.3 1.4 copy-done.5
  82.7 1.0 copy-done.7
  83.7 1.0 copy-done.8
  84.7 5.0 %all-to-all-start = ((bf16[16,16,4224]{2,1,0:T(8,128)(2,1)}), bf16[16,16,4224]{2,1,0:T(8,128)(2,1)S(1)}, u32[]{:S(2)}, u32[]{:S(2)}) async-start(bf16[16,16,4224]{2,1,0:T(8,128)(2,1)} %copy-done.5), calls=%async_computation | async-start | bytes 4325376 | tf_op jit(solution)/shard_map/all_to_all | solution.py:245
  89.7 0.0 reduce-scatter.2.cloned.1.call-start
  89.8 2.1 collective-permute-start.3
  91.8 5.4 %collective-permute-start.4 = (bf16[512,1024]{1,0:T(8,128)(2,1)}, bf16[512,1024]{1,0:T(8,128)(2,1)}, u32[]{:S(2)}, u32[]{:S(2)}) collective-permute-start(bf16[512,1024]{1,0:T(8,128)(2,1)} %copy-done.7), channel_id=1, source_target_pairs={{0,384},{128,0},{256,128},{384,256},{1,385},{129,1},{257,129},{385... | collective-permute-start | bytes 3145736 | tf_op jit(solution)/shard_map/ppermute | solution.py:213
  97.3 2.3 dynamic-slice_bitcast_fusion
  99.6 2.4 collective-permute-start.5
  102.0 0.1 pad_add_fusion.at
  102.0 17.0 %collective-permute-done.3.refs_3_ = bf16[512,1024]{1,0:T(8,128)(2,1)} collective-permute-done((bf16[512,1024]{1,0:T(8,128)(2,1)}, bf16[512,1024]{1,0:T(8,128)(2,1)}, u32[]{:S(2)}, u32[]{:S(2)}) %collective-permute-start.3) | collective-permute-done | bytes 1048608 | tf_op jit(solution)/shard_map/ppermute | solution.py:213
  119.0 0.9 collective-permute-done.4.refs_4_
  119.9 0.0 all-to-all-done
  119.9 1.6 copy-done.1
  121.5 1.2 copy-done.4
  122.7 7.1 %up.1 = bf16[256,1152]{1,0:T(8,128)(2,1)S(1)} custom-call(s32[2]{0:T(128)S(1)} %pad_add_fusion.at, bf16[256,4224]{1,0:T(8,128)(2,1)S(1)} %bitcast.20, bf16[1024,1024]{1,0:T(8,128)(2,1)S(1)} %copy-done.1, bf16[1024,1024]{1,0:T(8,128)(2,1)} %collective-permute-done.1.left.refs_1_, bf16[1024,1024]{1,0:T(8,128)(2,1)} %collective-permute-done.2.right.refs_2_, ...), custom_call_target="tpu_custom_call" | custom-call | tf_op jit(solution)/shard_map/up/pallas_call | solution.py:128
  129.8 0.1 convert_element_type.34
  129.9 22.6 %all-gather.9 = f16[1024,1152]{1,0:T(8,128)(2,1)S(1)} all-gather(f16[256,1152]{1,0:T(8,128)(2,1)S(1)} %convert_element_type.34), channel_id=4, replica_groups=mesh['x'=4,'core'=2,'z1'=8,'z0'=2,'y'=4] {'x'}, dimensions={0}, use_global_device_ids=true | all-gather | bytes 2949120 | tf_op jit(solution)/shard_map/all_gather | solution.py:248
  152.5 0.4 convert_element_type.37
  152.9 0.0 collective-permute-done.5.w_other
  152.9 1.2 copy-done.2
  154.1 4.3 %down.1 = bf16[4,16,16,1024]{3,2,1,0:T(8,128)(2,1)S(1)} custom-call(s32[1]{0:T(128)} %bitcast.2.c_ref, bf16[4,256,1152]{2,1,0:T(8,128)(2,1)S(1)} %bitcast.18, bf16[4,256,1152]{2,1,0:T(8,128)(2,1)S(1)} %bitcast.19, bf16[2,1024,512]{2,1,0:T(8,128)(2,1)S(1)} %copy-done.2, bf16[1024,512]{1,0:T(8,128)(2,1)} %collective-permute-done.5.w_other), custom_call_target="tpu_custom_call" | custom-call | tf_op jit(solution)/shard_map/down/pallas_call | solution.py:161
  158.4 38.2 %all_to_all.10 = bf16[64,16,1024]{2,1,0:T(8,128)(2,1)S(1)} all-to-all(bf16[64,16,1024]{2,1,0:T(8,128)(2,1)S(1)} %bitcast.21), channel_id=1, replica_groups=mesh['x'=4,'core'=2,'z1'=8,'z0'=2,'y'=4] {'x','y','core','z0'}, dimensions={0} | all-to-all | bytes 4194304 | tf_op jit(solution)/shard_map/all_to_all | solution.py:250
  196.6 2.6 %combine.1 = bf16[128,4096]{1,0:T(8,128)(2,1)} custom-call(s32[1]{0:T(128)} %bitcast.z_ref, bf16[8,16,4224]{2,1,0:T(8,128)(2,1)S(1)} %fusion.m_ref.t_ref, bf16[4,16,16,1024]{3,2,1,0:T(8,128)(2,1)S(1)} %bitcast.22), custom_call_target="tpu_custom_call" | custom-call | tf_op jit(solution)/shard_map/combine/pallas_call | solution.py:194
  199.3 0.0 reduce-scatter.2.cloned.1.call-update
  199.3 46.7 %reduce-scatter.2.cloned.1.call-done = bf16[16,4096]{1,0:T(8,128)(2,1)} async-done(((bf16[128,4096]{1,0:T(8,128)(2,1)}), bf16[16,4096]{1,0:T(8,128)(2,1)}) %reduce-scatter.2.cloned.1.call-update) | async-done | bytes 131088 | tf_op jit(solution)/shard_map/reduce_scatter | solution.py:252
  (25 shorter events, 0.1 us)
Async XLA Ops:
  6.5 13.7 %copy-start.9 = (bf16[2,512,1024]{2,1,0:T(8,128)(2,1)S(1)}, bf16[2,512,1024]{2,1,0:T(8,128)(2,1)}, u32[]{:S(2)}) copy-start(bf16[2,512,1024]{2,1,0:T(8,128)(2,1)} %param.12) | copy-start | bytes 6291460
  6.5 11.3 %copy-start.10 = (bf16[16,4096]{1,0:T(8,128)(2,1)S(1)}, bf16[16,4096]{1,0:T(8,128)(2,1)}, u32[]{:S(2)}) copy-start(bf16[16,4096]{1,0:T(8,128)(2,1)} %param.8) | copy-start | bytes 393220
  6.5 51.7 %all-gather.7.cloned.1.call-start = ((), (), s32[]{:S(2)}) async-start(), calls=%async_computation.4 | async-start | bytes 1179648 | tf_op jit(solution)/shard_map/all_gather | solution.py:231
  9.0 11.3 %collective-permute-start = (bf16[512,1024]{1,0:T(8,128)(2,1)}, bf16[512,1024]{1,0:T(8,128)(2,1)S(1)}, u32[]{:S(2)}, u32[]{:S(2)}) collective-permute-start(bf16[512,1024]{1,0:T(8,128)(2,1)} %dynamic-slice_bitcast_fusion.1), channel_id=1, source_target_pairs={{0,64},{64,0},{1,65},{65,1},{2,66},{66,2},{3,67},{67,3},{4,68},{68... | collective-permute-start | bytes 3145736 | tf_op jit(solution)/shard_map/ppermute | solution.py:217
  20.4 6.8 %copy-start.13 = (s32[16]{0:T(128)S(1)}, s32[16]{0:T(128)}, u32[]{:S(2)}) copy-start(s32[16]{0:T(128)} %param.11) | copy-start | bytes 196
  20.4 6.8 %copy-start.11 = (s32[16,8]{0,1:T(8,128)S(1)}, s32[16,8]{0,1:T(8,128)}, u32[]{:S(2)}) copy-start(s32[16,8]{0,1:T(8,128)} %param.9) | copy-start | bytes 1540
  20.4 6.9 %copy-start.12 = (f32[16,8]{0,1:T(8,128)S(1)}, f32[16,8]{0,1:T(8,128)}, u32[]{:S(2)}) copy-start(f32[16,8]{0,1:T(8,128)} %param.10) | copy-start | bytes 1540
  20.6 60.7 %copy-start = (bf16[1024,1024]{1,0:T(8,128)(2,1)}, bf16[1024,1024]{1,0:T(8,128)(2,1)S(1)}, u32[]{:S(2)}) copy-start(bf16[1024,1024]{1,0:T(8,128)(2,1)S(1)} %pad_maximum_fusion.refs_0_) | copy-start | bytes 6291460
  20.6 54.3 %collective-permute-start.1 = (bf16[1024,1024]{1,0:T(8,128)(2,1)S(1)}, bf16[1024,1024]{1,0:T(8,128)(2,1)}, u32[]{:S(2)}, u32[]{:S(2)}) collective-permute-start(bf16[1024,1024]{1,0:T(8,128)(2,1)S(1)} %pad_maximum_fusion.refs_0_), channel_id=1, source_target_pairs={{0,128},{128,256},{256,384},{384,0},{1,129},{129,257},{257,385},{3... | collective-permute-start | bytes 6291464 | tf_op jit(solution)/shard_map/ppermute | solution.py:213
  22.6 53.1 %collective-permute-start.2 = (bf16[1024,1024]{1,0:T(8,128)(2,1)S(1)}, bf16[1024,1024]{1,0:T(8,128)(2,1)}, u32[]{:S(2)}, u32[]{:S(2)}) collective-permute-start(bf16[1024,1024]{1,0:T(8,128)(2,1)S(1)} %pad_maximum_fusion.refs_0_), channel_id=1, source_target_pairs={{0,384},{128,0},{256,128},{384,256},{1,385},{129,1},{257,129},{385... | collective-permute-start | bytes 6291464 | tf_op jit(solution)/shard_map/ppermute | solution.py:213
  75.7 1.2 copy-start.3
  81.3 1.4 copy-start.5
  82.7 1.0 copy-start.7
  83.7 1.0 copy-start.8
  84.7 35.2 %all-to-all-start = ((bf16[16,16,4224]{2,1,0:T(8,128)(2,1)}), bf16[16,16,4224]{2,1,0:T(8,128)(2,1)S(1)}, u32[]{:S(2)}, u32[]{:S(2)}) async-start(bf16[16,16,4224]{2,1,0:T(8,128)(2,1)} %copy-done.5), calls=%async_computation | async-start | bytes 4325376 | tf_op jit(solution)/shard_map/all_to_all | solution.py:245
  89.7 30.2 %copy-start.6 = (bf16[2,64,1024]{2,1,0:T(8,128)(2,1)S(1)}, bf16[2,64,1024]{2,1,0:T(8,128)(2,1)}, u32[]{:S(2)}) copy-start(bf16[2,64,1024]{2,1,0:T(8,128)(2,1)} %refs_6_.1) | copy-start | bytes 786436
  89.7 156.2 %reduce-scatter.2.cloned.1.call-start = ((), (), s32[]{:S(2)}) async-start(), calls=%async_computation.3 | async-start | bytes 1179648 | tf_op jit(solution)/shard_map/reduce_scatter | solution.py:252
  89.8 29.3 %collective-permute-start.3 = (bf16[512,1024]{1,0:T(8,128)(2,1)}, bf16[512,1024]{1,0:T(8,128)(2,1)}, u32[]{:S(2)}, u32[]{:S(2)}) collective-permute-start(bf16[512,1024]{1,0:T(8,128)(2,1)} %copy-done.8), channel_id=1, source_target_pairs={{0,128},{128,256},{256,384},{384,0},{1,129},{129,257},{257,385},{3... | collective-permute-start | bytes 3145736 | tf_op jit(solution)/shard_map/ppermute | solution.py:213
  91.8 28.1 %collective-permute-start.4 = (bf16[512,1024]{1,0:T(8,128)(2,1)}, bf16[512,1024]{1,0:T(8,128)(2,1)}, u32[]{:S(2)}, u32[]{:S(2)}) collective-permute-start(bf16[512,1024]{1,0:T(8,128)(2,1)} %copy-done.7), channel_id=1, source_target_pairs={{0,384},{128,0},{256,128},{384,256},{1,385},{129,1},{257,129},{385... | collective-permute-start | bytes 3145736 | tf_op jit(solution)/shard_map/ppermute | solution.py:213
  99.6 53.3 %collective-permute-start.5 = (bf16[1024,512]{1,0:T(8,128)(2,1)}, bf16[1024,512]{1,0:T(8,128)(2,1)}, u32[]{:S(2)}, u32[]{:S(2)}) collective-permute-start(bf16[1024,512]{1,0:T(8,128)(2,1)} %dynamic-slice_bitcast_fusion), channel_id=1, source_target_pairs={{0,64},{64,0},{1,65},{65,1},{2,66},{66,2},{3,67},{67,3},{4,68},{68... | collective-permute-start | bytes 3145736 | tf_op jit(solution)/shard_map/ppermute | solution.py:217
  119.9 1.6 copy-start.1
  121.5 1.2 copy-start.4
  152.5 1.6 copy-start.2
Sparse Core Ops, SparseCore 0:
  17.9 32.1 all-gather.6
  199.4 46.5 reduce-scatter.1
